TPU v7x, 128 devices: a whole 4x4x4 slice. The times are simulated.
128 devices in a mesh: gx: 8 (over x, z_hi), gy: 16 (over z_lo, y, core).
Axes of the slice: x: 4, y: 4, z: 4 (z_hi: 2, z_lo: 2; z = z_hi * 2 + z_lo), core: 2. Of those that a mesh axis runs over, the one named last changes fastest.
Arguments:
- links: float32 [4, 3, 3, 2, 16, 32, 6, 128], P(None, None, None, None, 'gx', 'gy'), may hold values from -1 to 1, as said below
- incoming: float32 [4, 3, 3, 2, 16, 32, 4, 128], P(None, None, None, None, 'gx', 'gy'), may hold values from -6 to 6
Outputs:
- force: float32 [4, 3, 3, 2, 16, 32, 4, 128], P(None, None, None, None, 'gx', 'gy')
Inputs may be any that keep to these rules, and one draw needn't show every extreme that they name: `links`: each link is a special unitary 3 x 3 matrix.
All inputs are finite; a program needn't handle non-finite values.
Results may differ from a plain program's by a relative error of at most 0.0003.
Values sent between devices are 32-bit elements; how exact they have to be, the bound alone decides.
No kernel may reach another device: no remote copies, remote signals or barrier semaphores. Data moves between devices by JAX's collectives and lax.ppermute only.
A program may use at most 128 MiB of HBM per device.

v0:
```python
import jax
import jax.numpy as jnp
from jax import lax
from jax.experimental import pallas as pl
from jax.experimental.pallas import tpu as pltpu
from jax.sharding import PartitionSpec as P

smear_weight = 0.2
NC, NA = 18, 8
ROWS = 12
VM = 40 * 2**20
O, YP, YM, ZP, ZM, ZPYM, ZMYP = range(7)
buffer_of = {(0, 0): O, (1, 0): YP, (-1, 0): YM, (0, 1): ZP, (0, -1): ZM, (-1, 1): ZPYM, (1, -1): ZMYP}
base_dir = {ZPYM: 1, ZMYP: 2}
PAIRS = [(m, n) for m in range(4) for n in range(m + 1, 4)]
UPPER = [(0, 1), (0, 2), (1, 2)]


def total(terms):
    plus = [a * b for s, a, b in terms if s > 0]
    minus = [a * b for s, a, b in terms if s < 0]
    if not plus:
        value = -minus[0]
        minus = minus[1:]
    else:
        value = plus[0]
        for other in plus[1:]:
            value = value + other
    for other in minus:
        value = value - other
    return value


def entry(left, right, i, k, dag_left=False, dag_right=False, want=(True, True)):
    real, imag = [], []
    for j in range(3):
        ar, ai = left[j][i] if dag_left else left[i][j]
        br, bi = right[k][j] if dag_right else right[j][k]
        sa = -1 if dag_left else 1
        sb = -1 if dag_right else 1
        if ar is not None and br is not None:
            real.append((1, ar, br))
        if ai is not None and bi is not None:
            real.append((-sa * sb, ai, bi))
        if ar is not None and bi is not None:
            imag.append((sb, ar, bi))
        if ai is not None and br is not None:
            imag.append((sa, ai, br))
    return (total(real) if want[0] else None, total(imag) if want[1] else None)


def mm(left, right, dag_left=False, dag_right=False):
    return [[entry(left, right, i, k, dag_left, dag_right) for k in range(3)] for i in range(3)]


def madd(a, b):
    return [[(a[i][j][0] + b[i][j][0], a[i][j][1] + b[i][j][1]) for j in range(3)] for i in range(3)]


def msub(a, b):
    return [[(a[i][j][0] - b[i][j][0], a[i][j][1] - b[i][j][1]) for j in range(3)] for i in range(3)]


def skew(m):
    out = [m[i][i][1] + m[i][i][1] for i in range(3)]
    for i, j in UPPER:
        out += [m[i][j][0] - m[j][i][0], m[i][j][1] + m[j][i][1]]
    return out


def skew_product(left, right, dag_right=False):
    return skew(mm(left, right, False, dag_right))


def unpack8(v):
    return [v[0], v[1], -v[0] - v[1]] + list(v[2:])


def anti(v):
    out = [[None] * 3 for _ in range(3)]
    for i in range(3):
        out[i][i] = (None, v[i])
    for k, (i, j) in enumerate(UPPER):
        r, s = v[3 + 2 * k], v[4 + 2 * k]
        out[i][j] = (r, s)
        out[j][i] = (-r, s)
    return out


def carried(u, v):
    half = mm(u, anti(v))
    diag = [entry(half, u, i, i, False, True, (False, True))[1] for i in range(2)]
    out = [diag[0], diag[1], -diag[0] - diag[1]]
    for i, j in UPPER:
        out += list(entry(half, u, i, j, False, True))
    return out


def third_row(m):
    row = []
    for j in range(3):
        p, q = (j + 1) % 3, (j + 2) % 3
        ar, ai = m[0][p]
        br, bi = m[1][q]
        cr, ci = m[0][q]
        dr, di = m[1][p]
        row.append(
            (ar * br - ai * bi - cr * dr + ci * di, cr * di + ci * dr - ar * bi - ai * br)
        )
    return row


def comp(d, i, j, ri):
    return ((d * 3 + i) * 3 + j) * 2 + ri


def place(c, xe):
    return (c * 4 + xe) * ROWS


def load_matrix(read):
    return [[(read(i, j, 0), read(i, j, 1)) for j in range(3)] for i in range(3)]


def pack_y_body(links, up, down):
    for d in range(4):
        for q in range(12):
            c = d * 18 + q
            for x in range(2):
                base = (c * 2 + x) * ROWS
                to = pl.ds(((d * 12 + q) * 2 + x) * 4, 4)
                up[to, :] = links[pl.ds(base + 3, 4, stride=2), :]
                down[to, :] = links[pl.ds(base + 2, 4, stride=2), :]
    for q in range(12):
        for x in range(2):
            to = pl.ds(384 + q * 2 + x, 1)
            up[to, :] = links[pl.ds(((18 + q) * 2 + x) * ROWS + 11, 1), :]
            down[to, :] = links[pl.ds(((54 + q) * 2 + x) * ROWS, 1), :]


def pack_x_body(links, ynext, yprev, up, down):
    for d in range(4):
        for q in range(12):
            c = d * 18 + q
            to = pl.ds((d * 12 + q) * 8, 8)
            up[to, :] = links[pl.ds((c * 2 + 1) * ROWS + 2, 8), :]
            down[to, :] = links[pl.ds(c * 2 * ROWS + 2, 8), :]
    for q in range(12):
        at = 384 + q * 6
        up[pl.ds(at, 2), :] = links[pl.ds((q * 2 + 1) * ROWS + 10, 2), :]
        down[pl.ds(at, 2), :] = links[pl.ds((54 + q) * 2 * ROWS, 2), :]
        up[pl.ds(at + 2, 4), :] = ynext[pl.ds(q * 8 + 4, 4), :]
        down[pl.ds(at + 2, 4), :] = yprev[pl.ds((12 + q) * 8, 4), :]


def two_rows(read):
    m = [[(read((i * 3 + j) * 2), read((i * 3 + j) * 2 + 1)) for j in range(3)] for i in range(2)]
    return m + [third_row(m)]


def put(write, m):
    for i in range(3):
        for j in range(3):
            for ri in range(2):
                write((i * 3 + j) * 2 + ri, m[i][j][ri])


def roll_z(v, by):
    return pltpu.roll(v, (128 - by) % 128, 1)


def fill_y(bufs, n, dirs_p, dirs_m):
    for x in (1, 2):
        for d in range(4):
            for k in range(n):
                at = place(d * n + k, x)
                if d in dirs_p:
                    bufs[YP][pl.ds(at, 6, stride=2), :] = bufs[O][pl.ds(at + 1, 6, stride=2), :]
                if d in dirs_m:
                    bufs[YM][pl.ds(at + 1, 6, stride=2), :] = bufs[O][pl.ds(at, 6, stride=2), :]


def fill_z(bufs, n):
    for d in range(4):
        for k in range(n):
            c = d * n + k
            for x in (1, 2):
                at = place(c, x)
                zp, zm = bufs[ZP], bufs[ZM]
                if d != 2:
                    zp[pl.ds(at + 2, 8), :] = roll_z(bufs[O][pl.ds(at + 2, 8), :], 1)
                if d == 3:
                    zp[pl.ds(at, 2), :] = roll_z(bufs[O][pl.ds(at, 2), :], 1)
                zm[pl.ds(at + 2, 8), :] = roll_z(bufs[O][pl.ds(at + 2, 8), :], -1)
                if d == 2:
                    zm[pl.ds(at + 10, 2), :] = roll_z(bufs[O][pl.ds(at + 10, 2), :], -1)


def fill_mixed(bufs, n):
    for k in range(n):
        for x in (1, 2):
            bufs[ZPYM][pl.ds(place(k, x) + 2, 8), :] = roll_z(bufs[YM][pl.ds(place(n + k, x) + 2, 8), :], 1)
            bufs[ZMYP][pl.ds(place(k, x) + 2, 8), :] = roll_z(bufs[YP][pl.ds(place(2 * n + k, x) + 2, 8), :], -1)


def fill_edges(bufs, n):
    for k in range(n):
        low, high = place(k, 0), place(2 * n + k, 3)
        bufs[ZP][pl.ds(low + 2, 8), :] = roll_z(bufs[O][pl.ds(low + 2, 8), :], 1)
        bufs[ZM][pl.ds(high + 2, 8), :] = roll_z(bufs[O][pl.ds(high + 2, 8), :], -1)
        bufs[YP][pl.ds(low + 2, 4, stride=2), :] = bufs[O][pl.ds(low + 3, 4, stride=2), :]
        side = place(n + k, 3)
        bufs[YM][pl.ds(side + 3, 4, stride=2), :] = bufs[O][pl.ds(side + 2, 4, stride=2), :]


def fill_links_local(links, bufs):
    for c in range(72):
        for x in range(2):
            source, to = (c * 2 + x) * ROWS, place(c, x + 1)
            bufs[O][pl.ds(to, 8), :] = links[pl.ds(source, 8), :]
            bufs[O][pl.ds(to + 8, 4), :] = links[pl.ds(source + 8, 4), :]
    fill_y(bufs, NC, (0, 2, 3), (0, 1, 2, 3))
    fill_z(bufs, NC)


def fill_links_y(ynext, yprev, bufs):
    for d in range(4):
        for source, buf, off in ((ynext, YP, 3), (yprev, YM, 2)):
            if buf == YP and d == 1:
                continue
            m = two_rows(lambda q: source[pl.ds((d * 12 + q) * 8, 8), :])

            def write(q, v):
                for x in range(2):
                    bufs[buf][pl.ds(place(d * NC + q, x + 1) + off, 4, stride=2), :] = v[4 * x : 4 * x + 4]

            put(write, m)
    for source, buf, d, row in ((ynext, YP, 3, 1), (yprev, YM, 1, 10)):
        m = two_rows(lambda q: source[pl.ds(384 + q * 2, 2), :])

        def write_row(q, v):
            for x in range(2):
                bufs[buf][pl.ds(place(d * NC + q, x + 1) + row, 1), :] = v[x : x + 1]

        put(write_row, m)
    fill_mixed(bufs, NC)


def fill_links_x(xnext, xprev, bufs):
    for d in range(4):
        for source, xe in ((xnext, 3), (xprev, 0)):
            if xe == 3 and d == 0:
                continue
            m = two_rows(lambda q: source[pl.ds((d * 12 + q) * 8, 8), :])

            def write(q, v):
                bufs[O][pl.ds(place(d * NC + q, xe) + 2, 8), :] = v

            put(write, m)
    for source, d, xe, row, buf, cd, off in ((xnext, 3, 3, 0, YM, 1, 2), (xprev, 0, 0, 10, YP, 0, 3)):
        m = two_rows(lambda q: source[pl.ds(384 + q * 6, 2), :])

        def write_edge(q, v):
            bufs[O][pl.ds(place(d * NC + q, xe) + row, 2), :] = v

        put(write_edge, m)
        m = two_rows(lambda q: source[pl.ds(384 + q * 6 + 2, 4), :])

        def write_corner(q, v):
            bufs[buf][pl.ds(place(cd * NC + q, xe) + off, 4, stride=2), :] = v

        put(write_corner, m)
    fill_edges(bufs, NC)


def fill_lambda_local(lam, bufs):
    zero = jnp.zeros((2, 128), jnp.float32)
    for c in range(32):
        for x in range(2):
            to = place(c, x + 1)
            bufs[O][pl.ds(to + 2, 8), :] = lam[pl.ds((c * 2 + x) * 8, 8), :]
            bufs[O][pl.ds(to, 2), :] = zero
            bufs[O][pl.ds(to + 10, 2), :] = zero
    fill_y(bufs, NA, (0, 2, 3), (0, 1, 2, 3))
    fill_z(bufs, NA)


def fill_lambda_y(ynext, yprev, bufs):
    zero = jnp.zeros((1, 128), jnp.float32)
    for d in range(4):
        for k in range(NA):
            for x in range(2):
                source = pl.ds((d * NA + k) * 8 + x * 4, 4)
                to = place(d * NA + k, x + 1)
                bufs[YP][pl.ds(to + 3, 4, stride=2), :] = ynext[source, :]
                bufs[YM][pl.ds(to + 2, 4, stride=2), :] = yprev[source, :]
                if d == 3:
                    bufs[YP][pl.ds(to + 1, 1), :] = zero
                if d == 1:
                    bufs[YM][pl.ds(to + 10, 1), :] = zero
    fill_mixed(bufs, NA)


def fill_lambda_x(xnext, xprev, bufs):
    zero = jnp.zeros((2, 128), jnp.float32)
    for d in range(4):
        for k in range(NA):
            source = pl.ds((d * NA + k) * 8, 8)
            high, low = place(d * NA + k, 3), place(d * NA + k, 0)
            bufs[O][pl.ds(high + 2, 8), :] = xnext[source, :]
            bufs[O][pl.ds(low + 2, 8), :] = xprev[source, :]
            if d == 3:
                bufs[O][pl.ds(high, 2), :] = zero
            if d == 0:
                bufs[O][pl.ds(low + 10, 2), :] = zero
    for k in range(NA):
        corner = pl.ds(256 + k * 4, 4)
        bufs[YM][pl.ds(place(NA + k, 3) + 2, 4, stride=2), :] = xnext[corner, :]
        bufs[YP][pl.ds(place(k, 0) + 3, 4, stride=2), :] = xprev[corner, :]
    fill_edges(bufs, NA)


def step(*signed):
    vector = [0, 0, 0, 0]
    for which, sign in signed:
        vector[which] += sign
    return vector


def where(bufs, n, d, offset, x):
    key = buffer_of[(offset[1], offset[2])]
    row = 2 + 2 * offset[3]
    dd = d - base_dir.get(key, 0)
    shift = (x + 1 + offset[0]) * ROWS

    def read(k):
        return bufs[key][pl.ds(place(dd * n + k, 0) + row + shift, 8), :]

    return read


def link(bufs, d, offset, x):
    read = where(bufs, NC, d, offset, x)
    return load_matrix(lambda i, j, ri: read((i * 3 + j) * 2 + ri))


def lam_at(bufs, d, offset, x):
    read = where(bufs, NA, d, offset, x)
    return unpack8([read(k) for k in range(NA)])


def exponent_force(v, u, target, clow):
    a = v[:3]
    off = [(v[3 + 2 * k], v[4 + 2 * k]) for k in range(3)]
    norm = [r * r + s * s for r, s in off]
    sd = [
        -(a[0] * a[0] + norm[0] + norm[1]),
        -(a[1] * a[1] + norm[0] + norm[2]),
        -(a[2] * a[2] + norm[1] + norm[2]),
    ]
    (r0, s0), (r1, s1), (r2, s2) = off
    so = [
        (a[2] * s0 - (r1 * r2 + s1 * s2), -a[2] * r0 - (s1 * r2 - r1 * s2)),
        (a[1] * s1 + (r0 * r2 - s0 * s2), -a[1] * r1 + (r0 * s2 + s0 * r2)),
        (a[0] * s2 - (r0 * r1 + s0 * s1), -a[0] * r2 - (r0 * s1 - s0 * r1)),
    ]
    c = 0.5 * (sd[0] + sd[1] + sd[2])
    cross = [off[k][1] * so[k][0] - off[k][0] * so[k][1] for k in range(3)]
    dd = (a[0] * sd[0] + a[1] * sd[1] + a[2] * sd[2] + 2.0 * (cross[0] + cross[1] + cross[2])) * (1.0 / 3.0)
    p0r = 1.0 - dd * dd * (1.0 / 720.0)
    p0i = dd * (1.0 / 6.0 + c * (1.0 / 120.0))
    p1r = 1.0 + c * (1.0 / 6.0 + c * (1.0 / 120.0))
    p1i = dd * (1.0 / 24.0 + c * (1.0 / 360.0))
    p2r = 0.5 + c * (1.0 / 24.0 + c * (1.0 / 720.0))
    p2i = dd * (1.0 / 120.0)
    m = mm(target, u, False, True)
    hd = [m[i][i][0] for i in range(3)]
    kd = [m[i][i][1] for i in range(3)]
    ho = [(0.5 * (m[i][j][0] + m[j][i][0]), 0.5 * (m[i][j][1] - m[j][i][1])) for i, j in UPPER]
    ko = [(0.5 * (m[i][j][0] - m[j][i][0]), 0.5 * (m[i][j][1] + m[j][i][1])) for i, j in UPPER]
    t0r = hd[0] + hd[1] + hd[2]
    t0i = -(kd[0] + kd[1] + kd[2])

    def dots(x, y, xo, yo):
        diag = x[0] * y[0] + x[1] * y[1] + x[2] * y[2]
        rest = [xo[k][0] * yo[k][0] + xo[k][1] * yo[k][1] for k in range(3)]
        return diag + 2.0 * (rest[0] + rest[1] + rest[2])

    def crossed(x, y, xo, yo):
        diag = x[0] * y[0] + x[1] * y[1] + x[2] * y[2]
        rest = [yo[k][1] * xo[k][0] - yo[k][0] * xo[k][1] for k in range(3)]
        return diag + 2.0 * (rest[0] + rest[1] + rest[2])

    t1r = dots(kd, a, ko, off)
    t1i = crossed(hd, a, ho, off)
    t2r = dots(hd, sd, ho, so)
    t2i = -crossed(sd, kd, so, ko)
    by_c = (
        t1r * (1.0 / 6.0 + c * (1.0 / 60.0))
        + t2r * (1.0 / 24.0 + c * (1.0 / 360.0))
        - dd * (t0i * (1.0 / 120.0) + t1i * (1.0 / 360.0))
    )
    by_d = -(
        dd * t0r * (1.0 / 360.0)
        + t0i * (1.0 / 6.0 + c * (1.0 / 120.0))
        + t1i * (1.0 / 24.0 + c * (1.0 / 360.0))
        + t2i * (1.0 / 120.0)
    )
    herm = [[None] * 3 for _ in range(3)]
    for i in range(3):
        herm[i][i] = (-(p2r * hd[i] + p2i * kd[i]), None)
    for k, (i, j) in enumerate(UPPER):
        re = -(p2r * ho[k][0] + p2i * ko[k][1])
        im = p2i * ko[k][0] - p2r * ho[k][1]
        herm[i][j] = (re, im)
        herm[j][i] = (re, -im)
    amat = anti(v)
    g = skew(mm(amat, herm))
    lam = [p1r * kd[i] - p1i * hd[i] + g[i] - by_c * a[i] + by_d * sd[i] for i in range(3)]
    for k in range(3):
        lam.append(p1r * ko[k][0] + p1i * ho[k][1] + g[3 + 2 * k] - by_c * off[k][0] - by_d * so[k][1])
        lam.append(p1r * ko[k][1] - p1i * ho[k][0] + g[4 + 2 * k] - by_c * off[k][1] + by_d * so[k][0])
    mean = (lam[0] + lam[1] + lam[2]) * (1.0 / 3.0)
    lam = [smear_weight * (lam[i] - mean) for i in range(3)] + [smear_weight * lam[k] for k in range(3, 9)]
    edag = [[None] * 3 for _ in range(3)]
    for i in range(3):
        edag[i][i] = (p0r - p1i * a[i] + p2r * sd[i], -(p0i + p1r * a[i] + p2i * sd[i]))
    for k, (i, j) in enumerate(UPPER):
        r, s = off[k]
        sr, si = so[k]
        edag[i][j] = (
            (p2r * sr - p1i * s) + (p2i * si - p1r * r),
            (p1i * r - p2i * sr) + (p2r * si - p1r * s),
        )
        edag[j][i] = (
            (p2r * sr - p1i * s) - (p2i * si - p1r * r),
            -(p1i * r + p2i * sr) - (p2r * si + p1r * s),
        )
    direct = msub(mm(edag, target), mm(anti(lam), clow))
    return lam, direct


def take_incoming(incoming, inner):
    for c in range(144):
        inner[pl.ds(c * 8, 4, stride=2), :] = incoming[pl.ds(c * 8, 4), :]
        inner[pl.ds(c * 8 + 1, 4, stride=2), :] = incoming[pl.ds(c * 8 + 4, 4), :]


def forward(bufs, inner, loops, omega, lam_out, direct, x):
    here = [0, 0, 0, 0]
    for p, (m, n) in enumerate(PAIRS):
        a, d = link(bufs, m, here, x), link(bufs, n, here, x)
        b, c = link(bufs, n, step((m, 1)), x), link(bufs, m, step((n, 1)), x)
        loop = mm(mm(a, b), mm(d, c), False, True)
        for i in range(3):
            for j in range(3):
                for ri in range(2):
                    omega[pl.ds(((p * 18 + (i * 3 + j) * 2 + ri) * 2 + x) * 8, 8), :] = loop[i][j][ri]
        for k, v in enumerate(skew(loop)):
            loops[pl.ds((p * 9 + k) * 8, 8), :] = v
    for m in range(4):
        low = None
        for n in range(4):
            if n == m:
                continue
            e, g = link(bufs, n, step((n, -1)), x), link(bufs, m, step((n, -1)), x)
            h = link(bufs, n, step((n, -1), (m, 1)), x)
            term = mm(mm(e, g, True, False), h)
            low = term if low is None else madd(low, term)
        u = link(bufs, m, here, x)
        v = skew_product(low, u, True)
        for p, (f, s) in enumerate(PAIRS):
            if m == f:
                v = [v[k] - loops[pl.ds((p * 9 + k) * 8, 8), :] for k in range(9)]
            if m == s:
                v = [v[k] + loops[pl.ds((p * 9 + k) * 8, 8), :] for k in range(9)]
        mean = (v[0] + v[1] + v[2]) * (1.0 / 3.0)
        v = [(0.5 * smear_weight) * (v[k] - mean) for k in range(3)] + [
            (0.5 * smear_weight) * v[k] for k in range(3, 9)
        ]
        target = load_matrix(lambda i, j, ri: inner[pl.ds((comp(m, i, j, ri) * 2 + x) * 8, 8), :])
        lam, force = exponent_force(v, u, target, low)
        for k, v in enumerate(lam[:2] + lam[3:]):
            lam_out[pl.ds(((m * NA + k) * 2 + x) * 8, 8), :] = v
        for i in range(3):
            for j in range(3):
                for ri in range(2):
                    direct[pl.ds((comp(m, i, j, ri) * 2 + x) * 8, 8), :] = force[i][j][ri]


def pack_lambda_y(lam, up, down):
    for c in range(32):
        for x in range(2):
            to = pl.ds(c * 8 + x * 4, 4)
            up[to, :] = lam[pl.ds((c * 2 + x) * 8 + 1, 4, stride=2), :]
            down[to, :] = lam[pl.ds((c * 2 + x) * 8, 4, stride=2), :]


def forward_body(*refs):
    links, incoming, ynext, yprev, xnext, xprev = refs[:6]
    bufs, (omega, lam, direct, up, down) = refs[6:13], refs[13:18]
    loops, inner = refs[18:]
    fill_links_local(links, bufs)
    fill_links_y(ynext, yprev, bufs)
    fill_links_x(xnext, xprev, bufs)
    take_incoming(incoming, inner)

    @pl.loop(0, 2)
    def _(x):
        forward(bufs, inner, loops, omega, lam, direct, x)

    pack_lambda_y(lam, up, down)


def pack_lambda_x_body(lam, ynext, yprev, up, down):
    for c in range(32):
        to = pl.ds(c * 8, 8)
        up[to, :] = lam[pl.ds((c * 2 + 1) * 8, 8), :]
        down[to, :] = lam[pl.ds(c * 16, 8), :]
    for k in range(NA):
        to = pl.ds(256 + k * 4, 4)
        up[to, :] = ynext[pl.ds(k * 8 + 4, 4), :]
        down[to, :] = yprev[pl.ds((NA + k) * 8, 4), :]


def backward(bufs, lams, omega, direct, sums, result, x):
    here = [0, 0, 0, 0]
    started = set()

    def gather(d, m):
        for i in range(3):
            for j in range(3):
                for ri in range(2):
                    at = pl.ds(comp(d, i, j, ri) * 8, 8)
                    sums[at, :] = sums[at, :] + m[i][j][ri] if d in started else m[i][j][ri]
        started.add(d)

    for p, (m, n) in enumerate(PAIRS):
        la, ld = lam_at(lams, m, here, x), lam_at(lams, n, here, x)
        lb = carried(link(bufs, m, here, x), lam_at(lams, n, step((m, 1)), x))
        lc = carried(link(bufs, n, here, x), lam_at(lams, m, step((n, 1)), x))
        loop = load_matrix(
            lambda i, j, ri: omega[pl.ds(((p * 18 + (i * 3 + j) * 2 + ri) * 2 + x) * 8, 8), :]
        )
        z = [ld[k] - la[k] for k in range(9)]
        first = anti([z[k] + lc[k] for k in range(9)])
        second = anti([lb[k] - z[k] for k in range(9)])
        gather(m, msub(mm(first, loop, False, True), mm(loop, anti(lb), True, False)))
        gather(n, msub(mm(second, loop), mm(loop, anti(lc))))
    for m in range(4):
        f = load_matrix(lambda i, j, ri: sums[pl.ds(comp(m, i, j, ri) * 8, 8), :])
        force = mm(f, link(bufs, m, here, x))
        for n in range(4):
            if n == m:
                continue
            back = step((n, -1))
            e, g, h = link(bufs, n, back, x), link(bufs, m, back, x), link(bufs, n, step((n, -1), (m, 1)), x)
            le, lg, lh = (
                lam_at(lams, n, back, x),
                lam_at(lams, m, back, x),
                lam_at(lams, n, step((n, -1), (m, 1)), x),
            )
            inside = madd(mm(anti([lg[k] - le[k] for k in range(9)]), g), mm(g, anti(lh)))
            force = madd(force, mm(mm(e, inside, True, False), h))
        for i in range(3):
            for j in range(3):
                for ri in range(2):
                    at = pl.ds((comp(m, i, j, ri) * 2 + x) * 8, 8)
                    result[at, :] = force[i][j][ri] + direct[at, :]


def give_force(result, out):
    for c in range(144):
        out[pl.ds(c * 8, 4), :] = result[pl.ds(c * 8, 4, stride=2), :]
        out[pl.ds(c * 8 + 4, 4), :] = result[pl.ds(c * 8 + 1, 4, stride=2), :]


def backward_body(*refs):
    bufs, (omega, lam, direct, ynext, yprev, xnext, xprev, out) = refs[:7], refs[7:15]
    lams, (sums, result) = refs[15:22], refs[22:]
    fill_lambda_local(lam, lams)
    fill_lambda_y(ynext, yprev, lams)
    fill_lambda_x(xnext, xprev, lams)

    @pl.loop(0, 2)
    def _(x):
        backward(bufs, lams, omega, direct, sums, result, x)

    give_force(result, out)


def rows(n):
    return jax.ShapeDtypeStruct((n, 128), jnp.float32)


def buffer_rows(n):
    return [(n if key in base_dir else 4 * n) * 4 * ROWS for key in range(7)]


def call(body, outs, args, scratch=()):
    return pl.pallas_call(
        body,
        out_shape=tuple(rows(n) for n in outs),
        in_specs=[pl.BlockSpec(memory_space=pltpu.VMEM)] * len(args),
        out_specs=(pl.BlockSpec(memory_space=pltpu.VMEM),) * len(outs),
        scratch_shapes=[pltpu.VMEM((n, 128), jnp.float32) for n in scratch],
        compiler_params=pltpu.CompilerParams(vmem_limit_bytes=VM),
    )(*args)


def shifted(shard, axis, by):
    length = lax.axis_size(axis)
    return lax.ppermute(shard, axis, [(i, (i + by) % length) for i in range(length)])


def body(links, incoming):
    links = jnp.transpose(links, (0, 1, 2, 3, 4, 6, 5, 7)).reshape(144 * ROWS, 128)
    shape = incoming.shape
    incoming = incoming.reshape(1152, 128)
    up, down = call(pack_y_body, (408, 408), (links,))
    yprev, ynext = shifted(up, "gy", 1), shifted(down, "gy", -1)
    up, down = call(pack_x_body, (456, 456), (links, ynext, yprev))
    xprev, xnext = shifted(up, "gx", 1), shifted(down, "gx", -1)
    *kept, up, down = call(
        forward_body,
        buffer_rows(NC) + [6 * 18 * 16, 32 * 16, 1152, 256, 256],
        (links, incoming, ynext, yprev, xnext, xprev),
        (54 * 8, 1152),
    )
    yprev, ynext = shifted(up, "gy", 1), shifted(down, "gy", -1)
    up, down = call(pack_lambda_x_body, (288, 288), (kept[8], ynext, yprev))
    xprev, xnext = shifted(up, "gx", 1), shifted(down, "gx", -1)
    (out,) = call(
        backward_body,
        (1152,),
        (*kept, ynext, yprev, xnext, xprev),
        buffer_rows(NA) + [72 * 8, 1152],
    )
    return out.reshape(shape)


def solution(mesh):
    placed = P(None, None, None, None, "gx", "gy", None, None)
    return jax.shard_map(body, mesh=mesh, in_specs=(placed, placed), out_specs=placed, check_vma=False)
```

profile of v0, /device:TPU:0, one launch (start us, length us, event | category | flops | bytes accessed | tf_op | source)
XLA Modules:
  0.0 58.6 jit_solution(16917672813464799826)
XLA Ops:
  0.0 0.0 copy-start
  0.0 1.2 %copy-done = f32[4,3,3,2,2,2,6,128]{7,5,6,4,3,2,1,0:T(2,128)S(1)} copy-done((f32[4,3,3,2,2,2,6,128]{7,5,6,4,3,2,1,0:T(2,128)S(1)}, f32[4,3,3,2,2,2,6,128]{7,5,6,4,3,2,1,0:T(2,128)}, u32[]{:S(2)}) %copy-start) | copy-done | bytes 884760
  1.2 0.0 copy-start.1
  1.2 0.1 shard_map.28
  1.3 4.0 %collective-permute-start = (f32[408,128]{1,0:T(8,128)S(1)}, f32[408,128]{1,0:T(8,128)S(1)}, u32[]{:S(2)}, u32[]{:S(2)}) collective-permute-start(f32[408,128]{1,0:T(8,128)S(1)} %get-tuple-element.23), channel_id=1, source_target_pairs={{0,15},{1,0},{2,1},{3,2},{4,3},{5,4},{6,5},{7,6},{8,7},{9,8},{10,9... | collective-permute-start | bytes 626696 | tf_op jit(solution)/shard_map/ppermute | solution.py:613
  5.3 0.0 collective-permute-start.1
  5.3 3.3 %collective-permute-done.ynext.refs_2_ = f32[408,128]{1,0:T(8,128)S(1)} collective-permute-done((f32[408,128]{1,0:T(8,128)S(1)}, f32[408,128]{1,0:T(8,128)S(1)}, u32[]{:S(2)}, u32[]{:S(2)}) %collective-permute-start) | collective-permute-done | bytes 208928 | tf_op jit(solution)/shard_map/ppermute | solution.py:613
  8.6 4.0 %collective-permute-done.1.yprev.refs_3_ = f32[408,128]{1,0:T(8,128)S(1)} collective-permute-done((f32[408,128]{1,0:T(8,128)S(1)}, f32[408,128]{1,0:T(8,128)S(1)}, u32[]{:S(2)}, u32[]{:S(2)}) %collective-permute-start.1) | collective-permute-done | bytes 208928 | tf_op jit(solution)/shard_map/ppermute | solution.py:613
  12.6 5.9 %collective-permute-start.2 = (f32[456,128]{1,0:T(8,128)S(1)}, f32[456,128]{1,0:T(8,128)S(1)}, u32[]{:S(2)}, u32[]{:S(2)}) collective-permute-start(f32[456,128]{1,0:T(8,128)S(1)} %get-tuple-element.25), channel_id=1, source_target_pairs={{0,112},{16,0},{32,16},{48,32},{64,48},{80,64},{96,80},{112,96},{1... | collective-permute-start | bytes 700424 | tf_op jit(solution)/shard_map/ppermute | solution.py:613
  18.6 0.0 collective-permute-start.3
  18.6 4.3 %collective-permute-done.2.refs_4_ = f32[456,128]{1,0:T(8,128)S(1)} collective-permute-done((f32[456,128]{1,0:T(8,128)S(1)}, f32[456,128]{1,0:T(8,128)S(1)}, u32[]{:S(2)}, u32[]{:S(2)}) %collective-permute-start.2) | collective-permute-done | bytes 233504 | tf_op jit(solution)/shard_map/ppermute | solution.py:613
  22.9 5.3 %collective-permute-done.3.refs_5_ = f32[456,128]{1,0:T(8,128)S(1)} collective-permute-done((f32[456,128]{1,0:T(8,128)S(1)}, f32[456,128]{1,0:T(8,128)S(1)}, u32[]{:S(2)}, u32[]{:S(2)}) %collective-permute-start.3) | collective-permute-done | bytes 233504 | tf_op jit(solution)/shard_map/ppermute | solution.py:613
  28.3 0.0 copy-done.1
  28.3 4.8 %shard_map.30 = (f32[3456,128]{1,0:T(8,128)S(1)}, f32[3456,128]{1,0:T(8,128)S(1)}, f32[3456,128]{1,0:T(8,128)S(1)}, f32[3456,128]{1,0:T(8,128)S(1)}, f32[3456,12...) custom-call(f32[1728,128]{1,0:T(8,128)S(1)} %bitcast.7, ...), custom_call_target="tpu_custom_call" | custom-call | tf_op jit(solution)/shard_map/pallas_call | solution.py:601
  33.0 0.1 collective-permute-start.4
  33.1 0.5 collective-permute-start.5
  33.6 2.0 %collective-permute-done.4.ynext.refs_10_ = f32[256,128]{1,0:T(8,128)S(1)} collective-permute-done((f32[256,128]{1,0:T(8,128)S(1)}, f32[256,128]{1,0:T(8,128)S(1)}, u32[]{:S(2)}, u32[]{:S(2)}) %collective-permute-start.4) | collective-permute-done | bytes 131104 | tf_op jit(solution)/shard_map/ppermute | solution.py:613
  35.6 5.4 %collective-permute-done.5.yprev.refs_11_ = f32[256,128]{1,0:T(8,128)S(1)} collective-permute-done((f32[256,128]{1,0:T(8,128)S(1)}, f32[256,128]{1,0:T(8,128)S(1)}, u32[]{:S(2)}, u32[]{:S(2)}) %collective-permute-start.5) | collective-permute-done | bytes 131104 | tf_op jit(solution)/shard_map/ppermute | solution.py:613
  41.0 2.7 %collective-permute-start.6 = (f32[288,128]{1,0:T(8,128)S(1)}, f32[288,128]{1,0:T(8,128)S(1)}, u32[]{:S(2)}, u32[]{:S(2)}) collective-permute-start(f32[288,128]{1,0:T(8,128)S(1)} %get-tuple-element.39), channel_id=1, source_target_pairs={{0,112},{16,0},{32,16},{48,32},{64,48},{80,64},{96,80},{112,96},{1... | collective-permute-start | bytes 442376 | tf_op jit(solution)/shard_map/ppermute | solution.py:613
  43.8 0.9 %collective-permute-start.7 = (f32[288,128]{1,0:T(8,128)S(1)}, f32[288,128]{1,0:T(8,128)S(1)}, u32[]{:S(2)}, u32[]{:S(2)}) collective-permute-start(f32[288,128]{1,0:T(8,128)S(1)} %get-tuple-element.40), channel_id=1, source_target_pairs={{0,16},{16,32},{32,48},{48,64},{64,80},{80,96},{96,112},{112,0},{1... | collective-permute-start | bytes 442376 | tf_op jit(solution)/shard_map/ppermute | solution.py:613
  44.6 3.1 %collective-permute-done.6.refs_12_ = f32[288,128]{1,0:T(8,128)S(1)} collective-permute-done((f32[288,128]{1,0:T(8,128)S(1)}, f32[288,128]{1,0:T(8,128)S(1)}, u32[]{:S(2)}, u32[]{:S(2)}) %collective-permute-start.6) | collective-permute-done | bytes 147488 | tf_op jit(solution)/shard_map/ppermute | solution.py:613
  47.8 4.8 %collective-permute-done.7.refs_13_ = f32[288,128]{1,0:T(8,128)S(1)} collective-permute-done((f32[288,128]{1,0:T(8,128)S(1)}, f32[288,128]{1,0:T(8,128)S(1)}, u32[]{:S(2)}, u32[]{:S(2)}) %collective-permute-start.7) | collective-permute-done | bytes 147488 | tf_op jit(solution)/shard_map/ppermute | solution.py:613
  52.5 6.1 %shard_map.32 = f32[1152,128]{1,0:T(8,128)} custom-call(f32[3456,128]{1,0:T(8,128)S(1)} %get-tuple-element.27.refs_0_, f32[3456,128]{1,0:T(8,128)S(1)} %get-tuple-element.28.refs_1_, f32[3456,128]{1,0:T(8,128)S(1)} %get-tuple-element.29.refs_2_, f32[3456,128]{1,0:T(8,128)S(1)} %get-tuple-element.30.refs_3_, f32[3456,128]{1,0:T(8,128)S(1)} %get-tuple-element.31.refs_4_, ...), custom_call_target="tpu_custom_call" | custom-call | tf_op jit(solution)/shard_map/pallas_call | solution.py:601
  (2 shorter events, 0.1 us)
Async XLA Ops:
  0.0 1.2 %copy-start = (f32[4,3,3,2,2,2,6,128]{7,5,6,4,3,2,1,0:T(2,128)S(1)}, f32[4,3,3,2,2,2,6,128]{7,5,6,4,3,2,1,0:T(2,128)}, u32[]{:S(2)}) copy-start(f32[4,3,3,2,2,2,6,128]{7,5,6,4,3,2,1,0:T(2,128)} %param.2) | copy-start | bytes 2654212
  1.2 27.1 %copy-start.1 = (f32[4,3,3,2,2,2,4,128]{7,6,5,4,3,2,1,0:T(4,128)S(1)}, f32[4,3,3,2,2,2,4,128]{7,6,5,4,3,2,1,0:T(4,128)}, u32[]{:S(2)}) copy-start(f32[4,3,3,2,2,2,4,128]{7,6,5,4,3,2,1,0:T(4,128)} %param.3) | copy-start | bytes 1769476
  1.3 7.3 %collective-permute-start = (f32[408,128]{1,0:T(8,128)S(1)}, f32[408,128]{1,0:T(8,128)S(1)}, u32[]{:S(2)}, u32[]{:S(2)}) collective-permute-start(f32[408,128]{1,0:T(8,128)S(1)} %get-tuple-element.23), channel_id=1, source_target_pairs={{0,15},{1,0},{2,1},{3,2},{4,3},{5,4},{6,5},{7,6},{8,7},{9,8},{10,9... | collective-permute-start | bytes 626696 | tf_op jit(solution)/shard_map/ppermute | solution.py:613
  5.3 7.3 %collective-permute-start.1 = (f32[408,128]{1,0:T(8,128)S(1)}, f32[408,128]{1,0:T(8,128)S(1)}, u32[]{:S(2)}, u32[]{:S(2)}) collective-permute-start(f32[408,128]{1,0:T(8,128)S(1)} %get-tuple-element.24), channel_id=1, source_target_pairs={{0,1},{1,2},{2,3},{3,4},{4,5},{5,6},{6,7},{7,8},{8,9},{9,10},{10,1... | collective-permute-start | bytes 626696 | tf_op jit(solution)/shard_map/ppermute | solution.py:613
  12.6 10.3 %collective-permute-start.2 = (f32[456,128]{1,0:T(8,128)S(1)}, f32[456,128]{1,0:T(8,128)S(1)}, u32[]{:S(2)}, u32[]{:S(2)}) collective-permute-start(f32[456,128]{1,0:T(8,128)S(1)} %get-tuple-element.25), channel_id=1, source_target_pairs={{0,112},{16,0},{32,16},{48,32},{64,48},{80,64},{96,80},{112,96},{1... | collective-permute-start | bytes 700424 | tf_op jit(solution)/shard_map/ppermute | solution.py:613
  18.6 9.7 %collective-permute-start.3 = (f32[456,128]{1,0:T(8,128)S(1)}, f32[456,128]{1,0:T(8,128)S(1)}, u32[]{:S(2)}, u32[]{:S(2)}) collective-permute-start(f32[456,128]{1,0:T(8,128)S(1)} %get-tuple-element.26), channel_id=1, source_target_pairs={{0,16},{16,32},{32,48},{48,64},{64,80},{80,96},{96,112},{112,0},{1... | collective-permute-start | bytes 700424 | tf_op jit(solution)/shard_map/ppermute | solution.py:613
  33.0 2.6 %collective-permute-start.4 = (f32[256,128]{1,0:T(8,128)S(1)}, f32[256,128]{1,0:T(8,128)S(1)}, u32[]{:S(2)}, u32[]{:S(2)}) collective-permute-start(f32[256,128]{1,0:T(8,128)S(1)} %get-tuple-element.37), channel_id=1, source_target_pairs={{0,15},{1,0},{2,1},{3,2},{4,3},{5,4},{6,5},{7,6},{8,7},{9,8},{10,9... | collective-permute-start | bytes 393224 | tf_op jit(solution)/shard_map/ppermute | solution.py:613
  33.1 7.9 %collective-permute-start.5 = (f32[256,128]{1,0:T(8,128)S(1)}, f32[256,128]{1,0:T(8,128)S(1)}, u32[]{:S(2)}, u32[]{:S(2)}) collective-permute-start(f32[256,128]{1,0:T(8,128)S(1)} %get-tuple-element.38), channel_id=1, source_target_pairs={{0,1},{1,2},{2,3},{3,4},{4,5},{5,6},{6,7},{7,8},{8,9},{9,10},{10,1... | collective-permute-start | bytes 393224 | tf_op jit(solution)/shard_map/ppermute | solution.py:613
  41.0 6.7 %collective-permute-start.6 = (f32[288,128]{1,0:T(8,128)S(1)}, f32[288,128]{1,0:T(8,128)S(1)}, u32[]{:S(2)}, u32[]{:S(2)}) collective-permute-start(f32[288,128]{1,0:T(8,128)S(1)} %get-tuple-element.39), channel_id=1, source_target_pairs={{0,112},{16,0},{32,16},{48,32},{64,48},{80,64},{96,80},{112,96},{1... | collective-permute-start | bytes 442376 | tf_op jit(solution)/shard_map/ppermute | solution.py:613
  43.8 8.8 %collective-permute-start.7 = (f32[288,128]{1,0:T(8,128)S(1)}, f32[288,128]{1,0:T(8,128)S(1)}, u32[]{:S(2)}, u32[]{:S(2)}) collective-permute-start(f32[288,128]{1,0:T(8,128)S(1)} %get-tuple-element.40), channel_id=1, source_target_pairs={{0,16},{16,32},{32,48},{48,64},{64,80},{80,96},{96,112},{112,0},{1... | collective-permute-start | bytes 442376 | tf_op jit(solution)/shard_map/ppermute | solution.py:613
where the time goes:
time: 58.7 us; the launch traced here: 58.6 us
  waiting for transfers between devices  32.3 us (55%)
  starting transfers between devices  14.1 us (24%)
  Pallas kernels  11 us (19%)
  local copies, waits for them, and re-layouts  1.17 us (2%)
    ppermute x8, waiting for transfers between devices, shifted(): lax.ppermute(shard, axis, [(i, (i + by) % length) for i in range(length)])  32.3 us
    ppermute x8, starting transfers between devices, shifted(): lax.ppermute(shard, axis, [(i, (i + by) % length) for i in range(length)])  14.1 us
    pallas_call x5, Pallas kernels, call(): pl.pallas_call(body, out_shape=tuple((rows(n) for n in outs)), in_specs=[...  11 us
  transfers between devices with their start and end apart: 8, of which 8 were waited for; matrix products, arithmetic and copies ran while one was open for 0% of the time, Pallas kernels for 0%

commit v1 on v0

--- a/solution.py
+++ b/solution.py
@@ -13,6 +13,7 @@
 buffer_of = {(0, 0): O, (1, 0): YP, (-1, 0): YM, (0, 1): ZP, (0, -1): ZM, (-1, 1): ZPYM, (1, -1): ZMYP}
 base_dir = {ZPYM: 1, ZMYP: 2}
 PAIRS = [(m, n) for m in range(4) for n in range(m + 1, 4)]
+DOWN_Y = [0, 2, 3]
 UPPER = [(0, 1), (0, 2), (1, 2)]
 
 
@@ -122,35 +123,46 @@
     return [[(read(i, j, 0), read(i, j, 1)) for j in range(3)] for i in range(3)]
 
 
-def pack_y_body(links, up, down):
+def pack_y(up, down, n, read_up, read_down):
     for d in range(4):
-        for q in range(12):
-            c = d * 18 + q
+        for q in range(n):
             for x in range(2):
-                base = (c * 2 + x) * ROWS
-                to = pl.ds(((d * 12 + q) * 2 + x) * 4, 4)
-                up[to, :] = links[pl.ds(base + 3, 4, stride=2), :]
-                down[to, :] = links[pl.ds(base + 2, 4, stride=2), :]
+                up[pl.ds(((d * n + q) * 2 + x) * 4, 4), :] = read_up(d, q, x)
+                if d != 1:
+                    down[pl.ds(((DOWN_Y.index(d) * n + q) * 2 + x) * 4, 4), :] = read_down(d, q, x)
+
+
+def pack_first_body(links, yup, ydown, xdown, corner):
+    def reader(row):
+        return lambda d, q, x: links[pl.ds(((d * 18 + q) * 2 + x) * ROWS + row, 4, stride=2), :]
+
+    pack_y(yup, ydown, 12, reader(3), reader(2))
     for q in range(12):
         for x in range(2):
-            to = pl.ds(384 + q * 2 + x, 1)
-            up[to, :] = links[pl.ds(((18 + q) * 2 + x) * ROWS + 11, 1), :]
-            down[to, :] = links[pl.ds(((54 + q) * 2 + x) * ROWS, 1), :]
-
-
-def pack_x_body(links, ynext, yprev, up, down):
-    for d in range(4):
-        for q in range(12):
-            c = d * 18 + q
-            to = pl.ds((d * 12 + q) * 8, 8)
-            up[to, :] = links[pl.ds((c * 2 + 1) * ROWS + 2, 8), :]
-            down[to, :] = links[pl.ds(c * 2 * ROWS + 2, 8), :]
+            yup[pl.ds(384 + q * 2 + x, 1), :] = links[pl.ds(((18 + q) * 2 + x) * ROWS + 11, 1), :]
+            ydown[pl.ds(288 + q * 2 + x, 1), :] = links[pl.ds(((54 + q) * 2 + x) * ROWS, 1), :]
+        for d in range(1, 4):
+            xdown[pl.ds(((d - 1) * 12 + q) * 8, 8), :] = links[pl.ds((d * 18 + q) * 2 * ROWS + 2, 8), :]
+        xdown[pl.ds(288 + q * 2, 2), :] = links[pl.ds((54 + q) * 2 * ROWS, 2), :]
+        corner[pl.ds(q * 4, 4), :] = links[pl.ds((18 + q) * 2 * ROWS + 3, 4, stride=2), :]
+
+
+def pack_x_body(links, ynext, up):
     for q in range(12):
-        at = 384 + q * 6
-        up[pl.ds(at, 2), :] = links[pl.ds((q * 2 + 1) * ROWS + 10, 2), :]
-        down[pl.ds(at, 2), :] = links[pl.ds((54 + q) * 2 * ROWS, 2), :]
-        up[pl.ds(at + 2, 4), :] = ynext[pl.ds(q * 8 + 4, 4), :]
-        down[pl.ds(at + 2, 4), :] = yprev[pl.ds((12 + q) * 8, 4), :]
+        for d in range(4):
+            up[pl.ds((d * 12 + q) * 8, 8), :] = links[pl.ds(((d * 18 + q) * 2 + 1) * ROWS + 2, 8), :]
+        up[pl.ds(384 + q * 2, 2), :] = links[pl.ds((q * 2 + 1) * ROWS + 10, 2), :]
+        up[pl.ds(408 + q * 4, 4), :] = ynext[pl.ds(q * 8 + 4, 4), :]
+
+
+def pack_lambda_x_body(lam, ynext, yprev, up, down):
+    for c in range(32):
+        up[pl.ds(c * 8, 8), :] = lam[pl.ds((c * 2 + 1) * 8, 8), :]
+        if c >= NA:
+            down[pl.ds((c - NA) * 8, 8), :] = lam[pl.ds(c * 16, 8), :]
+    for k in range(NA):
+        up[pl.ds(256 + k * 4, 4), :] = ynext[pl.ds(k * 8 + 4, 4), :]
+        down[pl.ds(192 + k * 4, 4), :] = yprev[pl.ds((NA + k) * 8, 4), :]
 
 
 def two_rows(read):
@@ -228,15 +240,16 @@
         for source, buf, off in ((ynext, YP, 3), (yprev, YM, 2)):
             if buf == YP and d == 1:
                 continue
-            m = two_rows(lambda q: source[pl.ds((d * 12 + q) * 8, 8), :])
+            slot = DOWN_Y.index(d) if buf == YP else d
+            m = two_rows(lambda q: source[pl.ds((slot * 12 + q) * 8, 8), :])
 
             def write(q, v):
                 for x in range(2):
                     bufs[buf][pl.ds(place(d * NC + q, x + 1) + off, 4, stride=2), :] = v[4 * x : 4 * x + 4]
 
             put(write, m)
-    for source, buf, d, row in ((ynext, YP, 3, 1), (yprev, YM, 1, 10)):
-        m = two_rows(lambda q: source[pl.ds(384 + q * 2, 2), :])
+    for source, buf, d, row, at in ((ynext, YP, 3, 1, 288), (yprev, YM, 1, 10, 384)):
+        m = two_rows(lambda q: source[pl.ds(at + q * 2, 2), :])
 
         def write_row(q, v):
             for x in range(2):
@@ -246,28 +259,30 @@
     fill_mixed(bufs, NC)
 
 
-def fill_links_x(xnext, xprev, bufs):
+def fill_links_x(xnext, corner, xprev, bufs):
     for d in range(4):
         for source, xe in ((xnext, 3), (xprev, 0)):
             if xe == 3 and d == 0:
                 continue
-            m = two_rows(lambda q: source[pl.ds((d * 12 + q) * 8, 8), :])
+            slot = d - 1 if xe == 3 else d
+            m = two_rows(lambda q: source[pl.ds((slot * 12 + q) * 8, 8), :])
 
             def write(q, v):
                 bufs[O][pl.ds(place(d * NC + q, xe) + 2, 8), :] = v
 
             put(write, m)
-    for source, d, xe, row, buf, cd, off in ((xnext, 3, 3, 0, YM, 1, 2), (xprev, 0, 0, 10, YP, 0, 3)):
-        m = two_rows(lambda q: source[pl.ds(384 + q * 6, 2), :])
+    for source, d, xe, row, at in ((xnext, 3, 3, 0, 288), (xprev, 0, 0, 10, 384)):
+        m = two_rows(lambda q: source[pl.ds(at + q * 2, 2), :])
 
         def write_edge(q, v):
             bufs[O][pl.ds(place(d * NC + q, xe) + row, 2), :] = v
 
         put(write_edge, m)
-        m = two_rows(lambda q: source[pl.ds(384 + q * 6 + 2, 4), :])
+    for source, at, buf, d, xe, off in ((corner, 0, YM, 1, 3, 2), (xprev, 408, YP, 0, 0, 3)):
+        m = two_rows(lambda q: source[pl.ds(at + q * 4, 4), :])
 
         def write_corner(q, v):
-            bufs[buf][pl.ds(place(cd * NC + q, xe) + off, 4, stride=2), :] = v
+            bufs[buf][pl.ds(place(d * NC + q, xe) + off, 4, stride=2), :] = v
 
         put(write_corner, m)
     fill_edges(bufs, NC)
@@ -290,10 +305,11 @@
     for d in range(4):
         for k in range(NA):
             for x in range(2):
-                source = pl.ds((d * NA + k) * 8 + x * 4, 4)
                 to = place(d * NA + k, x + 1)
-                bufs[YP][pl.ds(to + 3, 4, stride=2), :] = ynext[source, :]
-                bufs[YM][pl.ds(to + 2, 4, stride=2), :] = yprev[source, :]
+                if d != 1:
+                    source = pl.ds((DOWN_Y.index(d) * NA + k) * 8 + x * 4, 4)
+                    bufs[YP][pl.ds(to + 3, 4, stride=2), :] = ynext[source, :]
+                bufs[YM][pl.ds(to + 2, 4, stride=2), :] = yprev[pl.ds((d * NA + k) * 8 + x * 4, 4), :]
                 if d == 3:
                     bufs[YP][pl.ds(to + 1, 1), :] = zero
                 if d == 1:
@@ -305,18 +321,17 @@
     zero = jnp.zeros((2, 128), jnp.float32)
     for d in range(4):
         for k in range(NA):
-            source = pl.ds((d * NA + k) * 8, 8)
             high, low = place(d * NA + k, 3), place(d * NA + k, 0)
-            bufs[O][pl.ds(high + 2, 8), :] = xnext[source, :]
-            bufs[O][pl.ds(low + 2, 8), :] = xprev[source, :]
+            if d != 0:
+                bufs[O][pl.ds(high + 2, 8), :] = xnext[pl.ds(((d - 1) * NA + k) * 8, 8), :]
+            bufs[O][pl.ds(low + 2, 8), :] = xprev[pl.ds((d * NA + k) * 8, 8), :]
             if d == 3:
                 bufs[O][pl.ds(high, 2), :] = zero
             if d == 0:
                 bufs[O][pl.ds(low + 10, 2), :] = zero
     for k in range(NA):
-        corner = pl.ds(256 + k * 4, 4)
-        bufs[YM][pl.ds(place(NA + k, 3) + 2, 4, stride=2), :] = xnext[corner, :]
-        bufs[YP][pl.ds(place(k, 0) + 3, 4, stride=2), :] = xprev[corner, :]
+        bufs[YM][pl.ds(place(NA + k, 3) + 2, 4, stride=2), :] = xnext[pl.ds(192 + k * 4, 4), :]
+        bufs[YP][pl.ds(place(k, 0) + 3, 4, stride=2), :] = xprev[pl.ds(256 + k * 4, 4), :]
     fill_edges(bufs, NA)
 
 
@@ -440,153 +455,193 @@
     return lam, direct
 
 
+def plane_fields(m, n):
+    here = step()
+    return [(m, here), (n, here), (n, step((m, 1))), (m, step((n, 1)))]
+
+
+def lower_fields(m, n):
+    back = step((n, -1))
+    return [(n, back), (m, back), (n, step((n, -1), (m, 1)))]
+
+
+def level(fields, x):
+    found = 0
+    for _, offset in fields:
+        if x + offset[0] not in (0, 1):
+            found = 2
+        elif offset[1]:
+            found = max(found, 1)
+    return found
+
+
+LOWERS = [(m, n) for m in range(4) for n in range(4) if n != m]
+
+
+def items(wanted):
+    planes = [(p, m, n, x) for x in range(2) for p, (m, n) in enumerate(PAIRS) if level(plane_fields(m, n), x) == wanted]
+    lowers = [(m, n, x) for x in range(2) for m, n in LOWERS if level(lower_fields(m, n), x) == wanted]
+    return planes, lowers
+
+
+def cells(n, k, x):
+    return pl.ds((n + k) * 16 + x * 8, 8)
+
+
+def load_cells(ref, n, x):
+    return load_matrix(lambda i, j, ri: ref[cells(n, (i * 3 + j) * 2 + ri, x), :])
+
+
+def store_cells(ref, n, x, m):
+    for i in range(3):
+        for j in range(3):
+            for ri in range(2):
+                ref[cells(n, (i * 3 + j) * 2 + ri, x), :] = m[i][j][ri]
+
+
 def take_incoming(incoming, inner):
     for c in range(144):
         inner[pl.ds(c * 8, 4, stride=2), :] = incoming[pl.ds(c * 8, 4), :]
         inner[pl.ds(c * 8 + 1, 4, stride=2), :] = incoming[pl.ds(c * 8 + 4, 4), :]
 
 
-def forward(bufs, inner, loops, omega, lam_out, direct, x):
-    here = [0, 0, 0, 0]
-    for p, (m, n) in enumerate(PAIRS):
-        a, d = link(bufs, m, here, x), link(bufs, n, here, x)
-        b, c = link(bufs, n, step((m, 1)), x), link(bufs, m, step((n, 1)), x)
+def forward_items(wanted, bufs, omega, loops, low):
+    planes, lowers = items(wanted)
+    begun = {(m, x) for w in range(wanted) for m, _, x in items(w)[1]}
+    for p, m, n, x in planes:
+        a, d, b, c = [link(bufs, which, offset, x) for which, offset in plane_fields(m, n)]
         loop = mm(mm(a, b), mm(d, c), False, True)
-        for i in range(3):
-            for j in range(3):
-                for ri in range(2):
-                    omega[pl.ds(((p * 18 + (i * 3 + j) * 2 + ri) * 2 + x) * 8, 8), :] = loop[i][j][ri]
+        store_cells(omega, p * 18, x, loop)
         for k, v in enumerate(skew(loop)):
-            loops[pl.ds((p * 9 + k) * 8, 8), :] = v
+            loops[cells(p * 9, k, x), :] = v
     for m in range(4):
-        low = None
-        for n in range(4):
-            if n == m:
+        for x in range(2):
+            value = load_cells(low, m * 18, x) if (m, x) in begun else None
+            mine = [n for mm_, n, xx in lowers if (mm_, xx) == (m, x)]
+            if not mine:
                 continue
-            e, g = link(bufs, n, step((n, -1)), x), link(bufs, m, step((n, -1)), x)
-            h = link(bufs, n, step((n, -1), (m, 1)), x)
-            term = mm(mm(e, g, True, False), h)
-            low = term if low is None else madd(low, term)
-        u = link(bufs, m, here, x)
-        v = skew_product(low, u, True)
-        for p, (f, s) in enumerate(PAIRS):
-            if m == f:
-                v = [v[k] - loops[pl.ds((p * 9 + k) * 8, 8), :] for k in range(9)]
-            if m == s:
-                v = [v[k] + loops[pl.ds((p * 9 + k) * 8, 8), :] for k in range(9)]
-        mean = (v[0] + v[1] + v[2]) * (1.0 / 3.0)
-        v = [(0.5 * smear_weight) * (v[k] - mean) for k in range(3)] + [
-            (0.5 * smear_weight) * v[k] for k in range(3, 9)
-        ]
-        target = load_matrix(lambda i, j, ri: inner[pl.ds((comp(m, i, j, ri) * 2 + x) * 8, 8), :])
-        lam, force = exponent_force(v, u, target, low)
-        for k, v in enumerate(lam[:2] + lam[3:]):
-            lam_out[pl.ds(((m * NA + k) * 2 + x) * 8, 8), :] = v
-        for i in range(3):
-            for j in range(3):
-                for ri in range(2):
-                    direct[pl.ds((comp(m, i, j, ri) * 2 + x) * 8, 8), :] = force[i][j][ri]
-
-
-def pack_lambda_y(lam, up, down):
-    for c in range(32):
-        for x in range(2):
-            to = pl.ds(c * 8 + x * 4, 4)
-            up[to, :] = lam[pl.ds((c * 2 + x) * 8 + 1, 4, stride=2), :]
-            down[to, :] = lam[pl.ds((c * 2 + x) * 8, 4, stride=2), :]
-
-
-def forward_body(*refs):
-    links, incoming, ynext, yprev, xnext, xprev = refs[:6]
-    bufs, (omega, lam, direct, up, down) = refs[6:13], refs[13:18]
-    loops, inner = refs[18:]
-    fill_links_local(links, bufs)
-    fill_links_y(ynext, yprev, bufs)
-    fill_links_x(xnext, xprev, bufs)
-    take_incoming(incoming, inner)
-
-    @pl.loop(0, 2)
-    def _(x):
-        forward(bufs, inner, loops, omega, lam, direct, x)
-
-    pack_lambda_y(lam, up, down)
-
-
-def pack_lambda_x_body(lam, ynext, yprev, up, down):
-    for c in range(32):
-        to = pl.ds(c * 8, 8)
-        up[to, :] = lam[pl.ds((c * 2 + 1) * 8, 8), :]
-        down[to, :] = lam[pl.ds(c * 16, 8), :]
-    for k in range(NA):
-        to = pl.ds(256 + k * 4, 4)
-        up[to, :] = ynext[pl.ds(k * 8 + 4, 4), :]
-        down[to, :] = yprev[pl.ds((NA + k) * 8, 4), :]
-
-
-def backward(bufs, lams, omega, direct, sums, result, x):
-    here = [0, 0, 0, 0]
-    started = set()
-
-    def gather(d, m):
-        for i in range(3):
-            for j in range(3):
-                for ri in range(2):
-                    at = pl.ds(comp(d, i, j, ri) * 8, 8)
-                    sums[at, :] = sums[at, :] + m[i][j][ri] if d in started else m[i][j][ri]
-        started.add(d)
-
-    for p, (m, n) in enumerate(PAIRS):
-        la, ld = lam_at(lams, m, here, x), lam_at(lams, n, here, x)
-        lb = carried(link(bufs, m, here, x), lam_at(lams, n, step((m, 1)), x))
-        lc = carried(link(bufs, n, here, x), lam_at(lams, m, step((n, 1)), x))
-        loop = load_matrix(
-            lambda i, j, ri: omega[pl.ds(((p * 18 + (i * 3 + j) * 2 + ri) * 2 + x) * 8, 8), :]
-        )
+            for n in mine:
+                e, g, h = [link(bufs, which, offset, x) for which, offset in lower_fields(m, n)]
+                term = mm(mm(e, g, True, False), h)
+                value = term if value is None else madd(value, term)
+            store_cells(low, m * 18, x, value)
+
+
+def finish_forward(bufs, inner, loops, low, lam_out, direct):
+    for x in range(2):
+        for m in range(4):
+            u = link(bufs, m, step(), x)
+            below = load_cells(low, m * 18, x)
+            v = skew_product(below, u, True)
+            for p, (f, s) in enumerate(PAIRS):
+                if m == f:
+                    v = [v[k] - loops[cells(p * 9, k, x), :] for k in range(9)]
+                if m == s:
+                    v = [v[k] + loops[cells(p * 9, k, x), :] for k in range(9)]
+            mean = (v[0] + v[1] + v[2]) * (1.0 / 3.0)
+            v = [(0.5 * smear_weight) * (v[k] - mean) for k in range(3)] + [
+                (0.5 * smear_weight) * v[k] for k in range(3, 9)
+            ]
+            lam, force = exponent_force(v, u, load_cells(inner, m * 18, x), below)
+            for k, v in enumerate(lam[:2] + lam[3:]):
+                lam_out[cells(m * NA, k, x), :] = v
+            store_cells(direct, m * 18, x, force)
+
+
+def backward_items(wanted, bufs, lams, omega, sums, acc):
+    planes, lowers = items(wanted)
+    begun = {(d, x) for w in range(wanted) for _, m, n, x in items(w)[0] for d in (m, n)}
+
+    def gather(d, x, m):
+        store_cells(sums, d * 18, x, madd(load_cells(sums, d * 18, x), m) if (d, x) in begun else m)
+        begun.add((d, x))
+
+    for p, m, n, x in planes:
+        fields = plane_fields(m, n)
+        a, d = [link(bufs, which, offset, x) for which, offset in fields[:2]]
+        la, ld, lb, lc = [lam_at(lams, which, offset, x) for which, offset in fields]
+        lb, lc = carried(a, lb), carried(d, lc)
+        loop = load_cells(omega, p * 18, x)
         z = [ld[k] - la[k] for k in range(9)]
         first = anti([z[k] + lc[k] for k in range(9)])
         second = anti([lb[k] - z[k] for k in range(9)])
-        gather(m, msub(mm(first, loop, False, True), mm(loop, anti(lb), True, False)))
-        gather(n, msub(mm(second, loop), mm(loop, anti(lc))))
+        gather(m, x, msub(mm(first, loop, False, True), mm(loop, anti(lb), True, False)))
+        gather(n, x, msub(mm(second, loop), mm(loop, anti(lc))))
     for m in range(4):
-        f = load_matrix(lambda i, j, ri: sums[pl.ds(comp(m, i, j, ri) * 8, 8), :])
-        force = mm(f, link(bufs, m, here, x))
-        for n in range(4):
-            if n == m:
+        for x in range(2):
+            mine = [n for mm_, n, xx in lowers if (mm_, xx) == (m, x)]
+            if not mine:
                 continue
-            back = step((n, -1))
-            e, g, h = link(bufs, n, back, x), link(bufs, m, back, x), link(bufs, n, step((n, -1), (m, 1)), x)
-            le, lg, lh = (
-                lam_at(lams, n, back, x),
-                lam_at(lams, m, back, x),
-                lam_at(lams, n, step((n, -1), (m, 1)), x),
-            )
-            inside = madd(mm(anti([lg[k] - le[k] for k in range(9)]), g), mm(g, anti(lh)))
-            force = madd(force, mm(mm(e, inside, True, False), h))
-        for i in range(3):
-            for j in range(3):
-                for ri in range(2):
-                    at = pl.ds((comp(m, i, j, ri) * 2 + x) * 8, 8)
-                    result[at, :] = force[i][j][ri] + direct[at, :]
-
-
-def give_force(result, out):
-    for c in range(144):
-        out[pl.ds(c * 8, 4), :] = result[pl.ds(c * 8, 4, stride=2), :]
-        out[pl.ds(c * 8 + 4, 4), :] = result[pl.ds(c * 8 + 1, 4, stride=2), :]
-
-
-def backward_body(*refs):
-    bufs, (omega, lam, direct, ynext, yprev, xnext, xprev, out) = refs[:7], refs[7:15]
-    lams, (sums, result) = refs[15:22], refs[22:]
+            force = load_cells(acc, m * 18, x)
+            for n in mine:
+                fields = lower_fields(m, n)
+                e, g, h = [link(bufs, which, offset, x) for which, offset in fields]
+                le, lg, lh = [lam_at(lams, which, offset, x) for which, offset in fields]
+                inside = madd(mm(anti([lg[k] - le[k] for k in range(9)]), g), mm(g, anti(lh)))
+                force = madd(force, mm(mm(e, inside, True, False), h))
+            store_cells(acc, m * 18, x, force)
+
+
+def finish_backward(bufs, sums, acc, out):
+    for x in range(2):
+        for m in range(4):
+            f = load_cells(sums, m * 18, x)
+            force = madd(mm(f, link(bufs, m, step(), x)), load_cells(acc, m * 18, x))
+            store_cells(acc, m * 18, x, force)
+            for k in range(18):
+                at = ((m * 18 + k) * 2 + x) * 8
+                out[pl.ds(at, 4), :] = acc[pl.ds(at, 4, stride=2), :]
+                out[pl.ds(at + 4, 4), :] = acc[pl.ds(at + 1, 4, stride=2), :]
+
+
+def links_local_body(*refs):
+    links, incoming = refs[:2]
+    bufs, (inner, omega, loops, low) = refs[2:9], refs[9:]
+    fill_links_local(links, bufs)
+    take_incoming(incoming, inner)
+    forward_items(0, bufs, omega, loops, low)
+
+
+def links_y_body(*refs):
+    ynext, yprev = refs[:2]
+    bufs, (omega, loops, low) = refs[12:19], refs[19:]
+    fill_links_y(ynext, yprev, bufs)
+    forward_items(1, bufs, omega, loops, low)
+
+
+def links_x_body(*refs):
+    xnext, corner, xprev, inner = refs[:4]
+    bufs, (omega, loops, low, lam, direct, up, down) = refs[14:21], refs[21:]
+    fill_links_x(xnext, corner, xprev, bufs)
+    forward_items(2, bufs, omega, loops, low)
+    finish_forward(bufs, inner, loops, low, lam, direct)
+
+    def reader(row):
+        return lambda d, q, x: lam[pl.ds(((d * NA + q) * 2 + x) * 8 + row, 4, stride=2), :]
+
+    pack_y(up, down, NA, reader(1), reader(0))
+
+
+def lambda_local_body(*refs):
+    bufs, (omega, lam) = refs[:7], refs[7:9]
+    acc, lams, sums = refs[10], refs[11:18], refs[18]
     fill_lambda_local(lam, lams)
+    backward_items(0, bufs, lams, omega, sums, acc)
+
+
+def lambda_y_body(*refs):
+    bufs, (omega, ynext, yprev) = refs[:7], refs[7:10]
+    acc, lams, sums = refs[19], refs[20:27], refs[27]
     fill_lambda_y(ynext, yprev, lams)
+    backward_items(1, bufs, lams, omega, sums, acc)
+
+
+def lambda_x_body(*refs):
+    bufs, (omega, xnext, xprev) = refs[:7], refs[7:10]
+    out, acc, lams, sums = refs[19], refs[20], refs[21:28], refs[28]
     fill_lambda_x(xnext, xprev, lams)
-
-    @pl.loop(0, 2)
-    def _(x):
-        backward(bufs, lams, omega, direct, sums, result, x)
-
-    give_force(result, out)
+    backward_items(2, bufs, lams, omega, sums, acc)
+    finish_backward(bufs, sums, acc, out)
 
 
 def rows(n):
@@ -597,45 +652,52 @@
     return [(n if key in base_dir else 4 * n) * 4 * ROWS for key in range(7)]
 
 
-def call(body, outs, args, scratch=()):
+def call(body, args, outs, kept=(), cost=0, first=0):
+    shapes = [rows(n) for n in outs]
+    shapes[first:first] = [rows(a.shape[0]) for a in kept]
     return pl.pallas_call(
         body,
-        out_shape=tuple(rows(n) for n in outs),
-        in_specs=[pl.BlockSpec(memory_space=pltpu.VMEM)] * len(args),
-        out_specs=(pl.BlockSpec(memory_space=pltpu.VMEM),) * len(outs),
-        scratch_shapes=[pltpu.VMEM((n, 128), jnp.float32) for n in scratch],
+        out_shape=tuple(shapes),
+        in_specs=[pl.BlockSpec(memory_space=pltpu.VMEM)] * (len(args) + len(kept)),
+        out_specs=(pl.BlockSpec(memory_space=pltpu.VMEM),) * len(shapes),
+        input_output_aliases={len(args) + k: first + k for k in range(len(kept))},
+        cost_estimate=pl.CostEstimate(flops=cost, bytes_accessed=0, transcendentals=0) if cost else None,
         compiler_params=pltpu.CompilerParams(vmem_limit_bytes=VM),
-    )(*args)
+    )(*args, *kept)
 
 
 def shifted(shard, axis, by):
     length = lax.axis_size(axis)
     return lax.ppermute(shard, axis, [(i, (i + by) % length) for i in range(length)])
+
+
+def diagonal(shard, by_x, by_y):
+    nx, ny = lax.axis_size("gx"), lax.axis_size("gy")
+    pairs = [(i * ny + j, (i + by_x) % nx * ny + (j + by_y) % ny) for i in range(nx) for j in range(ny)]
+    return lax.ppermute(shard, ("gx", "gy"), pairs)
 
 
 def body(links, incoming):
     links = jnp.transpose(links, (0, 1, 2, 3, 4, 6, 5, 7)).reshape(144 * ROWS, 128)
     shape = incoming.shape
     incoming = incoming.reshape(1152, 128)
-    up, down = call(pack_y_body, (408, 408), (links,))
-    yprev, ynext = shifted(up, "gy", 1), shifted(down, "gy", -1)
-    up, down = call(pack_x_body, (456, 456), (links, ynext, yprev))
-    xprev, xnext = shifted(up, "gx", 1), shifted(down, "gx", -1)
-    *kept, up, down = call(
-        forward_body,
-        buffer_rows(NC) + [6 * 18 * 16, 32 * 16, 1152, 256, 256],
-        (links, incoming, ynext, yprev, xnext, xprev),
-        (54 * 8, 1152),
+    yup, ydown, xdown, corner = call(pack_first_body, (links,), (408, 312, 312, 48))
+    yprev, ynext = shifted(yup, "gy", 1), shifted(ydown, "gy", -1)
+    xnext, corner = shifted(xdown, "gx", -1), diagonal(corner, -1, 1)
+    (xup,) = call(pack_x_body, (links, ynext), (456,))
+    xprev = shifted(xup, "gx", 1)
+    inner, *kept = (lambda r: (r[7], *r[:7], *r[8:]))(
+        call(links_local_body, (links, incoming), buffer_rows(NC) + [1152, 1728, 864, 1152])
     )
-    yprev, ynext = shifted(up, "gy", 1), shifted(down, "gy", -1)
-    up, down = call(pack_lambda_x_body, (288, 288), (kept[8], ynext, yprev))
-    xprev, xnext = shifted(up, "gx", 1), shifted(down, "gx", -1)
-    (out,) = call(
-        backward_body,
-        (1152,),
-        (*kept, ynext, yprev, xnext, xprev),
-        buffer_rows(NA) + [72 * 8, 1152],
-    )
+    kept = call(links_y_body, (ynext, yprev), (), kept)
+    r = call(links_x_body, (xnext, corner, xprev, inner), (512, 1152, 256, 192), kept)
+    bufs, omega, (lam, acc, yup, ydown) = r[:7], r[7], r[10:]
+    yprev, ynext = shifted(yup, "gy", 1), shifted(ydown, "gy", -1)
+    kept = call(lambda_local_body, (*bufs, omega, lam), buffer_rows(NA) + [1152], (acc,))
+    xup, xdown = call(pack_lambda_x_body, (lam, ynext, yprev), (288, 224))
+    xprev, xnext = shifted(xup, "gx", 1), shifted(xdown, "gx", -1)
+    kept = call(lambda_y_body, (*bufs, omega, ynext, yprev), (), kept)
+    out = call(lambda_x_body, (*bufs, omega, xnext, xprev), (1152,), kept, first=1)[0]
     return out.reshape(shape)
 
 

time: 58.7 us -> 50.4 us (0.86)
  waiting for transfers between devices: 32.3 us -> 12.2 us
  starting transfers between devices: 14.1 us -> 20.4 us
  Pallas kernels: 11 us -> 15.1 us
  local copies, waits for them, and re-layouts: 1.17 us -> 2.42 us
    ppermute x8, waiting for transfers between devices: 32.3 us -> 12.1 us  [shifted(): lax.ppermute(shard, axis, [(i, (i + by) % length) for i in range(length)])]
    ppermute x8, starting transfers between devices: 14.1 us -> 19.5 us  [shifted(): lax.ppermute(shard, axis, [(i, (i + by) % length) for i in range(length)])]
    pallas_call x5 -> x9, Pallas kernels: 11 us -> 15.1 us  [call(): pl.pallas_call(body, out_shape=tuple(shapes), in_specs=[pl.BlockSpec(memo...]
    unnamed x4 -> x6, local copies, waits for them, and re-layouts: 1.17 us -> 2.42 us
    ppermute x0 -> x1, starting transfers between devices: none -> 0.87 us  [diagonal(): return lax.ppermute(shard, ('gx', 'gy'), pairs)]
  transfers between devices with their start and end apart: 8 -> 9, of which waited for: 8 -> 5; matrix products, arithmetic and copies ran while one was open for 0% -> 0% of each run, Pallas kernels for 0% -> 18%
where the time goes in v1:
time: 50.4 us; the launch traced here: 50.1 us
  starting transfers between devices  20.4 us (40%)
  Pallas kernels  15.1 us (30%)
  waiting for transfers between devices  12.2 us (24%)
  local copies, waits for them, and re-layouts  2.42 us (5%)
    ppermute x8, starting transfers between devices, shifted(): lax.ppermute(shard, axis, [(i, (i + by) % length) for i in range(length)])  19.5 us
    pallas_call x9, Pallas kernels, call(): pl.pallas_call(body, out_shape=tuple(shapes), in_specs=[pl.BlockSpec(memo...  15.1 us
    ppermute x8, waiting for transfers between devices, shifted(): lax.ppermute(shard, axis, [(i, (i + by) % length) for i in range(length)])  12.1 us
    unnamed x6, local copies, waits for them, and re-layouts  2.42 us
  transfers between devices with their start and end apart: 9, of which 5 were waited for; matrix products, arithmetic and copies ran while one was open for 0% of the time, Pallas kernels for 18%

profile of v1, /device:TPU:0, one launch (start us, length us, event | category | flops | bytes accessed | tf_op | source)
XLA Modules:
  0.0 50.1 jit_solution(5776061101849082133)
XLA Ops:
  0.0 1.2 %copy-done.1 = f32[4,3,3,2,2,2,6,128]{7,5,6,4,3,2,1,0:T(2,128)S(1)} copy-done((f32[4,3,3,2,2,2,6,128]{7,5,6,4,3,2,1,0:T(2,128)S(1)}, f32[4,3,3,2,2,2,6,128]{7,5,6,4,3,2,1,0:T(2,128)}, u32[]{:S(2)}) %copy-start.1) | copy-done | bytes 884760
  1.2 0.1 shard_map.28
  1.3 4.0 %collective-permute-start.2 = (f32[312,128]{1,0:T(8,128)S(1)}, f32[312,128]{1,0:T(8,128)S(1)}, u32[]{:S(2)}, u32[]{:S(2)}) collective-permute-start(f32[312,128]{1,0:T(8,128)S(1)} %get-tuple-element.65), channel_id=1, source_target_pairs={{0,15},{1,0},{2,1},{3,2},{4,3},{5,4},{6,5},{7,6},{8,7},{9,8},{10,9... | collective-permute-start | bytes 479240 | tf_op jit(solution)/shard_map/ppermute | solution.py:671
  5.2 2.8 %collective-permute-done.2.ynext.refs_0_ = f32[312,128]{1,0:T(8,128)S(1)} collective-permute-done((f32[312,128]{1,0:T(8,128)S(1)}, f32[312,128]{1,0:T(8,128)S(1)}, u32[]{:S(2)}, u32[]{:S(2)}) %collective-permute-start.2) | collective-permute-done | bytes 159776 | tf_op jit(solution)/shard_map/ppermute | solution.py:671
  8.1 3.7 %collective-permute-start.3 = (f32[456,128]{1,0:T(8,128)S(1)}, f32[456,128]{1,0:T(8,128)S(1)}, u32[]{:S(2)}, u32[]{:S(2)}) collective-permute-start(f32[456,128]{1,0:T(8,128)S(1)} %shard_map.29), channel_id=1, source_target_pairs={{0,16},{16,32},{32,48},{48,64},{64,80},{80,96},{96,112},{112,0},{1... | collective-permute-start | bytes 700424 | tf_op jit(solution)/shard_map/ppermute | solution.py:671
  11.7 0.0 collective-permute-start.4
  11.7 2.4 %collective-permute-start = (f32[312,128]{1,0:T(8,128)S(1)}, f32[312,128]{1,0:T(8,128)S(1)}, u32[]{:S(2)}, u32[]{:S(2)}) collective-permute-start(f32[312,128]{1,0:T(8,128)S(1)} %get-tuple-element.63), channel_id=1, source_target_pairs={{0,112},{16,0},{32,16},{48,32},{64,48},{80,64},{96,80},{112,96},{1... | collective-permute-start | bytes 479240 | tf_op jit(solution)/shard_map/ppermute | solution.py:671
  14.1 0.9 %collective-permute-start.1 = (f32[48,128]{1,0:T(8,128)S(1)}, f32[48,128]{1,0:T(8,128)S(1)}, u32[]{:S(2)}, u32[]{:S(2)}) collective-permute-start(f32[48,128]{1,0:T(8,128)S(1)} %get-tuple-element.64), channel_id=1, source_target_pairs={{0,113},{1,114},{2,115},{3,116},{4,117},{5,118},{6,119},{7,120},{8... | collective-permute-start | bytes 73736 | tf_op jit(solution)/shard_map/ppermute | solution.py:677
  15.0 1.2 %shard_map.30 = (f32[3456,128]{1,0:T(8,128)S(1)}, f32[3456,128]{1,0:T(8,128)S(1)}, f32[3456,128]{1,0:T(8,128)S(1)}, f32[3456,128]{1,0:T(8,128)S(1)}, f32[3456,12...) custom-call(f32[1728,128]{1,0:T(8,128)S(1)} %bitcast.7, ...), custom_call_target="tpu_custom_call" | custom-call | tf_op jit(solution)/shard_map/pallas_call | solution.py:658
  16.2 3.7 %collective-permute-done.4.refs_1_ = f32[408,128]{1,0:T(8,128)S(1)} collective-permute-done((f32[408,128]{1,0:T(8,128)S(1)}, f32[408,128]{1,0:T(8,128)S(1)}, u32[]{:S(2)}, u32[]{:S(2)}) %collective-permute-start.4) | collective-permute-done | bytes 208928 | tf_op jit(solution)/shard_map/ppermute | solution.py:671
  19.9 1.1 %shard_map.31 = (f32[3456,128]{1,0:T(8,128)S(1)}, f32[3456,128]{1,0:T(8,128)S(1)}, f32[3456,128]{1,0:T(8,128)S(1)}, f32[3456,128]{1,0:T(8,128)S(1)}, f32[3456,12...) custom-call(f32[312,128]{1,0:T(8,128)S(1)} %collective-permute-done., ...), custom_call_target="tpu_custom_call", output_to_operand_aliasing={{0}: (2, {}), {1}: (3, {}), {2}: (4, {}), {3}: (5, {}), {4}... | custom-call | tf_op jit(solution)/shard_map/pallas_call | solution.py:658
  21.0 0.0 collective-permute-done.1.refs_1_
  21.0 3.0 %collective-permute-done.refs_0_ = f32[312,128]{1,0:T(8,128)S(1)} collective-permute-done((f32[312,128]{1,0:T(8,128)S(1)}, f32[312,128]{1,0:T(8,128)S(1)}, u32[]{:S(2)}, u32[]{:S(2)}) %collective-permute-start) | collective-permute-done | bytes 159776 | tf_op jit(solution)/shard_map/ppermute | solution.py:671
  24.0 2.3 %shard_map.32 = (f32[3456,128]{1,0:T(8,128)S(1)}, f32[3456,128]{1,0:T(8,128)S(1)}, f32[3456,128]{1,0:T(8,128)S(1)}, f32[3456,128]{1,0:T(8,128)S(1)}, f32[3456,12...) custom-call(f32[312,128]{1,0:T(8,128)S(1)} %collective-permute-done., ...), custom_call_target="tpu_custom_call", output_to_operand_aliasing={{0}: (4, {}), {1}: (5, {}), {2}: (6, {}), {3}: (7, {}), {4}... | custom-call | tf_op jit(solution)/shard_map/pallas_call | solution.py:658
  26.3 1.2 %copy-done = f32[3456,128]{1,0:T(8,128)} copy-done((f32[3456,128]{1,0:T(8,128)}, f32[3456,128]{1,0:T(8,128)S(1)}, u32[]{:S(2)}) %copy-start) | copy-done | bytes 1769496
  27.6 0.1 collective-permute-start.6
  27.7 3.8 %collective-permute-start.5 = (f32[192,128]{1,0:T(8,128)S(1)}, f32[192,128]{1,0:T(8,128)S(1)}, u32[]{:S(2)}, u32[]{:S(2)}) collective-permute-start(f32[192,128]{1,0:T(8,128)S(1)} %get-tuple-element.97), channel_id=1, source_target_pairs={{0,15},{1,0},{2,1},{3,2},{4,3},{5,4},{6,5},{7,6},{8,7},{9,8},{10,9... | collective-permute-start | bytes 294920 | tf_op jit(solution)/shard_map/ppermute | solution.py:671
  31.4 2.2 %collective-permute-done.5.ynext.refs_8_ = f32[192,128]{1,0:T(8,128)S(1)} collective-permute-done((f32[192,128]{1,0:T(8,128)S(1)}, f32[192,128]{1,0:T(8,128)S(1)}, u32[]{:S(2)}, u32[]{:S(2)}) %collective-permute-start.5) | collective-permute-done | bytes 98336 | tf_op jit(solution)/shard_map/ppermute | solution.py:671
  33.7 0.5 collective-permute-done.6.yprev.refs_9_
  34.2 1.4 %collective-permute-start.8 = (f32[288,128]{1,0:T(8,128)S(1)}, f32[288,128]{1,0:T(8,128)S(1)}, u32[]{:S(2)}, u32[]{:S(2)}) collective-permute-start(f32[288,128]{1,0:T(8,128)S(1)} %get-tuple-element.100), channel_id=1, source_target_pairs={{0,16},{16,32},{32,48},{48,64},{64,80},{80,96},{96,112},{112,0},{1... | collective-permute-start | bytes 442376 | tf_op jit(solution)/shard_map/ppermute | solution.py:671
  35.6 4.3 %collective-permute-start.7 = (f32[224,128]{1,0:T(8,128)S(1)}, f32[224,128]{1,0:T(8,128)S(1)}, u32[]{:S(2)}, u32[]{:S(2)}) collective-permute-start(f32[224,128]{1,0:T(8,128)S(1)} %get-tuple-element.99), channel_id=1, source_target_pairs={{0,112},{16,0},{32,16},{48,32},{64,48},{80,64},{96,80},{112,96},{1... | collective-permute-start | bytes 344072 | tf_op jit(solution)/shard_map/ppermute | solution.py:671
  39.9 3.1 %shard_map.34 = (f32[1152,128]{1,0:T(8,128)S(1)}, f32[1536,128]{1,0:T(8,128)S(1)}, f32[1536,128]{1,0:T(8,128)S(1)}, f32[1536,128]{1,0:T(8,128)S(1)}, f32[1536,12...) custom-call(f32[3456,128]{1,0:T(8,128)S(1)} %get-tuple-element.88.re, ...), custom_call_target="tpu_custom_call", output_to_operand_aliasing={{0}: (9, {})} | custom-call | tf_op jit(solution)/shard_map/pallas_call | solution.py:658
  43.0 3.4 %shard_map.35 = (f32[1152,128]{1,0:T(8,128)S(1)}, f32[1536,128]{1,0:T(8,128)S(1)}, f32[1536,128]{1,0:T(8,128)S(1)}, f32[1536,128]{1,0:T(8,128)S(1)}, f32[1536,12...) custom-call(f32[3456,128]{1,0:T(8,128)S(1)} %get-tuple-element.88.re, ...), custom_call_target="tpu_custom_call", output_to_operand_aliasing={{0}: (10, {}), {1}: (11, {}), {2}: (12, {}), {3}: (13, {}),... | custom-call | tf_op jit(solution)/shard_map/pallas_call | solution.py:658
  46.4 3.7 %shard_map.36 = (f32[1152,128]{1,0:T(8,128)}, f32[1152,128]{1,0:T(8,128)S(1)}, f32[1536,128]{1,0:T(8,128)S(1)}, f32[1536,128]{1,0:T(8,128)S(1)}, f32[1536,128]{1...) custom-call(f32[3456,128]{1,0:T(8,128)S(1)} %get-tuple-element.88.re, ...), custom_call_target="tpu_custom_call", output_to_operand_aliasing={{1}: (10, {}), {2}: (11, {}), {3}: (12, {}), {4}: (13, {}),... | custom-call | tf_op jit(solution)/shard_map/pallas_call | solution.py:658
  (9 shorter events, 0.1 us)
Async XLA Ops:
  0.0 1.2 %copy-start.1 = (f32[4,3,3,2,2,2,6,128]{7,5,6,4,3,2,1,0:T(2,128)S(1)}, f32[4,3,3,2,2,2,6,128]{7,5,6,4,3,2,1,0:T(2,128)}, u32[]{:S(2)}) copy-start(f32[4,3,3,2,2,2,6,128]{7,5,6,4,3,2,1,0:T(2,128)} %param.2) | copy-start | bytes 2654212
  1.2 13.8 %copy-start.2 = (f32[4,3,3,2,2,2,4,128]{7,6,5,4,3,2,1,0:T(4,128)S(1)}, f32[4,3,3,2,2,2,4,128]{7,6,5,4,3,2,1,0:T(4,128)}, u32[]{:S(2)}) copy-start(f32[4,3,3,2,2,2,4,128]{7,6,5,4,3,2,1,0:T(4,128)} %param.3) | copy-start | bytes 1769476
  1.3 6.8 %collective-permute-start.2 = (f32[312,128]{1,0:T(8,128)S(1)}, f32[312,128]{1,0:T(8,128)S(1)}, u32[]{:S(2)}, u32[]{:S(2)}) collective-permute-start(f32[312,128]{1,0:T(8,128)S(1)} %get-tuple-element.65), channel_id=1, source_target_pairs={{0,15},{1,0},{2,1},{3,2},{4,3},{5,4},{6,5},{7,6},{8,7},{9,8},{10,9... | collective-permute-start | bytes 479240 | tf_op jit(solution)/shard_map/ppermute | solution.py:671
  8.1 15.9 %collective-permute-start.3 = (f32[456,128]{1,0:T(8,128)S(1)}, f32[456,128]{1,0:T(8,128)S(1)}, u32[]{:S(2)}, u32[]{:S(2)}) collective-permute-start(f32[456,128]{1,0:T(8,128)S(1)} %shard_map.29), channel_id=1, source_target_pairs={{0,16},{16,32},{32,48},{48,64},{64,80},{80,96},{96,112},{112,0},{1... | collective-permute-start | bytes 700424 | tf_op jit(solution)/shard_map/ppermute | solution.py:671
  11.7 8.2 %collective-permute-start.4 = (f32[408,128]{1,0:T(8,128)S(1)}, f32[408,128]{1,0:T(8,128)S(1)}, u32[]{:S(2)}, u32[]{:S(2)}) collective-permute-start(f32[408,128]{1,0:T(8,128)S(1)} %get-tuple-element.67), channel_id=1, source_target_pairs={{0,1},{1,2},{2,3},{3,4},{4,5},{5,6},{6,7},{7,8},{8,9},{9,10},{10,1... | collective-permute-start | bytes 626696 | tf_op jit(solution)/shard_map/ppermute | solution.py:671
  11.7 12.3 %collective-permute-start = (f32[312,128]{1,0:T(8,128)S(1)}, f32[312,128]{1,0:T(8,128)S(1)}, u32[]{:S(2)}, u32[]{:S(2)}) collective-permute-start(f32[312,128]{1,0:T(8,128)S(1)} %get-tuple-element.63), channel_id=1, source_target_pairs={{0,112},{16,0},{32,16},{48,32},{64,48},{80,64},{96,80},{112,96},{1... | collective-permute-start | bytes 479240 | tf_op jit(solution)/shard_map/ppermute | solution.py:671
  14.1 6.9 %collective-permute-start.1 = (f32[48,128]{1,0:T(8,128)S(1)}, f32[48,128]{1,0:T(8,128)S(1)}, u32[]{:S(2)}, u32[]{:S(2)}) collective-permute-start(f32[48,128]{1,0:T(8,128)S(1)} %get-tuple-element.64), channel_id=1, source_target_pairs={{0,113},{1,114},{2,115},{3,116},{4,117},{5,118},{6,119},{7,120},{8... | collective-permute-start | bytes 73736 | tf_op jit(solution)/shard_map/ppermute | solution.py:677
  26.3 1.3 %copy-start = (f32[3456,128]{1,0:T(8,128)}, f32[3456,128]{1,0:T(8,128)S(1)}, u32[]{:S(2)}) copy-start(f32[3456,128]{1,0:T(8,128)S(1)} %get-tuple-element.92.refs_4_) | copy-start | bytes 5308420
  27.6 6.5 %collective-permute-start.6 = (f32[256,128]{1,0:T(8,128)S(1)}, f32[256,128]{1,0:T(8,128)S(1)}, u32[]{:S(2)}, u32[]{:S(2)}) collective-permute-start(f32[256,128]{1,0:T(8,128)S(1)} %get-tuple-element.98), channel_id=1, source_target_pairs={{0,1},{1,2},{2,3},{3,4},{4,5},{5,6},{6,7},{7,8},{8,9},{9,10},{10,1... | collective-permute-start | bytes 393224 | tf_op jit(solution)/shard_map/ppermute | solution.py:671
  27.7 6.0 %collective-permute-start.5 = (f32[192,128]{1,0:T(8,128)S(1)}, f32[192,128]{1,0:T(8,128)S(1)}, u32[]{:S(2)}, u32[]{:S(2)}) collective-permute-start(f32[192,128]{1,0:T(8,128)S(1)} %get-tuple-element.97), channel_id=1, source_target_pairs={{0,15},{1,0},{2,1},{3,2},{4,3},{5,4},{6,5},{7,6},{8,7},{9,8},{10,9... | collective-permute-start | bytes 294920 | tf_op jit(solution)/shard_map/ppermute | solution.py:671
  34.2 12.2 %collective-permute-start.8 = (f32[288,128]{1,0:T(8,128)S(1)}, f32[288,128]{1,0:T(8,128)S(1)}, u32[]{:S(2)}, u32[]{:S(2)}) collective-permute-start(f32[288,128]{1,0:T(8,128)S(1)} %get-tuple-element.100), channel_id=1, source_target_pairs={{0,16},{16,32},{32,48},{48,64},{64,80},{80,96},{96,112},{112,0},{1... | collective-permute-start | bytes 442376 | tf_op jit(solution)/shard_map/ppermute | solution.py:671
  35.6 10.8 %collective-permute-start.7 = (f32[224,128]{1,0:T(8,128)S(1)}, f32[224,128]{1,0:T(8,128)S(1)}, u32[]{:S(2)}, u32[]{:S(2)}) collective-permute-start(f32[224,128]{1,0:T(8,128)S(1)} %get-tuple-element.99), channel_id=1, source_target_pairs={{0,112},{16,0},{32,16},{48,32},{64,48},{80,64},{96,80},{112,96},{1... | collective-permute-start | bytes 344072 | tf_op jit(solution)/shard_map/ppermute | solution.py:671

commit v2 on v1

--- a/solution.py
+++ b/solution.py
@@ -8,7 +8,7 @@
 smear_weight = 0.2
 NC, NA = 18, 8
 ROWS = 12
-VM = 40 * 2**20
+VM = 8 * 2**20
 O, YP, YM, ZP, ZM, ZPYM, ZMYP = range(7)
 buffer_of = {(0, 0): O, (1, 0): YP, (-1, 0): YM, (0, 1): ZP, (0, -1): ZM, (-1, 1): ZPYM, (1, -1): ZMYP}
 base_dir = {ZPYM: 1, ZMYP: 2}
@@ -147,7 +147,7 @@
         corner[pl.ds(q * 4, 4), :] = links[pl.ds((18 + q) * 2 * ROWS + 3, 4, stride=2), :]
 
 
-def pack_x_body(links, ynext, up):
+def pack_x_body(links, ynext, yprev, xnext, corner, after, up):
     for q in range(12):
         for d in range(4):
             up[pl.ds((d * 12 + q) * 8, 8), :] = links[pl.ds(((d * 18 + q) * 2 + 1) * ROWS + 2, 8), :]
@@ -155,7 +155,7 @@
         up[pl.ds(408 + q * 4, 4), :] = ynext[pl.ds(q * 8 + 4, 4), :]
 
 
-def pack_lambda_x_body(lam, ynext, yprev, up, down):
+def pack_lambda_x_body(lam, ynext, yprev, after, up, down):
     for c in range(32):
         up[pl.ds(c * 8, 8), :] = lam[pl.ds((c * 2 + 1) * 8, 8), :]
         if c >= NA:
@@ -215,14 +215,18 @@
             bufs[ZMYP][pl.ds(place(k, x) + 2, 8), :] = roll_z(bufs[YP][pl.ds(place(2 * n + k, x) + 2, 8), :], -1)
 
 
-def fill_edges(bufs, n):
+def fill_high(bufs, n):
     for k in range(n):
-        low, high = place(k, 0), place(2 * n + k, 3)
+        high, side = place(2 * n + k, 3), place(n + k, 3)
+        bufs[ZM][pl.ds(high + 2, 8), :] = roll_z(bufs[O][pl.ds(high + 2, 8), :], -1)
+        bufs[YM][pl.ds(side + 3, 4, stride=2), :] = bufs[O][pl.ds(side + 2, 4, stride=2), :]
+
+
+def fill_low(bufs, n):
+    for k in range(n):
+        low = place(k, 0)
         bufs[ZP][pl.ds(low + 2, 8), :] = roll_z(bufs[O][pl.ds(low + 2, 8), :], 1)
-        bufs[ZM][pl.ds(high + 2, 8), :] = roll_z(bufs[O][pl.ds(high + 2, 8), :], -1)
         bufs[YP][pl.ds(low + 2, 4, stride=2), :] = bufs[O][pl.ds(low + 3, 4, stride=2), :]
-        side = place(n + k, 3)
-        bufs[YM][pl.ds(side + 3, 4, stride=2), :] = bufs[O][pl.ds(side + 2, 4, stride=2), :]
 
 
 def fill_links_local(links, bufs):
@@ -259,33 +263,38 @@
     fill_mixed(bufs, NC)
 
 
-def fill_links_x(xnext, corner, xprev, bufs):
-    for d in range(4):
-        for source, xe in ((xnext, 3), (xprev, 0)):
-            if xe == 3 and d == 0:
-                continue
-            slot = d - 1 if xe == 3 else d
-            m = two_rows(lambda q: source[pl.ds((slot * 12 + q) * 8, 8), :])
-
-            def write(q, v):
-                bufs[O][pl.ds(place(d * NC + q, xe) + 2, 8), :] = v
-
-            put(write, m)
-    for source, d, xe, row, at in ((xnext, 3, 3, 0, 288), (xprev, 0, 0, 10, 384)):
-        m = two_rows(lambda q: source[pl.ds(at + q * 2, 2), :])
-
-        def write_edge(q, v):
-            bufs[O][pl.ds(place(d * NC + q, xe) + row, 2), :] = v
-
-        put(write_edge, m)
-    for source, at, buf, d, xe, off in ((corner, 0, YM, 1, 3, 2), (xprev, 408, YP, 0, 0, 3)):
-        m = two_rows(lambda q: source[pl.ds(at + q * 4, 4), :])
-
-        def write_corner(q, v):
-            bufs[buf][pl.ds(place(d * NC + q, xe) + off, 4, stride=2), :] = v
-
-        put(write_corner, m)
-    fill_edges(bufs, NC)
+def fill_column(source, slots, corner, at, bufs, xe, edge, corner_to):
+    for slot, d in enumerate(slots):
+        m = two_rows(lambda q: source[pl.ds((slot * 12 + q) * 8, 8), :])
+
+        def write(q, v):
+            bufs[O][pl.ds(place(d * NC + q, xe) + 2, 8), :] = v
+
+        put(write, m)
+    d, row = edge
+    m = two_rows(lambda q: source[pl.ds(len(slots) * 96 + q * 2, 2), :])
+
+    def write_edge(q, v):
+        bufs[O][pl.ds(place(d * NC + q, xe) + row, 2), :] = v
+
+    put(write_edge, m)
+    buf, corner_dir, off = corner_to
+    m = two_rows(lambda q: corner[pl.ds(at + q * 4, 4), :])
+
+    def write_corner(q, v):
+        bufs[buf][pl.ds(place(corner_dir * NC + q, xe) + off, 4, stride=2), :] = v
+
+    put(write_corner, m)
+
+
+def fill_links_next(xnext, corner, bufs):
+    fill_column(xnext, (1, 2, 3), corner, 0, bufs, 3, (3, 0), (YM, 1, 2))
+    fill_high(bufs, NC)
+
+
+def fill_links_prev(xprev, bufs):
+    fill_column(xprev, (0, 1, 2, 3), xprev, 408, bufs, 0, (0, 10), (YP, 0, 3))
+    fill_low(bufs, NC)
 
 
 def fill_lambda_local(lam, bufs):
@@ -332,7 +341,8 @@
     for k in range(NA):
         bufs[YM][pl.ds(place(NA + k, 3) + 2, 4, stride=2), :] = xnext[pl.ds(192 + k * 4, 4), :]
         bufs[YP][pl.ds(place(k, 0) + 3, 4, stride=2), :] = xprev[pl.ds(256 + k * 4, 4), :]
-    fill_edges(bufs, NA)
+    fill_high(bufs, NA)
+    fill_low(bufs, NA)
 
 
 def step(*signed):
@@ -468,8 +478,10 @@
 def level(fields, x):
     found = 0
     for _, offset in fields:
-        if x + offset[0] not in (0, 1):
-            found = 2
+        if x + offset[0] == -1:
+            found = 3
+        elif x + offset[0] == 2:
+            found = max(found, 2)
         elif offset[1]:
             found = max(found, 1)
     return found
@@ -527,8 +539,8 @@
             store_cells(low, m * 18, x, value)
 
 
-def finish_forward(bufs, inner, loops, low, lam_out, direct):
-    for x in range(2):
+def finish_forward(xs, bufs, inner, loops, low, lam_out, direct):
+    for x in xs:
         for m in range(4):
             u = link(bufs, m, step(), x)
             below = load_cells(low, m * 18, x)
@@ -603,18 +615,21 @@
 
 
 def links_y_body(*refs):
-    ynext, yprev = refs[:2]
-    bufs, (omega, loops, low) = refs[12:19], refs[19:]
+    ynext, yprev, xnext, corner, inner = refs[:5]
+    bufs, (omega, loops, low, lam, direct) = refs[15:22], refs[22:]
     fill_links_y(ynext, yprev, bufs)
     forward_items(1, bufs, omega, loops, low)
+    fill_links_next(xnext, corner, bufs)
+    forward_items(2, bufs, omega, loops, low)
+    finish_forward((1,), bufs, inner, loops, low, lam, direct)
 
 
 def links_x_body(*refs):
-    xnext, corner, xprev, inner = refs[:4]
+    xprev, inner = refs[:2]
     bufs, (omega, loops, low, lam, direct, up, down) = refs[14:21], refs[21:]
-    fill_links_x(xnext, corner, xprev, bufs)
-    forward_items(2, bufs, omega, loops, low)
-    finish_forward(bufs, inner, loops, low, lam, direct)
+    fill_links_prev(xprev, bufs)
+    forward_items(3, bufs, omega, loops, low)
+    finish_forward((0,), bufs, inner, loops, low, lam, direct)
 
     def reader(row):
         return lambda d, q, x: lam[pl.ds(((d * NA + q) * 2 + x) * 8 + row, 4, stride=2), :]
@@ -641,6 +656,7 @@
     out, acc, lams, sums = refs[19], refs[20], refs[21:28], refs[28]
     fill_lambda_x(xnext, xprev, lams)
     backward_items(2, bufs, lams, omega, sums, acc)
+    backward_items(3, bufs, lams, omega, sums, acc)
     finish_backward(bufs, sums, acc, out)
 
 
@@ -684,17 +700,17 @@
     yup, ydown, xdown, corner = call(pack_first_body, (links,), (408, 312, 312, 48))
     yprev, ynext = shifted(yup, "gy", 1), shifted(ydown, "gy", -1)
     xnext, corner = shifted(xdown, "gx", -1), diagonal(corner, -1, 1)
-    (xup,) = call(pack_x_body, (links, ynext), (456,))
-    xprev = shifted(xup, "gx", 1)
     inner, *kept = (lambda r: (r[7], *r[:7], *r[8:]))(
         call(links_local_body, (links, incoming), buffer_rows(NC) + [1152, 1728, 864, 1152])
     )
-    kept = call(links_y_body, (ynext, yprev), (), kept)
-    r = call(links_x_body, (xnext, corner, xprev, inner), (512, 1152, 256, 192), kept)
+    (xup,) = call(pack_x_body, (links, ynext, yprev, xnext, corner, kept[-1]), (456,))
+    xprev = shifted(xup, "gx", 1)
+    kept = call(links_y_body, (ynext, yprev, xnext, corner, inner), (512, 1152), kept)
+    r = call(links_x_body, (xprev, inner), (256, 192), kept)
     bufs, omega, (lam, acc, yup, ydown) = r[:7], r[7], r[10:]
     yprev, ynext = shifted(yup, "gy", 1), shifted(ydown, "gy", -1)
     kept = call(lambda_local_body, (*bufs, omega, lam), buffer_rows(NA) + [1152], (acc,))
-    xup, xdown = call(pack_lambda_x_body, (lam, ynext, yprev), (288, 224))
+    xup, xdown = call(pack_lambda_x_body, (lam, ynext, yprev, kept[-1]), (288, 224))
     xprev, xnext = shifted(xup, "gx", 1), shifted(xdown, "gx", -1)
     kept = call(lambda_y_body, (*bufs, omega, ynext, yprev), (), kept)
     out = call(lambda_x_body, (*bufs, omega, xnext, xprev), (1152,), kept, first=1)[0]

time: 50.4 us -> 46.7 us (0.927)
  Pallas kernels: 15.1 us -> 10.6 us
  waiting for transfers between devices: 12.2 us -> 13.9 us
  starting transfers between devices: 20.4 us -> 19.8 us
    pallas_call x9, Pallas kernels: 15.1 us -> 10.6 us  [call(): pl.pallas_call(body, out_shape=tuple(shapes), in_specs=[pl.BlockSpec(memo...]
    ppermute x1, waiting for transfers between devices: 0.01 us -> 4.27 us  [diagonal(): return lax.ppermute(shard, ('gx', 'gy'), pairs)]
    ppermute x8, waiting for transfers between devices: 12.1 us -> 9.58 us  [shifted(): lax.ppermute(shard, axis, [(i, (i + by) % length) for i in range(length)])]
    ppermute x1, starting transfers between devices: 0.87 us -> 0.01 us  [diagonal(): return lax.ppermute(shard, ('gx', 'gy'), pairs)]
    unnamed x6 -> x4, local copies, waits for them, and re-layouts: 2.42 us -> 2.23 us
  transfers between devices with their start and end apart: 9 -> 9, of which waited for: 5 -> 6; matrix products, arithmetic and copies ran while one was open for 0% -> 0% of each run, Pallas kernels for 18% -> 15%
where the time goes in v2:
time: 46.7 us; the launch traced here: 46.5 us
  starting transfers between devices  19.8 us (42%)
  waiting for transfers between devices  13.9 us (30%)
  Pallas kernels  10.6 us (23%)
  local copies, waits for them, and re-layouts  2.23 us (5%)
    ppermute x8, starting transfers between devices, shifted(): lax.ppermute(shard, axis, [(i, (i + by) % length) for i in range(length)])  19.8 us
    pallas_call x9, Pallas kernels, call(): pl.pallas_call(body, out_shape=tuple(shapes), in_specs=[pl.BlockSpec(memo...  10.6 us
    ppermute x8, waiting for transfers between devices, shifted(): lax.ppermute(shard, axis, [(i, (i + by) % length) for i in range(length)])  9.58 us
    ppermute x1, waiting for transfers between devices, diagonal(): return lax.ppermute(shard, ('gx', 'gy'), pairs)  4.27 us
    unnamed x4, local copies, waits for them, and re-layouts  2.23 us
  transfers between devices with their start and end apart: 9, of which 6 were waited for; matrix products, arithmetic and copies ran while one was open for 0% of the time, Pallas kernels for 15%

profile of v2, /device:TPU:0, one launch (start us, length us, event | category | flops | bytes accessed | tf_op | source)
XLA Modules:
  0.0 46.5 jit_solution(10279213251636026005)
XLA Ops:
  0.0 1.2 %copy-done = f32[4,3,3,2,2,2,6,128]{7,5,6,4,3,2,1,0:T(2,128)S(1)} copy-done((f32[4,3,3,2,2,2,6,128]{7,5,6,4,3,2,1,0:T(2,128)S(1)}, f32[4,3,3,2,2,2,6,128]{7,5,6,4,3,2,1,0:T(2,128)}, u32[]{:S(2)}) %copy-start) | copy-done | bytes 884760
  1.2 0.1 shard_map.28
  1.3 0.1 collective-permute-start.1
  1.4 4.0 %collective-permute-start = (f32[312,128]{1,0:T(8,128)S(1)}, f32[312,128]{1,0:T(8,128)S(1)}, u32[]{:S(2)}, u32[]{:S(2)}) collective-permute-start(f32[312,128]{1,0:T(8,128)S(1)} %get-tuple-element.65), channel_id=1, source_target_pairs={{0,15},{1,0},{2,1},{3,2},{4,3},{5,4},{6,5},{7,6},{8,7},{9,8},{10,9... | collective-permute-start | bytes 479240 | tf_op jit(solution)/shard_map/ppermute | solution.py:687
  5.3 6.0 %collective-permute-start.2 = (f32[312,128]{1,0:T(8,128)S(1)}, f32[312,128]{1,0:T(8,128)S(1)}, u32[]{:S(2)}, u32[]{:S(2)}) collective-permute-start(f32[312,128]{1,0:T(8,128)S(1)} %get-tuple-element.67), channel_id=1, source_target_pairs={{0,112},{16,0},{32,16},{48,32},{64,48},{80,64},{96,80},{112,96},{1... | collective-permute-start | bytes 479240 | tf_op jit(solution)/shard_map/ppermute | solution.py:687
  11.4 1.1 %copy-done.1 = f32[4,3,3,2,2,2,4,128]{7,6,5,4,3,2,1,0:T(4,128)S(1)} copy-done((f32[4,3,3,2,2,2,4,128]{7,6,5,4,3,2,1,0:T(4,128)S(1)}, f32[4,3,3,2,2,2,4,128]{7,6,5,4,3,2,1,0:T(4,128)}, u32[]{:S(2)}) %copy-start.1) | copy-done | bytes 589848
  12.4 1.2 %shard_map.29 = (f32[3456,128]{1,0:T(8,128)S(1)}, f32[3456,128]{1,0:T(8,128)S(1)}, f32[3456,128]{1,0:T(8,128)S(1)}, f32[3456,128]{1,0:T(8,128)S(1)}, f32[3456,12...) custom-call(f32[1728,128]{1,0:T(8,128)S(1)} %bitcast.6, ...), custom_call_target="tpu_custom_call" | custom-call | tf_op jit(solution)/shard_map/pallas_call | solution.py:674
  13.7 4.3 %collective-permute-done.3.corner.refs_3_ = f32[48,128]{1,0:T(8,128)S(1)} collective-permute-done((f32[48,128]{1,0:T(8,128)S(1)}, f32[48,128]{1,0:T(8,128)S(1)}, u32[]{:S(2)}, u32[]{:S(2)}) %collective-permute-start.3) | collective-permute-done | bytes 24608 | tf_op jit(solution)/shard_map/ppermute | solution.py:693
  17.9 0.0 collective-permute-done.ynext.refs_0_
  18.0 0.1 collective-permute-start.4
  18.1 2.4 %shard_map.31 = (f32[3456,128]{1,0:T(8,128)S(1)}, f32[3456,128]{1,0:T(8,128)S(1)}, f32[3456,128]{1,0:T(8,128)S(1)}, f32[3456,128]{1,0:T(8,128)S(1)}, f32[3456,12...) custom-call(f32[312,128]{1,0:T(8,128)S(1)} %collective-permute-done., ...), custom_call_target="tpu_custom_call", output_to_operand_aliasing={{0}: (5, {}), {1}: (6, {}), {2}: (7, {}), {3}: (8, {}), {4}... | custom-call | tf_op jit(solution)/shard_map/pallas_call | solution.py:674
  20.4 7.3 %collective-permute-done.4.refs_0_ = f32[456,128]{1,0:T(8,128)S(1)} collective-permute-done((f32[456,128]{1,0:T(8,128)S(1)}, f32[456,128]{1,0:T(8,128)S(1)}, u32[]{:S(2)}, u32[]{:S(2)}) %collective-permute-start.4) | collective-permute-done | bytes 233504 | tf_op jit(solution)/shard_map/ppermute | solution.py:687
  27.7 1.0 %shard_map.32 = (f32[3456,128]{1,0:T(8,128)S(1)}, f32[3456,128]{1,0:T(8,128)S(1)}, f32[3456,128]{1,0:T(8,128)S(1)}, f32[3456,128]{1,0:T(8,128)S(1)}, f32[3456,12...) custom-call(f32[456,128]{1,0:T(8,128)S(1)} %collective-permute-done., ...), custom_call_target="tpu_custom_call", output_to_operand_aliasing={{0}: (2, {}), {1}: (3, {}), {2}: (4, {}), {3}: (5, {}), {4}... | custom-call | tf_op jit(solution)/shard_map/pallas_call | solution.py:674
  28.8 0.1 collective-permute-start.6
  28.9 3.8 %collective-permute-start.5 = (f32[192,128]{1,0:T(8,128)S(1)}, f32[192,128]{1,0:T(8,128)S(1)}, u32[]{:S(2)}, u32[]{:S(2)}) collective-permute-start(f32[192,128]{1,0:T(8,128)S(1)} %get-tuple-element.101), channel_id=1, source_target_pairs={{0,15},{1,0},{2,1},{3,2},{4,3},{5,4},{6,5},{7,6},{8,7},{9,8},{10,9... | collective-permute-start | bytes 294920 | tf_op jit(solution)/shard_map/ppermute | solution.py:687
  32.7 1.7 %shard_map.33 = (f32[1152,128]{1,0:T(8,128)S(1)}, f32[1536,128]{1,0:T(8,128)S(1)}, f32[1536,128]{1,0:T(8,128)S(1)}, f32[1536,128]{1,0:T(8,128)S(1)}, f32[1536,12...) custom-call(f32[3456,128]{1,0:T(8,128)S(1)} %get-tuple-element.92.re, ...), custom_call_target="tpu_custom_call", output_to_operand_aliasing={{0}: (9, {})} | custom-call | tf_op jit(solution)/shard_map/pallas_call | solution.py:674
  34.4 0.5 %collective-permute-done.5.ynext.refs_8_ = f32[192,128]{1,0:T(8,128)S(1)} collective-permute-done((f32[192,128]{1,0:T(8,128)S(1)}, f32[192,128]{1,0:T(8,128)S(1)}, u32[]{:S(2)}, u32[]{:S(2)}) %collective-permute-start.5) | collective-permute-done | bytes 98336 | tf_op jit(solution)/shard_map/ppermute | solution.py:687
  34.9 0.5 %collective-permute-done.6.yprev.refs_9_ = f32[256,128]{1,0:T(8,128)S(1)} collective-permute-done((f32[256,128]{1,0:T(8,128)S(1)}, f32[256,128]{1,0:T(8,128)S(1)}, u32[]{:S(2)}, u32[]{:S(2)}) %collective-permute-start.6) | collective-permute-done | bytes 131104 | tf_op jit(solution)/shard_map/ppermute | solution.py:687
  35.5 0.1 collective-permute-start.8
  35.6 5.6 %collective-permute-start.7 = (f32[224,128]{1,0:T(8,128)S(1)}, f32[224,128]{1,0:T(8,128)S(1)}, u32[]{:S(2)}, u32[]{:S(2)}) collective-permute-start(f32[224,128]{1,0:T(8,128)S(1)} %get-tuple-element.105), channel_id=1, source_target_pairs={{0,112},{16,0},{32,16},{48,32},{64,48},{80,64},{96,80},{112,96},{1... | collective-permute-start | bytes 344072 | tf_op jit(solution)/shard_map/ppermute | solution.py:687
  41.2 1.9 %shard_map.35 = (f32[1152,128]{1,0:T(8,128)S(1)}, f32[1536,128]{1,0:T(8,128)S(1)}, f32[1536,128]{1,0:T(8,128)S(1)}, f32[1536,128]{1,0:T(8,128)S(1)}, f32[1536,12...) custom-call(f32[3456,128]{1,0:T(8,128)S(1)} %get-tuple-element.92.re, ...), custom_call_target="tpu_custom_call", output_to_operand_aliasing={{0}: (10, {}), {1}: (11, {}), {2}: (12, {}), {3}: (13, {}),... | custom-call | tf_op jit(solution)/shard_map/pallas_call | solution.py:674
  43.1 0.5 %collective-permute-done.7.refs_8_ = f32[224,128]{1,0:T(8,128)S(1)} collective-permute-done((f32[224,128]{1,0:T(8,128)S(1)}, f32[224,128]{1,0:T(8,128)S(1)}, u32[]{:S(2)}, u32[]{:S(2)}) %collective-permute-start.7) | collective-permute-done | bytes 114720 | tf_op jit(solution)/shard_map/ppermute | solution.py:687
  43.6 0.7 %collective-permute-done.8.refs_9_ = f32[288,128]{1,0:T(8,128)S(1)} collective-permute-done((f32[288,128]{1,0:T(8,128)S(1)}, f32[288,128]{1,0:T(8,128)S(1)}, u32[]{:S(2)}, u32[]{:S(2)}) %collective-permute-start.8) | collective-permute-done | bytes 147488 | tf_op jit(solution)/shard_map/ppermute | solution.py:687
  44.3 2.2 %shard_map.36 = (f32[1152,128]{1,0:T(8,128)}, f32[1152,128]{1,0:T(8,128)S(1)}, f32[1536,128]{1,0:T(8,128)S(1)}, f32[1536,128]{1,0:T(8,128)S(1)}, f32[1536,128]{1...) custom-call(f32[3456,128]{1,0:T(8,128)S(1)} %get-tuple-element.92.re, ...), custom_call_target="tpu_custom_call", output_to_operand_aliasing={{1}: (10, {}), {2}: (11, {}), {3}: (12, {}), {4}: (13, {}),... | custom-call | tf_op jit(solution)/shard_map/pallas_call | solution.py:674
  (7 shorter events, 0.1 us)
Async XLA Ops:
  0.0 1.2 %copy-start = (f32[4,3,3,2,2,2,6,128]{7,5,6,4,3,2,1,0:T(2,128)S(1)}, f32[4,3,3,2,2,2,6,128]{7,5,6,4,3,2,1,0:T(2,128)}, u32[]{:S(2)}) copy-start(f32[4,3,3,2,2,2,6,128]{7,5,6,4,3,2,1,0:T(2,128)} %param.2) | copy-start | bytes 2654212
  1.3 16.7 %collective-permute-start.1 = (f32[408,128]{1,0:T(8,128)S(1)}, f32[408,128]{1,0:T(8,128)S(1)}, u32[]{:S(2)}, u32[]{:S(2)}) collective-permute-start(f32[408,128]{1,0:T(8,128)S(1)} %get-tuple-element.66), channel_id=1, source_target_pairs={{0,1},{1,2},{2,3},{3,4},{4,5},{5,6},{6,7},{7,8},{8,9},{9,10},{10,1... | collective-permute-start | bytes 626696 | tf_op jit(solution)/shard_map/ppermute | solution.py:687
  1.4 16.6 %collective-permute-start = (f32[312,128]{1,0:T(8,128)S(1)}, f32[312,128]{1,0:T(8,128)S(1)}, u32[]{:S(2)}, u32[]{:S(2)}) collective-permute-start(f32[312,128]{1,0:T(8,128)S(1)} %get-tuple-element.65), channel_id=1, source_target_pairs={{0,15},{1,0},{2,1},{3,2},{4,3},{5,4},{6,5},{7,6},{8,7},{9,8},{10,9... | collective-permute-start | bytes 479240 | tf_op jit(solution)/shard_map/ppermute | solution.py:687
  5.3 12.6 %collective-permute-start.2 = (f32[312,128]{1,0:T(8,128)S(1)}, f32[312,128]{1,0:T(8,128)S(1)}, u32[]{:S(2)}, u32[]{:S(2)}) collective-permute-start(f32[312,128]{1,0:T(8,128)S(1)} %get-tuple-element.67), channel_id=1, source_target_pairs={{0,112},{16,0},{32,16},{48,32},{64,48},{80,64},{96,80},{112,96},{1... | collective-permute-start | bytes 479240 | tf_op jit(solution)/shard_map/ppermute | solution.py:687
  11.4 6.6 %collective-permute-start.3 = (f32[48,128]{1,0:T(8,128)S(1)}, f32[48,128]{1,0:T(8,128)S(1)}, u32[]{:S(2)}, u32[]{:S(2)}) collective-permute-start(f32[48,128]{1,0:T(8,128)S(1)} %get-tuple-element.68), channel_id=1, source_target_pairs={{0,113},{1,114},{2,115},{3,116},{4,117},{5,118},{6,119},{7,120},{8... | collective-permute-start | bytes 73736 | tf_op jit(solution)/shard_map/ppermute | solution.py:693
  11.4 1.1 %copy-start.1 = (f32[4,3,3,2,2,2,4,128]{7,6,5,4,3,2,1,0:T(4,128)S(1)}, f32[4,3,3,2,2,2,4,128]{7,6,5,4,3,2,1,0:T(4,128)}, u32[]{:S(2)}) copy-start(f32[4,3,3,2,2,2,4,128]{7,6,5,4,3,2,1,0:T(4,128)} %param.3) | copy-start | bytes 1769476
  18.0 9.7 %collective-permute-start.4 = (f32[456,128]{1,0:T(8,128)S(1)}, f32[456,128]{1,0:T(8,128)S(1)}, u32[]{:S(2)}, u32[]{:S(2)}) collective-permute-start(f32[456,128]{1,0:T(8,128)S(1)} %shard_map.30), channel_id=1, source_target_pairs={{0,16},{16,32},{32,48},{48,64},{64,80},{80,96},{96,112},{112,0},{1... | collective-permute-start | bytes 700424 | tf_op jit(solution)/shard_map/ppermute | solution.py:687
  28.8 6.7 %collective-permute-start.6 = (f32[256,128]{1,0:T(8,128)S(1)}, f32[256,128]{1,0:T(8,128)S(1)}, u32[]{:S(2)}, u32[]{:S(2)}) collective-permute-start(f32[256,128]{1,0:T(8,128)S(1)} %get-tuple-element.102), channel_id=1, source_target_pairs={{0,1},{1,2},{2,3},{3,4},{4,5},{5,6},{6,7},{7,8},{8,9},{9,10},{10,1... | collective-permute-start | bytes 393224 | tf_op jit(solution)/shard_map/ppermute | solution.py:687
  28.9 6.1 %collective-permute-start.5 = (f32[192,128]{1,0:T(8,128)S(1)}, f32[192,128]{1,0:T(8,128)S(1)}, u32[]{:S(2)}, u32[]{:S(2)}) collective-permute-start(f32[192,128]{1,0:T(8,128)S(1)} %get-tuple-element.101), channel_id=1, source_target_pairs={{0,15},{1,0},{2,1},{3,2},{4,3},{5,4},{6,5},{7,6},{8,7},{9,8},{10,9... | collective-permute-start | bytes 294920 | tf_op jit(solution)/shard_map/ppermute | solution.py:687
  35.5 8.8 %collective-permute-start.8 = (f32[288,128]{1,0:T(8,128)S(1)}, f32[288,128]{1,0:T(8,128)S(1)}, u32[]{:S(2)}, u32[]{:S(2)}) collective-permute-start(f32[288,128]{1,0:T(8,128)S(1)} %get-tuple-element.106), channel_id=1, source_target_pairs={{0,16},{16,32},{32,48},{48,64},{64,80},{80,96},{96,112},{112,0},{1... | collective-permute-start | bytes 442376 | tf_op jit(solution)/shard_map/ppermute | solution.py:687
  35.6 8.0 %collective-permute-start.7 = (f32[224,128]{1,0:T(8,128)S(1)}, f32[224,128]{1,0:T(8,128)S(1)}, u32[]{:S(2)}, u32[]{:S(2)}) collective-permute-start(f32[224,128]{1,0:T(8,128)S(1)} %get-tuple-element.105), channel_id=1, source_target_pairs={{0,112},{16,0},{32,16},{48,32},{64,48},{80,64},{96,80},{112,96},{1... | collective-permute-start | bytes 344072 | tf_op jit(solution)/shard_map/ppermute | solution.py:687

commit v3 on v2

--- a/solution.py
+++ b/solution.py
@@ -132,7 +132,7 @@
                     down[pl.ds(((DOWN_Y.index(d) * n + q) * 2 + x) * 4, 4), :] = read_down(d, q, x)
 
 
-def pack_first_body(links, yup, ydown, xdown, corner):
+def pack_first_body(links, xdown, xup, yup, ydown, cdown, cup):
     def reader(row):
         return lambda d, q, x: links[pl.ds(((d * 18 + q) * 2 + x) * ROWS + row, 4, stride=2), :]
 
@@ -144,25 +144,25 @@
         for d in range(1, 4):
             xdown[pl.ds(((d - 1) * 12 + q) * 8, 8), :] = links[pl.ds((d * 18 + q) * 2 * ROWS + 2, 8), :]
         xdown[pl.ds(288 + q * 2, 2), :] = links[pl.ds((54 + q) * 2 * ROWS, 2), :]
-        corner[pl.ds(q * 4, 4), :] = links[pl.ds((18 + q) * 2 * ROWS + 3, 4, stride=2), :]
-
-
-def pack_x_body(links, ynext, yprev, xnext, corner, after, up):
-    for q in range(12):
         for d in range(4):
-            up[pl.ds((d * 12 + q) * 8, 8), :] = links[pl.ds(((d * 18 + q) * 2 + 1) * ROWS + 2, 8), :]
-        up[pl.ds(384 + q * 2, 2), :] = links[pl.ds((q * 2 + 1) * ROWS + 10, 2), :]
-        up[pl.ds(408 + q * 4, 4), :] = ynext[pl.ds(q * 8 + 4, 4), :]
-
-
-def pack_lambda_x_body(lam, ynext, yprev, after, up, down):
+            xup[pl.ds((d * 12 + q) * 8, 8), :] = links[pl.ds(((d * 18 + q) * 2 + 1) * ROWS + 2, 8), :]
+        xup[pl.ds(384 + q * 2, 2), :] = links[pl.ds((q * 2 + 1) * ROWS + 10, 2), :]
+        cdown[pl.ds(q * 4, 4), :] = links[pl.ds((18 + q) * 2 * ROWS + 3, 4, stride=2), :]
+        cup[pl.ds(q * 4, 4), :] = links[pl.ds((q * 2 + 1) * ROWS + 2, 4, stride=2), :]
+
+
+def pack_lambda(lam, xdown, xup, yup, ydown, cdown, cup):
+    def reader(row):
+        return lambda d, q, x: lam[pl.ds(((d * NA + q) * 2 + x) * 8 + row, 4, stride=2), :]
+
+    pack_y(yup, ydown, NA, reader(1), reader(0))
     for c in range(32):
-        up[pl.ds(c * 8, 8), :] = lam[pl.ds((c * 2 + 1) * 8, 8), :]
+        xup[pl.ds(c * 8, 8), :] = lam[pl.ds((c * 2 + 1) * 8, 8), :]
         if c >= NA:
-            down[pl.ds((c - NA) * 8, 8), :] = lam[pl.ds(c * 16, 8), :]
+            xdown[pl.ds((c - NA) * 8, 8), :] = lam[pl.ds(c * 16, 8), :]
     for k in range(NA):
-        up[pl.ds(256 + k * 4, 4), :] = ynext[pl.ds(k * 8 + 4, 4), :]
-        down[pl.ds(192 + k * 4, 4), :] = yprev[pl.ds((NA + k) * 8, 4), :]
+        cdown[pl.ds(k * 4, 4), :] = lam[pl.ds((NA + k) * 16 + 1, 4, stride=2), :]
+        cup[pl.ds(k * 4, 4), :] = lam[pl.ds((k * 2 + 1) * 8, 4, stride=2), :]
 
 
 def two_rows(read):
@@ -263,7 +263,7 @@
     fill_mixed(bufs, NC)
 
 
-def fill_column(source, slots, corner, at, bufs, xe, edge, corner_to):
+def fill_column(source, slots, corner, bufs, xe, edge, corner_to):
     for slot, d in enumerate(slots):
         m = two_rows(lambda q: source[pl.ds((slot * 12 + q) * 8, 8), :])
 
@@ -279,7 +279,7 @@
 
     put(write_edge, m)
     buf, corner_dir, off = corner_to
-    m = two_rows(lambda q: corner[pl.ds(at + q * 4, 4), :])
+    m = two_rows(lambda q: corner[pl.ds(q * 4, 4), :])
 
     def write_corner(q, v):
         bufs[buf][pl.ds(place(corner_dir * NC + q, xe) + off, 4, stride=2), :] = v
@@ -288,12 +288,12 @@
 
 
 def fill_links_next(xnext, corner, bufs):
-    fill_column(xnext, (1, 2, 3), corner, 0, bufs, 3, (3, 0), (YM, 1, 2))
+    fill_column(xnext, (1, 2, 3), corner, bufs, 3, (3, 0), (YM, 1, 2))
     fill_high(bufs, NC)
 
 
-def fill_links_prev(xprev, bufs):
-    fill_column(xprev, (0, 1, 2, 3), xprev, 408, bufs, 0, (0, 10), (YP, 0, 3))
+def fill_links_prev(xprev, corner, bufs):
+    fill_column(xprev, (0, 1, 2, 3), corner, bufs, 0, (0, 10), (YP, 0, 3))
     fill_low(bufs, NC)
 
 
@@ -326,7 +326,7 @@
     fill_mixed(bufs, NA)
 
 
-def fill_lambda_x(xnext, xprev, bufs):
+def fill_lambda_x(xnext, cnext, xprev, cprev, bufs):
     zero = jnp.zeros((2, 128), jnp.float32)
     for d in range(4):
         for k in range(NA):
@@ -339,8 +339,8 @@
             if d == 0:
                 bufs[O][pl.ds(low + 10, 2), :] = zero
     for k in range(NA):
-        bufs[YM][pl.ds(place(NA + k, 3) + 2, 4, stride=2), :] = xnext[pl.ds(192 + k * 4, 4), :]
-        bufs[YP][pl.ds(place(k, 0) + 3, 4, stride=2), :] = xprev[pl.ds(256 + k * 4, 4), :]
+        bufs[YM][pl.ds(place(NA + k, 3) + 2, 4, stride=2), :] = cnext[pl.ds(k * 4, 4), :]
+        bufs[YP][pl.ds(place(k, 0) + 3, 4, stride=2), :] = cprev[pl.ds(k * 4, 4), :]
     fill_high(bufs, NA)
     fill_low(bufs, NA)
 
@@ -607,34 +607,30 @@
 
 
 def links_local_body(*refs):
-    links, incoming = refs[:2]
-    bufs, (inner, omega, loops, low) = refs[2:9], refs[9:]
+    links = refs[0]
+    bufs, (omega, loops, low) = refs[1:8], refs[8:]
     fill_links_local(links, bufs)
+    forward_items(0, bufs, omega, loops, low)
+
+
+def links_y_body(*refs):
+    ynext, yprev, incoming = refs[:3]
+    bufs, (omega, loops, low, inner) = refs[13:20], refs[20:]
+    fill_links_y(ynext, yprev, bufs)
     take_incoming(incoming, inner)
-    forward_items(0, bufs, omega, loops, low)
-
-
-def links_y_body(*refs):
-    ynext, yprev, xnext, corner, inner = refs[:5]
-    bufs, (omega, loops, low, lam, direct) = refs[15:22], refs[22:]
-    fill_links_y(ynext, yprev, bufs)
     forward_items(1, bufs, omega, loops, low)
-    fill_links_next(xnext, corner, bufs)
+
+
+def links_x_body(*refs):
+    xnext, cnext, xprev, cprev, inner = refs[:5]
+    bufs, (omega, loops, low, lam, direct), messages = refs[15:22], refs[22:27], refs[27:]
+    fill_links_next(xnext, cnext, bufs)
     forward_items(2, bufs, omega, loops, low)
     finish_forward((1,), bufs, inner, loops, low, lam, direct)
-
-
-def links_x_body(*refs):
-    xprev, inner = refs[:2]
-    bufs, (omega, loops, low, lam, direct, up, down) = refs[14:21], refs[21:]
-    fill_links_prev(xprev, bufs)
+    fill_links_prev(xprev, cprev, bufs)
     forward_items(3, bufs, omega, loops, low)
     finish_forward((0,), bufs, inner, loops, low, lam, direct)
-
-    def reader(row):
-        return lambda d, q, x: lam[pl.ds(((d * NA + q) * 2 + x) * 8 + row, 4, stride=2), :]
-
-    pack_y(up, down, NA, reader(1), reader(0))
+    pack_lambda(lam, *messages)
 
 
 def lambda_local_body(*refs):
@@ -652,9 +648,9 @@
 
 
 def lambda_x_body(*refs):
-    bufs, (omega, xnext, xprev) = refs[:7], refs[7:10]
-    out, acc, lams, sums = refs[19], refs[20], refs[21:28], refs[28]
-    fill_lambda_x(xnext, xprev, lams)
+    bufs, (omega, xnext, cnext, xprev, cprev) = refs[:7], refs[7:12]
+    out, acc, lams, sums = refs[21], refs[22], refs[23:30], refs[30]
+    fill_lambda_x(xnext, cnext, xprev, cprev, lams)
     backward_items(2, bufs, lams, omega, sums, acc)
     backward_items(3, bufs, lams, omega, sums, acc)
     finish_backward(bufs, sums, acc, out)
@@ -693,27 +689,31 @@
     return lax.ppermute(shard, ("gx", "gy"), pairs)
 
 
+def exchanged(messages):
+    xdown, xup, yup, ydown, cdown, cup = messages
+    return (
+        shifted(xdown, "gx", -1),
+        shifted(xup, "gx", 1),
+        shifted(yup, "gy", 1),
+        shifted(ydown, "gy", -1),
+        diagonal(cdown, -1, 1),
+        diagonal(cup, 1, -1),
+    )
+
+
 def body(links, incoming):
     links = jnp.transpose(links, (0, 1, 2, 3, 4, 6, 5, 7)).reshape(144 * ROWS, 128)
     shape = incoming.shape
     incoming = incoming.reshape(1152, 128)
-    yup, ydown, xdown, corner = call(pack_first_body, (links,), (408, 312, 312, 48))
-    yprev, ynext = shifted(yup, "gy", 1), shifted(ydown, "gy", -1)
-    xnext, corner = shifted(xdown, "gx", -1), diagonal(corner, -1, 1)
-    inner, *kept = (lambda r: (r[7], *r[:7], *r[8:]))(
-        call(links_local_body, (links, incoming), buffer_rows(NC) + [1152, 1728, 864, 1152])
-    )
-    (xup,) = call(pack_x_body, (links, ynext, yprev, xnext, corner, kept[-1]), (456,))
-    xprev = shifted(xup, "gx", 1)
-    kept = call(links_y_body, (ynext, yprev, xnext, corner, inner), (512, 1152), kept)
-    r = call(links_x_body, (xprev, inner), (256, 192), kept)
-    bufs, omega, (lam, acc, yup, ydown) = r[:7], r[7], r[10:]
-    yprev, ynext = shifted(yup, "gy", 1), shifted(ydown, "gy", -1)
+    xnext, xprev, yprev, ynext, cnext, cprev = exchanged(call(pack_first_body, (links,), (312, 408, 408, 312, 48, 48)))
+    kept = call(links_local_body, (links,), buffer_rows(NC) + [1728, 864, 1152])
+    *kept, inner = call(links_y_body, (ynext, yprev, incoming), (1152,), kept)
+    r = call(links_x_body, (xnext, cnext, xprev, cprev, inner), (512, 1152, 192, 256, 256, 192, 32, 32), kept)
+    bufs, omega, (lam, acc) = r[:7], r[7], r[10:12]
+    xnext, xprev, yprev, ynext, cnext, cprev = exchanged(r[12:])
     kept = call(lambda_local_body, (*bufs, omega, lam), buffer_rows(NA) + [1152], (acc,))
-    xup, xdown = call(pack_lambda_x_body, (lam, ynext, yprev, kept[-1]), (288, 224))
-    xprev, xnext = shifted(xup, "gx", 1), shifted(xdown, "gx", -1)
     kept = call(lambda_y_body, (*bufs, omega, ynext, yprev), (), kept)
-    out = call(lambda_x_body, (*bufs, omega, xnext, xprev), (1152,), kept, first=1)[0]
+    out = call(lambda_x_body, (*bufs, omega, xnext, cnext, xprev, cprev), (1152,), kept, first=1)[0]
     return out.reshape(shape)
 
 

time: 46.7 us -> 46 us (0.985)
  the two profiles are of different devices: /device:TPU:0 before, /device:TPU:25 now
where the time goes in v3:
time: 46 us; the launch traced here: 45.9 us
  starting transfers between devices  23.1 us (50%)
  waiting for transfers between devices  10.8 us (23%)
  Pallas kernels  10.7 us (23%)
  local copies, waits for them, and re-layouts  1.17 us (3%)
    ppermute x8, starting transfers between devices, shifted(): lax.ppermute(shard, axis, [(i, (i + by) % length) for i in range(length)])  13.4 us
    ppermute x4, waiting for transfers between devices, diagonal(): return lax.ppermute(shard, ('gx', 'gy'), pairs)  10.8 us
    pallas_call x7, Pallas kernels, call(): pl.pallas_call(body, out_shape=tuple(shapes), in_specs=[pl.BlockSpec(memo...  10.7 us
    ppermute x4, starting transfers between devices, diagonal(): return lax.ppermute(shard, ('gx', 'gy'), pairs)  9.78 us
    unnamed x4, local copies, waits for them, and re-layouts  1.17 us
  transfers between devices with their start and end apart: 12, of which 3 were waited for; matrix products, arithmetic and copies ran while one was open for 0% of the time, Pallas kernels for 13%

profile of v3, /device:TPU:25, one launch (start us, length us, event | category | flops | bytes accessed | tf_op | source)
XLA Modules:
  0.0 45.9 jit_solution(2161949258167488285)
XLA Ops:
  0.0 1.2 %copy-done = f32[4,3,3,2,2,2,6,128]{7,5,6,4,3,2,1,0:T(2,128)S(1)} copy-done((f32[4,3,3,2,2,2,6,128]{7,5,6,4,3,2,1,0:T(2,128)S(1)}, f32[4,3,3,2,2,2,6,128]{7,5,6,4,3,2,1,0:T(2,128)}, u32[]{:S(2)}) %copy-start) | copy-done | bytes 884760
  1.2 0.1 shard_map.28
  1.3 1.9 %collective-permute-start.5 = (f32[408,128]{1,0:T(8,128)S(1)}, f32[408,128]{1,0:T(8,128)S(1)}, u32[]{:S(2)}, u32[]{:S(2)}) collective-permute-start(f32[408,128]{1,0:T(8,128)S(1)} %get-tuple-element.72), channel_id=1, source_target_pairs={{0,1},{1,2},{2,3},{3,4},{4,5},{5,6},{6,7},{7,8},{8,9},{9,10},{10,1... | collective-permute-start | bytes 626696 | tf_op jit(solution)/shard_map/ppermute | solution.py:683
  3.2 3.3 %collective-permute-start.2 = (f32[408,128]{1,0:T(8,128)S(1)}, f32[408,128]{1,0:T(8,128)S(1)}, u32[]{:S(2)}, u32[]{:S(2)}) collective-permute-start(f32[408,128]{1,0:T(8,128)S(1)} %get-tuple-element.69), channel_id=1, source_target_pairs={{0,16},{16,32},{32,48},{48,64},{64,80},{80,96},{96,112},{112,0},{1... | collective-permute-start | bytes 626696 | tf_op jit(solution)/shard_map/ppermute | solution.py:683
  6.5 2.2 %collective-permute-start = (f32[312,128]{1,0:T(8,128)S(1)}, f32[312,128]{1,0:T(8,128)S(1)}, u32[]{:S(2)}, u32[]{:S(2)}) collective-permute-start(f32[312,128]{1,0:T(8,128)S(1)} %get-tuple-element.67), channel_id=1, source_target_pairs={{0,112},{16,0},{32,16},{48,32},{64,48},{80,64},{96,80},{112,96},{1... | collective-permute-start | bytes 479240 | tf_op jit(solution)/shard_map/ppermute | solution.py:683
  8.7 6.5 %collective-permute-start.1 = (f32[48,128]{1,0:T(8,128)S(1)}, f32[48,128]{1,0:T(8,128)S(1)}, u32[]{:S(2)}, u32[]{:S(2)}) collective-permute-start(f32[48,128]{1,0:T(8,128)S(1)} %get-tuple-element.68), channel_id=1, source_target_pairs={{0,113},{1,114},{2,115},{3,116},{4,117},{5,118},{6,119},{7,120},{8... | collective-permute-start | bytes 73736 | tf_op jit(solution)/shard_map/ppermute | solution.py:689
  15.3 0.0 collective-permute-done.4.refs_0_
  15.3 0.0 collective-permute-start.3
  15.3 1.1 %shard_map.29 = (f32[3456,128]{1,0:T(8,128)S(1)}, f32[3456,128]{1,0:T(8,128)S(1)}, f32[3456,128]{1,0:T(8,128)S(1)}, f32[3456,128]{1,0:T(8,128)S(1)}, f32[3456,12...) custom-call(f32[1728,128]{1,0:T(8,128)S(1)} %bitcast.6), custom_call_target="tpu_custom_call" | custom-call | tf_op jit(solution)/shard_map/pallas_call | solution.py:670
  16.4 0.0 collective-permute-done.5.refs_1_
  16.4 1.2 %shard_map.30 = (f32[3456,128]{1,0:T(8,128)S(1)}, f32[3456,128]{1,0:T(8,128)S(1)}, f32[3456,128]{1,0:T(8,128)S(1)}, f32[3456,128]{1,0:T(8,128)S(1)}, f32[3456,12...) custom-call(f32[312,128]{1,0:T(8,128)S(1)} %collective-permute-done., ...), custom_call_target="tpu_custom_call", output_to_operand_aliasing={{0}: (3, {}), {1}: (4, {}), {2}: (5, {}), {3}: (6, {}), {4}... | custom-call | tf_op jit(solution)/shard_map/pallas_call | solution.py:670
  17.7 1.8 %collective-permute-done.1.refs_1_ = f32[48,128]{1,0:T(8,128)S(1)} collective-permute-done((f32[48,128]{1,0:T(8,128)S(1)}, f32[48,128]{1,0:T(8,128)S(1)}, u32[]{:S(2)}, u32[]{:S(2)}) %collective-permute-start.1) | collective-permute-done | bytes 24608 | tf_op jit(solution)/shard_map/ppermute | solution.py:689
  19.5 4.5 %collective-permute-done.3.refs_3_ = f32[48,128]{1,0:T(8,128)S(1)} collective-permute-done((f32[48,128]{1,0:T(8,128)S(1)}, f32[48,128]{1,0:T(8,128)S(1)}, u32[]{:S(2)}, u32[]{:S(2)}) %collective-permute-start.3) | collective-permute-done | bytes 24608 | tf_op jit(solution)/shard_map/ppermute | solution.py:689
  24.0 2.3 %shard_map.31 = (f32[3456,128]{1,0:T(8,128)S(1)}, f32[3456,128]{1,0:T(8,128)S(1)}, f32[3456,128]{1,0:T(8,128)S(1)}, f32[3456,128]{1,0:T(8,128)S(1)}, f32[3456,12...) custom-call(f32[312,128]{1,0:T(8,128)S(1)} %collective-permute-done., ...), custom_call_target="tpu_custom_call", output_to_operand_aliasing={{0}: (5, {}), {1}: (6, {}), {2}: (7, {}), {3}: (8, {}), {4}... | custom-call | tf_op jit(solution)/shard_map/pallas_call | solution.py:670
  26.3 0.1 collective-permute-start.11
  26.4 0.4 collective-permute-start.8
  26.8 0.1 collective-permute-start.10
  26.9 5.4 %collective-permute-start.6 = (f32[192,128]{1,0:T(8,128)S(1)}, f32[192,128]{1,0:T(8,128)S(1)}, u32[]{:S(2)}, u32[]{:S(2)}) collective-permute-start(f32[192,128]{1,0:T(8,128)S(1)} %get-tuple-element.102), channel_id=1, source_target_pairs={{0,112},{16,0},{32,16},{48,32},{64,48},{80,64},{96,80},{112,96},{1... | collective-permute-start | bytes 294920 | tf_op jit(solution)/shard_map/ppermute | solution.py:683
  32.2 2.8 %collective-permute-start.7 = (f32[32,128]{1,0:T(8,128)S(1)}, f32[32,128]{1,0:T(8,128)S(1)}, u32[]{:S(2)}, u32[]{:S(2)}) collective-permute-start(f32[32,128]{1,0:T(8,128)S(1)} %get-tuple-element.103), channel_id=1, source_target_pairs={{0,113},{1,114},{2,115},{3,116},{4,117},{5,118},{6,119},{7,120},{8... | collective-permute-start | bytes 49160 | tf_op jit(solution)/shard_map/ppermute | solution.py:689
  35.0 0.5 collective-permute-start.9
  35.5 1.7 %shard_map.32 = (f32[1152,128]{1,0:T(8,128)S(1)}, f32[1536,128]{1,0:T(8,128)S(1)}, f32[1536,128]{1,0:T(8,128)S(1)}, f32[1536,128]{1,0:T(8,128)S(1)}, f32[1536,12...) custom-call(f32[3456,128]{1,0:T(8,128)S(1)} %get-tuple-element.94.re, ...), custom_call_target="tpu_custom_call", output_to_operand_aliasing={{0}: (9, {})} | custom-call | tf_op jit(solution)/shard_map/pallas_call | solution.py:670
  37.2 1.9 %shard_map.33 = (f32[1152,128]{1,0:T(8,128)S(1)}, f32[1536,128]{1,0:T(8,128)S(1)}, f32[1536,128]{1,0:T(8,128)S(1)}, f32[1536,128]{1,0:T(8,128)S(1)}, f32[1536,12...) custom-call(f32[3456,128]{1,0:T(8,128)S(1)} %get-tuple-element.94.re, ...), custom_call_target="tpu_custom_call", output_to_operand_aliasing={{0}: (10, {}), {1}: (11, {}), {2}: (12, {}), {3}: (13, {}),... | custom-call | tf_op jit(solution)/shard_map/pallas_call | solution.py:670
  39.1 4.5 %collective-permute-done.9.refs_11_ = f32[32,128]{1,0:T(8,128)S(1)} collective-permute-done((f32[32,128]{1,0:T(8,128)S(1)}, f32[32,128]{1,0:T(8,128)S(1)}, u32[]{:S(2)}, u32[]{:S(2)}) %collective-permute-start.9) | collective-permute-done | bytes 16416 | tf_op jit(solution)/shard_map/ppermute | solution.py:689
  43.6 2.2 %shard_map.34 = (f32[1152,128]{1,0:T(8,128)}, f32[1152,128]{1,0:T(8,128)S(1)}, f32[1536,128]{1,0:T(8,128)S(1)}, f32[1536,128]{1,0:T(8,128)S(1)}, f32[1536,128]{1...) custom-call(f32[3456,128]{1,0:T(8,128)S(1)} %get-tuple-element.94.re, ...), custom_call_target="tpu_custom_call", output_to_operand_aliasing={{1}: (12, {}), {2}: (13, {}), {3}: (14, {}), {4}: (15, {}),... | custom-call | tf_op jit(solution)/shard_map/pallas_call | solution.py:670
  (11 shorter events, 0.0 us)
Async XLA Ops:
  0.0 1.2 %copy-start = (f32[4,3,3,2,2,2,6,128]{7,5,6,4,3,2,1,0:T(2,128)S(1)}, f32[4,3,3,2,2,2,6,128]{7,5,6,4,3,2,1,0:T(2,128)}, u32[]{:S(2)}) copy-start(f32[4,3,3,2,2,2,6,128]{7,5,6,4,3,2,1,0:T(2,128)} %param.2) | copy-start | bytes 2654212
  1.2 15.3 %copy-start.1 = (f32[4,3,3,2,2,2,4,128]{7,6,5,4,3,2,1,0:T(4,128)S(1)}, f32[4,3,3,2,2,2,4,128]{7,6,5,4,3,2,1,0:T(4,128)}, u32[]{:S(2)}) copy-start(f32[4,3,3,2,2,2,4,128]{7,6,5,4,3,2,1,0:T(4,128)} %param.3) | copy-start | bytes 1769476
  1.3 15.1 %collective-permute-start.5 = (f32[408,128]{1,0:T(8,128)S(1)}, f32[408,128]{1,0:T(8,128)S(1)}, u32[]{:S(2)}, u32[]{:S(2)}) collective-permute-start(f32[408,128]{1,0:T(8,128)S(1)} %get-tuple-element.72), channel_id=1, source_target_pairs={{0,1},{1,2},{2,3},{3,4},{4,5},{5,6},{6,7},{7,8},{8,9},{9,10},{10,1... | collective-permute-start | bytes 626696 | tf_op jit(solution)/shard_map/ppermute | solution.py:683
  3.2 20.7 %collective-permute-start.2 = (f32[408,128]{1,0:T(8,128)S(1)}, f32[408,128]{1,0:T(8,128)S(1)}, u32[]{:S(2)}, u32[]{:S(2)}) collective-permute-start(f32[408,128]{1,0:T(8,128)S(1)} %get-tuple-element.69), channel_id=1, source_target_pairs={{0,16},{16,32},{32,48},{48,64},{64,80},{80,96},{96,112},{112,0},{1... | collective-permute-start | bytes 626696 | tf_op jit(solution)/shard_map/ppermute | solution.py:683
  6.5 8.7 %collective-permute-start.4 = (f32[312,128]{1,0:T(8,128)S(1)}, f32[312,128]{1,0:T(8,128)S(1)}, u32[]{:S(2)}, u32[]{:S(2)}) collective-permute-start(f32[312,128]{1,0:T(8,128)S(1)} %get-tuple-element.71), channel_id=1, source_target_pairs={{0,15},{1,0},{2,1},{3,2},{4,3},{5,4},{6,5},{7,6},{8,7},{9,8},{10,9... | collective-permute-start | bytes 479240 | tf_op jit(solution)/shard_map/ppermute | solution.py:683
  6.5 17.4 %collective-permute-start = (f32[312,128]{1,0:T(8,128)S(1)}, f32[312,128]{1,0:T(8,128)S(1)}, u32[]{:S(2)}, u32[]{:S(2)}) collective-permute-start(f32[312,128]{1,0:T(8,128)S(1)} %get-tuple-element.67), channel_id=1, source_target_pairs={{0,112},{16,0},{32,16},{48,32},{64,48},{80,64},{96,80},{112,96},{1... | collective-permute-start | bytes 479240 | tf_op jit(solution)/shard_map/ppermute | solution.py:683
  8.7 10.8 %collective-permute-start.1 = (f32[48,128]{1,0:T(8,128)S(1)}, f32[48,128]{1,0:T(8,128)S(1)}, u32[]{:S(2)}, u32[]{:S(2)}) collective-permute-start(f32[48,128]{1,0:T(8,128)S(1)} %get-tuple-element.68), channel_id=1, source_target_pairs={{0,113},{1,114},{2,115},{3,116},{4,117},{5,118},{6,119},{7,120},{8... | collective-permute-start | bytes 73736 | tf_op jit(solution)/shard_map/ppermute | solution.py:689
  15.3 8.7 %collective-permute-start.3 = (f32[48,128]{1,0:T(8,128)S(1)}, f32[48,128]{1,0:T(8,128)S(1)}, u32[]{:S(2)}, u32[]{:S(2)}) collective-permute-start(f32[48,128]{1,0:T(8,128)S(1)} %get-tuple-element.70), channel_id=1, source_target_pairs={{0,31},{1,16},{2,17},{3,18},{4,19},{5,20},{6,21},{7,22},{8,23},{9,... | collective-permute-start | bytes 73736 | tf_op jit(solution)/shard_map/ppermute | solution.py:689
  26.3 10.9 %collective-permute-start.11 = (f32[256,128]{1,0:T(8,128)S(1)}, f32[256,128]{1,0:T(8,128)S(1)}, u32[]{:S(2)}, u32[]{:S(2)}) collective-permute-start(f32[256,128]{1,0:T(8,128)S(1)} %get-tuple-element.107), channel_id=1, source_target_pairs={{0,1},{1,2},{2,3},{3,4},{4,5},{5,6},{6,7},{7,8},{8,9},{9,10},{10,1... | collective-permute-start | bytes 393224 | tf_op jit(solution)/shard_map/ppermute | solution.py:683
  26.4 17.3 %collective-permute-start.8 = (f32[256,128]{1,0:T(8,128)S(1)}, f32[256,128]{1,0:T(8,128)S(1)}, u32[]{:S(2)}, u32[]{:S(2)}) collective-permute-start(f32[256,128]{1,0:T(8,128)S(1)} %get-tuple-element.104), channel_id=1, source_target_pairs={{0,16},{16,32},{32,48},{48,64},{64,80},{80,96},{96,112},{112,0},{1... | collective-permute-start | bytes 393224 | tf_op jit(solution)/shard_map/ppermute | solution.py:683
  26.8 8.3 %collective-permute-start.10 = (f32[192,128]{1,0:T(8,128)S(1)}, f32[192,128]{1,0:T(8,128)S(1)}, u32[]{:S(2)}, u32[]{:S(2)}) collective-permute-start(f32[192,128]{1,0:T(8,128)S(1)} %get-tuple-element.106), channel_id=1, source_target_pairs={{0,15},{1,0},{2,1},{3,2},{4,3},{5,4},{6,5},{7,6},{8,7},{9,8},{10,9... | collective-permute-start | bytes 294920 | tf_op jit(solution)/shard_map/ppermute | solution.py:683
  26.9 16.8 %collective-permute-start.6 = (f32[192,128]{1,0:T(8,128)S(1)}, f32[192,128]{1,0:T(8,128)S(1)}, u32[]{:S(2)}, u32[]{:S(2)}) collective-permute-start(f32[192,128]{1,0:T(8,128)S(1)} %get-tuple-element.102), channel_id=1, source_target_pairs={{0,112},{16,0},{32,16},{48,32},{64,48},{80,64},{96,80},{112,96},{1... | collective-permute-start | bytes 294920 | tf_op jit(solution)/shard_map/ppermute | solution.py:683
  32.2 6.9 %collective-permute-start.7 = (f32[32,128]{1,0:T(8,128)S(1)}, f32[32,128]{1,0:T(8,128)S(1)}, u32[]{:S(2)}, u32[]{:S(2)}) collective-permute-start(f32[32,128]{1,0:T(8,128)S(1)} %get-tuple-element.103), channel_id=1, source_target_pairs={{0,113},{1,114},{2,115},{3,116},{4,117},{5,118},{6,119},{7,120},{8... | collective-permute-start | bytes 49160 | tf_op jit(solution)/shard_map/ppermute | solution.py:689
  35.0 8.6 %collective-permute-start.9 = (f32[32,128]{1,0:T(8,128)S(1)}, f32[32,128]{1,0:T(8,128)S(1)}, u32[]{:S(2)}, u32[]{:S(2)}) collective-permute-start(f32[32,128]{1,0:T(8,128)S(1)} %get-tuple-element.105), channel_id=1, source_target_pairs={{0,31},{1,16},{2,17},{3,18},{4,19},{5,20},{6,21},{7,22},{8,23},{9,... | collective-permute-start | bytes 49160 | tf_op jit(solution)/shard_map/ppermute | solution.py:689

commit v4 on v2

--- a/solution.py
+++ b/solution.py
@@ -132,7 +132,7 @@
                     down[pl.ds(((DOWN_Y.index(d) * n + q) * 2 + x) * 4, 4), :] = read_down(d, q, x)
 
 
-def pack_first_body(links, yup, ydown, xdown, corner):
+def pack_first_body(links, xdown, xup, yup, ydown):
     def reader(row):
         return lambda d, q, x: links[pl.ds(((d * 18 + q) * 2 + x) * ROWS + row, 4, stride=2), :]
 
@@ -144,15 +144,15 @@
         for d in range(1, 4):
             xdown[pl.ds(((d - 1) * 12 + q) * 8, 8), :] = links[pl.ds((d * 18 + q) * 2 * ROWS + 2, 8), :]
         xdown[pl.ds(288 + q * 2, 2), :] = links[pl.ds((54 + q) * 2 * ROWS, 2), :]
-        corner[pl.ds(q * 4, 4), :] = links[pl.ds((18 + q) * 2 * ROWS + 3, 4, stride=2), :]
-
-
-def pack_x_body(links, ynext, yprev, xnext, corner, after, up):
+        for d in range(4):
+            xup[pl.ds((d * 12 + q) * 8, 8), :] = links[pl.ds(((d * 18 + q) * 2 + 1) * ROWS + 2, 8), :]
+        xup[pl.ds(384 + q * 2, 2), :] = links[pl.ds((q * 2 + 1) * ROWS + 10, 2), :]
+
+
+def pack_corners_body(ynext, yprev, up, down):
     for q in range(12):
-        for d in range(4):
-            up[pl.ds((d * 12 + q) * 8, 8), :] = links[pl.ds(((d * 18 + q) * 2 + 1) * ROWS + 2, 8), :]
-        up[pl.ds(384 + q * 2, 2), :] = links[pl.ds((q * 2 + 1) * ROWS + 10, 2), :]
-        up[pl.ds(408 + q * 4, 4), :] = ynext[pl.ds(q * 8 + 4, 4), :]
+        up[pl.ds(q * 4, 4), :] = ynext[pl.ds(q * 8 + 4, 4), :]
+        down[pl.ds(q * 4, 4), :] = yprev[pl.ds((12 + q) * 8, 4), :]
 
 
 def pack_lambda_x_body(lam, ynext, yprev, after, up, down):
@@ -263,7 +263,7 @@
     fill_mixed(bufs, NC)
 
 
-def fill_column(source, slots, corner, at, bufs, xe, edge, corner_to):
+def fill_column(source, slots, corner, bufs, xe, edge, corner_to):
     for slot, d in enumerate(slots):
         m = two_rows(lambda q: source[pl.ds((slot * 12 + q) * 8, 8), :])
 
@@ -279,7 +279,7 @@
 
     put(write_edge, m)
     buf, corner_dir, off = corner_to
-    m = two_rows(lambda q: corner[pl.ds(at + q * 4, 4), :])
+    m = two_rows(lambda q: corner[pl.ds(q * 4, 4), :])
 
     def write_corner(q, v):
         bufs[buf][pl.ds(place(corner_dir * NC + q, xe) + off, 4, stride=2), :] = v
@@ -288,12 +288,12 @@
 
 
 def fill_links_next(xnext, corner, bufs):
-    fill_column(xnext, (1, 2, 3), corner, 0, bufs, 3, (3, 0), (YM, 1, 2))
+    fill_column(xnext, (1, 2, 3), corner, bufs, 3, (3, 0), (YM, 1, 2))
     fill_high(bufs, NC)
 
 
-def fill_links_prev(xprev, bufs):
-    fill_column(xprev, (0, 1, 2, 3), xprev, 408, bufs, 0, (0, 10), (YP, 0, 3))
+def fill_links_prev(xprev, corner, bufs):
+    fill_column(xprev, (0, 1, 2, 3), corner, bufs, 0, (0, 10), (YP, 0, 3))
     fill_low(bufs, NC)
 
 
@@ -607,27 +607,27 @@
 
 
 def links_local_body(*refs):
-    links, incoming = refs[:2]
-    bufs, (inner, omega, loops, low) = refs[2:9], refs[9:]
+    links = refs[0]
+    bufs, (omega, loops, low) = refs[1:8], refs[8:]
     fill_links_local(links, bufs)
+    forward_items(0, bufs, omega, loops, low)
+
+
+def links_y_body(*refs):
+    ynext, yprev, incoming = refs[:3]
+    bufs, (omega, loops, low, inner) = refs[13:20], refs[20:]
+    fill_links_y(ynext, yprev, bufs)
     take_incoming(incoming, inner)
-    forward_items(0, bufs, omega, loops, low)
-
-
-def links_y_body(*refs):
-    ynext, yprev, xnext, corner, inner = refs[:5]
-    bufs, (omega, loops, low, lam, direct) = refs[15:22], refs[22:]
-    fill_links_y(ynext, yprev, bufs)
     forward_items(1, bufs, omega, loops, low)
-    fill_links_next(xnext, corner, bufs)
+
+
+def links_x_body(*refs):
+    xnext, cnext, xprev, cprev, inner = refs[:5]
+    bufs, (omega, loops, low, lam, direct, up, down) = refs[15:22], refs[22:]
+    fill_links_next(xnext, cnext, bufs)
     forward_items(2, bufs, omega, loops, low)
     finish_forward((1,), bufs, inner, loops, low, lam, direct)
-
-
-def links_x_body(*refs):
-    xprev, inner = refs[:2]
-    bufs, (omega, loops, low, lam, direct, up, down) = refs[14:21], refs[21:]
-    fill_links_prev(xprev, bufs)
+    fill_links_prev(xprev, cprev, bufs)
     forward_items(3, bufs, omega, loops, low)
     finish_forward((0,), bufs, inner, loops, low, lam, direct)
 
@@ -687,26 +687,18 @@
     return lax.ppermute(shard, axis, [(i, (i + by) % length) for i in range(length)])
 
 
-def diagonal(shard, by_x, by_y):
-    nx, ny = lax.axis_size("gx"), lax.axis_size("gy")
-    pairs = [(i * ny + j, (i + by_x) % nx * ny + (j + by_y) % ny) for i in range(nx) for j in range(ny)]
-    return lax.ppermute(shard, ("gx", "gy"), pairs)
-
-
 def body(links, incoming):
     links = jnp.transpose(links, (0, 1, 2, 3, 4, 6, 5, 7)).reshape(144 * ROWS, 128)
     shape = incoming.shape
     incoming = incoming.reshape(1152, 128)
-    yup, ydown, xdown, corner = call(pack_first_body, (links,), (408, 312, 312, 48))
+    xdown, xup, yup, ydown = call(pack_first_body, (links,), (312, 408, 408, 312))
+    xnext, xprev = shifted(xdown, "gx", -1), shifted(xup, "gx", 1)
     yprev, ynext = shifted(yup, "gy", 1), shifted(ydown, "gy", -1)
-    xnext, corner = shifted(xdown, "gx", -1), diagonal(corner, -1, 1)
-    inner, *kept = (lambda r: (r[7], *r[:7], *r[8:]))(
-        call(links_local_body, (links, incoming), buffer_rows(NC) + [1152, 1728, 864, 1152])
-    )
-    (xup,) = call(pack_x_body, (links, ynext, yprev, xnext, corner, kept[-1]), (456,))
-    xprev = shifted(xup, "gx", 1)
-    kept = call(links_y_body, (ynext, yprev, xnext, corner, inner), (512, 1152), kept)
-    r = call(links_x_body, (xprev, inner), (256, 192), kept)
+    cup, cdown = call(pack_corners_body, (ynext, yprev), (48, 48))
+    cprev, cnext = shifted(cup, "gx", 1), shifted(cdown, "gx", -1)
+    kept = call(links_local_body, (links,), buffer_rows(NC) + [1728, 864, 1152])
+    *kept, inner = call(links_y_body, (ynext, yprev, incoming), (1152,), kept)
+    r = call(links_x_body, (xnext, cnext, xprev, cprev, inner), (512, 1152, 256, 192), kept)
     bufs, omega, (lam, acc, yup, ydown) = r[:7], r[7], r[10:]
     yprev, ynext = shifted(yup, "gy", 1), shifted(ydown, "gy", -1)
     kept = call(lambda_local_body, (*bufs, omega, lam), buffer_rows(NA) + [1152], (acc,))

time: 46.7 us -> 44.6 us (0.955)
  waiting for transfers between devices: 13.9 us -> 7.58 us
  starting transfers between devices: 19.8 us -> 25 us
  local copies, waits for them, and re-layouts: 2.23 us -> 1.17 us
    ppermute x8 -> x10, starting transfers between devices: 19.8 us -> 25 us  [shifted(): lax.ppermute(shard, axis, [(i, (i + by) % length) for i in range(length)])]
    ppermute x1 -> x0, waiting for transfers between devices: 4.27 us -> none  [diagonal(): return lax.ppermute(shard, ('gx', 'gy'), pairs)]
    ppermute x8 -> x10, waiting for transfers between devices: 9.58 us -> 7.58 us  [shifted(): lax.ppermute(shard, axis, [(i, (i + by) % length) for i in range(length)])]
    unnamed x4 -> x6, local copies, waits for them, and re-layouts: 2.23 us -> 1.17 us
  transfers between devices with their start and end apart: 9 -> 10, of which waited for: 6 -> 7; matrix products, arithmetic and copies ran while one was open for 0% -> 0% of each run, Pallas kernels for 15% -> 13%
where the time goes in v4:
time: 44.6 us; the launch traced here: 44.4 us
  starting transfers between devices  25 us (56%)
  Pallas kernels  10.6 us (24%)
  waiting for transfers between devices  7.58 us (17%)
  local copies, waits for them, and re-layouts  1.17 us (3%)
    ppermute x10, starting transfers between devices, shifted(): lax.ppermute(shard, axis, [(i, (i + by) % length) for i in range(length)])  25 us
    pallas_call x9, Pallas kernels, call(): pl.pallas_call(body, out_shape=tuple(shapes), in_specs=[pl.BlockSpec(memo...  10.6 us
    ppermute x10, waiting for transfers between devices, shifted(): lax.ppermute(shard, axis, [(i, (i + by) % length) for i in range(length)])  7.58 us
    unnamed x6, local copies, waits for them, and re-layouts  1.17 us
  transfers between devices with their start and end apart: 10, of which 7 were waited for; matrix products, arithmetic and copies ran while one was open for 0% of the time, Pallas kernels for 13%

profile of v4, /device:TPU:0, one launch (start us, length us, event | category | flops | bytes accessed | tf_op | source)
XLA Modules:
  0.0 44.4 jit_solution(1545332907745086603)
XLA Ops:
  0.0 1.2 %copy-done = f32[4,3,3,2,2,2,6,128]{7,5,6,4,3,2,1,0:T(2,128)S(1)} copy-done((f32[4,3,3,2,2,2,6,128]{7,5,6,4,3,2,1,0:T(2,128)S(1)}, f32[4,3,3,2,2,2,6,128]{7,5,6,4,3,2,1,0:T(2,128)}, u32[]{:S(2)}) %copy-start) | copy-done | bytes 884760
  1.2 0.1 shard_map.28
  1.3 0.1 collective-permute-start.2
  1.4 4.0 %collective-permute-start.4 = (f32[408,128]{1,0:T(8,128)S(1)}, f32[408,128]{1,0:T(8,128)S(1)}, u32[]{:S(2)}, u32[]{:S(2)}) collective-permute-start(f32[408,128]{1,0:T(8,128)S(1)} %get-tuple-element.69), channel_id=1, source_target_pairs={{0,16},{16,32},{32,48},{48,64},{64,80},{80,96},{96,112},{112,0},{1... | collective-permute-start | bytes 626696 | tf_op jit(solution)/shard_map/ppermute | solution.py:687
  5.4 2.9 %collective-permute-start.1 = (f32[312,128]{1,0:T(8,128)S(1)}, f32[312,128]{1,0:T(8,128)S(1)}, u32[]{:S(2)}, u32[]{:S(2)}) collective-permute-start(f32[312,128]{1,0:T(8,128)S(1)} %get-tuple-element.66), channel_id=1, source_target_pairs={{0,15},{1,0},{2,1},{3,2},{4,3},{5,4},{6,5},{7,6},{8,7},{9,8},{10,9... | collective-permute-start | bytes 479240 | tf_op jit(solution)/shard_map/ppermute | solution.py:687
  8.3 3.1 %collective-permute-start = (f32[312,128]{1,0:T(8,128)S(1)}, f32[312,128]{1,0:T(8,128)S(1)}, u32[]{:S(2)}, u32[]{:S(2)}) collective-permute-start(f32[312,128]{1,0:T(8,128)S(1)} %get-tuple-element.65), channel_id=1, source_target_pairs={{0,112},{16,0},{32,16},{48,32},{64,48},{80,64},{96,80},{112,96},{1... | collective-permute-start | bytes 479240 | tf_op jit(solution)/shard_map/ppermute | solution.py:687
  11.4 5.3 %collective-permute-start.3 = (f32[48,128]{1,0:T(8,128)S(1)}, f32[48,128]{1,0:T(8,128)S(1)}, u32[]{:S(2)}, u32[]{:S(2)}) collective-permute-start(f32[48,128]{1,0:T(8,128)S(1)} %get-tuple-element.68), channel_id=1, source_target_pairs={{0,112},{16,0},{32,16},{48,32},{64,48},{80,64},{96,80},{112,96},{1... | collective-permute-start | bytes 73736 | tf_op jit(solution)/shard_map/ppermute | solution.py:687
  16.7 1.1 %shard_map.30 = (f32[3456,128]{1,0:T(8,128)S(1)}, f32[3456,128]{1,0:T(8,128)S(1)}, f32[3456,128]{1,0:T(8,128)S(1)}, f32[3456,128]{1,0:T(8,128)S(1)}, f32[3456,12...) custom-call(f32[1728,128]{1,0:T(8,128)S(1)} %bitcast.6), custom_call_target="tpu_custom_call" | custom-call | tf_op jit(solution)/shard_map/pallas_call | solution.py:674
  17.8 1.2 %shard_map.31 = (f32[3456,128]{1,0:T(8,128)S(1)}, f32[3456,128]{1,0:T(8,128)S(1)}, f32[3456,128]{1,0:T(8,128)S(1)}, f32[3456,128]{1,0:T(8,128)S(1)}, f32[3456,12...) custom-call(f32[312,128]{1,0:T(8,128)S(1)} %collective-permute-done., ...), custom_call_target="tpu_custom_call", output_to_operand_aliasing={{0}: (3, {}), {1}: (4, {}), {2}: (5, {}), {3}: (6, {}), {4}... | custom-call | tf_op jit(solution)/shard_map/pallas_call | solution.py:674
  19.1 0.3 collective-permute-done.refs_0_
  19.4 0.4 collective-permute-done.3.refs_1_
  19.8 4.3 %collective-permute-done.5.refs_3_ = f32[48,128]{1,0:T(8,128)S(1)} collective-permute-done((f32[48,128]{1,0:T(8,128)S(1)}, f32[48,128]{1,0:T(8,128)S(1)}, u32[]{:S(2)}, u32[]{:S(2)}) %collective-permute-start.5) | collective-permute-done | bytes 24608 | tf_op jit(solution)/shard_map/ppermute | solution.py:687
  24.1 2.3 %shard_map.32 = (f32[3456,128]{1,0:T(8,128)S(1)}, f32[3456,128]{1,0:T(8,128)S(1)}, f32[3456,128]{1,0:T(8,128)S(1)}, f32[3456,128]{1,0:T(8,128)S(1)}, f32[3456,12...) custom-call(f32[312,128]{1,0:T(8,128)S(1)} %collective-permute-done., ...), custom_call_target="tpu_custom_call", output_to_operand_aliasing={{0}: (5, {}), {1}: (6, {}), {2}: (7, {}), {3}: (8, {}), {4}... | custom-call | tf_op jit(solution)/shard_map/pallas_call | solution.py:674
  26.4 0.1 collective-permute-start.7
  26.5 3.8 %collective-permute-start.6 = (f32[192,128]{1,0:T(8,128)S(1)}, f32[192,128]{1,0:T(8,128)S(1)}, u32[]{:S(2)}, u32[]{:S(2)}) collective-permute-start(f32[192,128]{1,0:T(8,128)S(1)} %get-tuple-element.101), channel_id=1, source_target_pairs={{0,15},{1,0},{2,1},{3,2},{4,3},{5,4},{6,5},{7,6},{8,7},{9,8},{10,9... | collective-permute-start | bytes 294920 | tf_op jit(solution)/shard_map/ppermute | solution.py:687
  30.4 1.7 %shard_map.33 = (f32[1152,128]{1,0:T(8,128)S(1)}, f32[1536,128]{1,0:T(8,128)S(1)}, f32[1536,128]{1,0:T(8,128)S(1)}, f32[1536,128]{1,0:T(8,128)S(1)}, f32[1536,12...) custom-call(f32[3456,128]{1,0:T(8,128)S(1)} %get-tuple-element.92.re, ...), custom_call_target="tpu_custom_call", output_to_operand_aliasing={{0}: (9, {})} | custom-call | tf_op jit(solution)/shard_map/pallas_call | solution.py:674
  32.1 0.5 %collective-permute-done.6.ynext.refs_8_ = f32[192,128]{1,0:T(8,128)S(1)} collective-permute-done((f32[192,128]{1,0:T(8,128)S(1)}, f32[192,128]{1,0:T(8,128)S(1)}, u32[]{:S(2)}, u32[]{:S(2)}) %collective-permute-start.6) | collective-permute-done | bytes 98336 | tf_op jit(solution)/shard_map/ppermute | solution.py:687
  32.6 0.8 %collective-permute-done.7.yprev.refs_9_ = f32[256,128]{1,0:T(8,128)S(1)} collective-permute-done((f32[256,128]{1,0:T(8,128)S(1)}, f32[256,128]{1,0:T(8,128)S(1)}, u32[]{:S(2)}, u32[]{:S(2)}) %collective-permute-start.7) | collective-permute-done | bytes 131104 | tf_op jit(solution)/shard_map/ppermute | solution.py:687
  33.4 0.1 collective-permute-start.9
  33.5 5.6 %collective-permute-start.8 = (f32[224,128]{1,0:T(8,128)S(1)}, f32[224,128]{1,0:T(8,128)S(1)}, u32[]{:S(2)}, u32[]{:S(2)}) collective-permute-start(f32[224,128]{1,0:T(8,128)S(1)} %get-tuple-element.105), channel_id=1, source_target_pairs={{0,112},{16,0},{32,16},{48,32},{64,48},{80,64},{96,80},{112,96},{1... | collective-permute-start | bytes 344072 | tf_op jit(solution)/shard_map/ppermute | solution.py:687
  39.1 1.9 %shard_map.35 = (f32[1152,128]{1,0:T(8,128)S(1)}, f32[1536,128]{1,0:T(8,128)S(1)}, f32[1536,128]{1,0:T(8,128)S(1)}, f32[1536,128]{1,0:T(8,128)S(1)}, f32[1536,12...) custom-call(f32[3456,128]{1,0:T(8,128)S(1)} %get-tuple-element.92.re, ...), custom_call_target="tpu_custom_call", output_to_operand_aliasing={{0}: (10, {}), {1}: (11, {}), {2}: (12, {}), {3}: (13, {}),... | custom-call | tf_op jit(solution)/shard_map/pallas_call | solution.py:674
  41.0 0.5 %collective-permute-done.8.refs_8_ = f32[224,128]{1,0:T(8,128)S(1)} collective-permute-done((f32[224,128]{1,0:T(8,128)S(1)}, f32[224,128]{1,0:T(8,128)S(1)}, u32[]{:S(2)}, u32[]{:S(2)}) %collective-permute-start.8) | collective-permute-done | bytes 114720 | tf_op jit(solution)/shard_map/ppermute | solution.py:687
  41.5 0.7 %collective-permute-done.9.refs_9_ = f32[288,128]{1,0:T(8,128)S(1)} collective-permute-done((f32[288,128]{1,0:T(8,128)S(1)}, f32[288,128]{1,0:T(8,128)S(1)}, u32[]{:S(2)}, u32[]{:S(2)}) %collective-permute-start.9) | collective-permute-done | bytes 147488 | tf_op jit(solution)/shard_map/ppermute | solution.py:687
  42.2 2.2 %shard_map.36 = (f32[1152,128]{1,0:T(8,128)}, f32[1152,128]{1,0:T(8,128)S(1)}, f32[1536,128]{1,0:T(8,128)S(1)}, f32[1536,128]{1,0:T(8,128)S(1)}, f32[1536,128]{1...) custom-call(f32[3456,128]{1,0:T(8,128)S(1)} %get-tuple-element.92.re, ...), custom_call_target="tpu_custom_call", output_to_operand_aliasing={{1}: (10, {}), {2}: (11, {}), {3}: (12, {}), {4}: (13, {}),... | custom-call | tf_op jit(solution)/shard_map/pallas_call | solution.py:674
  (11 shorter events, 0.0 us)
Async XLA Ops:
  0.0 1.2 %copy-start = (f32[4,3,3,2,2,2,6,128]{7,5,6,4,3,2,1,0:T(2,128)S(1)}, f32[4,3,3,2,2,2,6,128]{7,5,6,4,3,2,1,0:T(2,128)}, u32[]{:S(2)}) copy-start(f32[4,3,3,2,2,2,6,128]{7,5,6,4,3,2,1,0:T(2,128)} %param.2) | copy-start | bytes 2654212
  1.2 15.5 %copy-start.1 = (f32[4,3,3,2,2,2,6,128]{7,5,6,4,3,2,1,0:T(2,128)S(1)}, f32[4,3,3,2,2,2,6,128]{7,5,6,4,3,2,1,0:T(2,128)}, u32[]{:S(2)}) copy-start(f32[4,3,3,2,2,2,6,128]{7,5,6,4,3,2,1,0:T(2,128)} %param.2) | copy-start | bytes 2654212
  1.2 16.7 %copy-start.2 = (f32[4,3,3,2,2,2,4,128]{7,6,5,4,3,2,1,0:T(4,128)S(1)}, f32[4,3,3,2,2,2,4,128]{7,6,5,4,3,2,1,0:T(4,128)}, u32[]{:S(2)}) copy-start(f32[4,3,3,2,2,2,4,128]{7,6,5,4,3,2,1,0:T(4,128)} %param.3) | copy-start | bytes 1769476
  1.3 10.1 %collective-permute-start.2 = (f32[408,128]{1,0:T(8,128)S(1)}, f32[408,128]{1,0:T(8,128)S(1)}, u32[]{:S(2)}, u32[]{:S(2)}) collective-permute-start(f32[408,128]{1,0:T(8,128)S(1)} %get-tuple-element.67), channel_id=1, source_target_pairs={{0,1},{1,2},{2,3},{3,4},{4,5},{5,6},{6,7},{7,8},{8,9},{9,10},{10,1... | collective-permute-start | bytes 626696 | tf_op jit(solution)/shard_map/ppermute | solution.py:687
  1.4 18.0 %collective-permute-start.4 = (f32[408,128]{1,0:T(8,128)S(1)}, f32[408,128]{1,0:T(8,128)S(1)}, u32[]{:S(2)}, u32[]{:S(2)}) collective-permute-start(f32[408,128]{1,0:T(8,128)S(1)} %get-tuple-element.69), channel_id=1, source_target_pairs={{0,16},{16,32},{32,48},{48,64},{64,80},{80,96},{96,112},{112,0},{1... | collective-permute-start | bytes 626696 | tf_op jit(solution)/shard_map/ppermute | solution.py:687
  5.4 6.0 %collective-permute-start.1 = (f32[312,128]{1,0:T(8,128)S(1)}, f32[312,128]{1,0:T(8,128)S(1)}, u32[]{:S(2)}, u32[]{:S(2)}) collective-permute-start(f32[312,128]{1,0:T(8,128)S(1)} %get-tuple-element.66), channel_id=1, source_target_pairs={{0,15},{1,0},{2,1},{3,2},{4,3},{5,4},{6,5},{7,6},{8,7},{9,8},{10,9... | collective-permute-start | bytes 479240 | tf_op jit(solution)/shard_map/ppermute | solution.py:687
  8.3 11.1 %collective-permute-start = (f32[312,128]{1,0:T(8,128)S(1)}, f32[312,128]{1,0:T(8,128)S(1)}, u32[]{:S(2)}, u32[]{:S(2)}) collective-permute-start(f32[312,128]{1,0:T(8,128)S(1)} %get-tuple-element.65), channel_id=1, source_target_pairs={{0,112},{16,0},{32,16},{48,32},{64,48},{80,64},{96,80},{112,96},{1... | collective-permute-start | bytes 479240 | tf_op jit(solution)/shard_map/ppermute | solution.py:687
  11.4 8.4 %collective-permute-start.3 = (f32[48,128]{1,0:T(8,128)S(1)}, f32[48,128]{1,0:T(8,128)S(1)}, u32[]{:S(2)}, u32[]{:S(2)}) collective-permute-start(f32[48,128]{1,0:T(8,128)S(1)} %get-tuple-element.68), channel_id=1, source_target_pairs={{0,112},{16,0},{32,16},{48,32},{64,48},{80,64},{96,80},{112,96},{1... | collective-permute-start | bytes 73736 | tf_op jit(solution)/shard_map/ppermute | solution.py:687
  16.7 7.4 %collective-permute-start.5 = (f32[48,128]{1,0:T(8,128)S(1)}, f32[48,128]{1,0:T(8,128)S(1)}, u32[]{:S(2)}, u32[]{:S(2)}) collective-permute-start(f32[48,128]{1,0:T(8,128)S(1)} %get-tuple-element.70), channel_id=1, source_target_pairs={{0,16},{16,32},{32,48},{48,64},{64,80},{80,96},{96,112},{112,0},{1... | collective-permute-start | bytes 73736 | tf_op jit(solution)/shard_map/ppermute | solution.py:687
  26.4 6.9 %collective-permute-start.7 = (f32[256,128]{1,0:T(8,128)S(1)}, f32[256,128]{1,0:T(8,128)S(1)}, u32[]{:S(2)}, u32[]{:S(2)}) collective-permute-start(f32[256,128]{1,0:T(8,128)S(1)} %get-tuple-element.102), channel_id=1, source_target_pairs={{0,1},{1,2},{2,3},{3,4},{4,5},{5,6},{6,7},{7,8},{8,9},{9,10},{10,1... | collective-permute-start | bytes 393224 | tf_op jit(solution)/shard_map/ppermute | solution.py:687
  26.5 6.1 %collective-permute-start.6 = (f32[192,128]{1,0:T(8,128)S(1)}, f32[192,128]{1,0:T(8,128)S(1)}, u32[]{:S(2)}, u32[]{:S(2)}) collective-permute-start(f32[192,128]{1,0:T(8,128)S(1)} %get-tuple-element.101), channel_id=1, source_target_pairs={{0,15},{1,0},{2,1},{3,2},{4,3},{5,4},{6,5},{7,6},{8,7},{9,8},{10,9... | collective-permute-start | bytes 294920 | tf_op jit(solution)/shard_map/ppermute | solution.py:687
  33.4 8.8 %collective-permute-start.9 = (f32[288,128]{1,0:T(8,128)S(1)}, f32[288,128]{1,0:T(8,128)S(1)}, u32[]{:S(2)}, u32[]{:S(2)}) collective-permute-start(f32[288,128]{1,0:T(8,128)S(1)} %get-tuple-element.106), channel_id=1, source_target_pairs={{0,16},{16,32},{32,48},{48,64},{64,80},{80,96},{96,112},{112,0},{1... | collective-permute-start | bytes 442376 | tf_op jit(solution)/shard_map/ppermute | solution.py:687
  33.5 8.0 %collective-permute-start.8 = (f32[224,128]{1,0:T(8,128)S(1)}, f32[224,128]{1,0:T(8,128)S(1)}, u32[]{:S(2)}, u32[]{:S(2)}) collective-permute-start(f32[224,128]{1,0:T(8,128)S(1)} %get-tuple-element.105), channel_id=1, source_target_pairs={{0,112},{16,0},{32,16},{48,32},{64,48},{80,64},{96,80},{112,96},{1... | collective-permute-start | bytes 344072 | tf_op jit(solution)/shard_map/ppermute | solution.py:687

commit v5 on v4

--- a/solution.py
+++ b/solution.py
@@ -97,6 +97,19 @@
     return out
 
 
+def carried_back(u, v):
+    half = mm(u, anti(v), True, False)
+    diag = [entry(half, u, i, i, False, False, (False, True))[1] for i in range(2)]
+    out = [diag[0], diag[1], -diag[0] - diag[1]]
+    for i, j in UPPER:
+        out += list(entry(half, u, i, j))
+    return out
+
+
+def first_rows():
+    return lax.broadcasted_iota(jnp.int32, (8, 128), 0) % 2 == 0
+
+
 def third_row(m):
     row = []
     for j in range(3):
@@ -132,7 +145,7 @@
                     down[pl.ds(((DOWN_Y.index(d) * n + q) * 2 + x) * 4, 4), :] = read_down(d, q, x)
 
 
-def pack_first_body(links, xdown, xup, yup, ydown):
+def pack_first_body(links, xdown, yup, ydown):
     def reader(row):
         return lambda d, q, x: links[pl.ds(((d * 18 + q) * 2 + x) * ROWS + row, 4, stride=2), :]
 
@@ -144,9 +157,26 @@
         for d in range(1, 4):
             xdown[pl.ds(((d - 1) * 12 + q) * 8, 8), :] = links[pl.ds((d * 18 + q) * 2 * ROWS + 2, 8), :]
         xdown[pl.ds(288 + q * 2, 2), :] = links[pl.ds((54 + q) * 2 * ROWS, 2), :]
-        for d in range(4):
-            xup[pl.ds((d * 12 + q) * 8, 8), :] = links[pl.ds(((d * 18 + q) * 2 + 1) * ROWS + 2, 8), :]
-        xup[pl.ds(384 + q * 2, 2), :] = links[pl.ds((q * 2 + 1) * ROWS + 10, 2), :]
+
+
+def pack_up_body(links, up):
+    def read(d, row):
+        return load_matrix(lambda i, j, ri: links[pl.ds((comp(d, i, j, ri) * 2 + 1) * ROWS + row, 8), :])
+
+    across = read(0, 2)
+    for m in (1, 2, 3):
+        side = read(m, 2)
+        half = [[entry(across, side, i, k, True, False) for k in range(3)] for i in range(2)]
+        if m == 2:
+            last = [[(roll_z(v[0], 1), roll_z(v[1], 1)) for v in row] for row in across]
+        else:
+            last = read(0, 3 if m == 1 else 4)
+        for i in range(2):
+            for j in range(3):
+                value = entry(half, last, i, j)
+                for ri in range(2):
+                    out = jnp.where(first_rows(), value[ri], half[i][j][ri]) if m == 1 else value[ri]
+                    up[pl.ds(((m - 1) * 12 + (i * 3 + j) * 2 + ri) * 8, 8), :] = out
 
 
 def pack_corners_body(ynext, yprev, up, down):
@@ -155,13 +185,10 @@
         down[pl.ds(q * 4, 4), :] = yprev[pl.ds((12 + q) * 8, 4), :]
 
 
-def pack_lambda_x_body(lam, ynext, yprev, after, up, down):
-    for c in range(32):
-        up[pl.ds(c * 8, 8), :] = lam[pl.ds((c * 2 + 1) * 8, 8), :]
-        if c >= NA:
-            down[pl.ds((c - NA) * 8, 8), :] = lam[pl.ds(c * 16, 8), :]
+def pack_lambda_down_body(lam, yprev, after, down):
+    for c in range(24):
+        down[pl.ds(c * 8, 8), :] = lam[pl.ds((c + NA) * 16, 8), :]
     for k in range(NA):
-        up[pl.ds(256 + k * 4, 4), :] = ynext[pl.ds(k * 8 + 4, 4), :]
         down[pl.ds(192 + k * 4, 4), :] = yprev[pl.ds((NA + k) * 8, 4), :]
 
 
@@ -222,13 +249,6 @@
         bufs[YM][pl.ds(side + 3, 4, stride=2), :] = bufs[O][pl.ds(side + 2, 4, stride=2), :]
 
 
-def fill_low(bufs, n):
-    for k in range(n):
-        low = place(k, 0)
-        bufs[ZP][pl.ds(low + 2, 8), :] = roll_z(bufs[O][pl.ds(low + 2, 8), :], 1)
-        bufs[YP][pl.ds(low + 2, 4, stride=2), :] = bufs[O][pl.ds(low + 3, 4, stride=2), :]
-
-
 def fill_links_local(links, bufs):
     for c in range(72):
         for x in range(2):
@@ -263,38 +283,49 @@
     fill_mixed(bufs, NC)
 
 
-def fill_column(source, slots, corner, bufs, xe, edge, corner_to):
-    for slot, d in enumerate(slots):
-        m = two_rows(lambda q: source[pl.ds((slot * 12 + q) * 8, 8), :])
+def fill_links_next(xnext, bufs):
+    for d in (1, 2, 3):
+        m = two_rows(lambda q: xnext[pl.ds(((d - 1) * 12 + q) * 8, 8), :])
 
         def write(q, v):
-            bufs[O][pl.ds(place(d * NC + q, xe) + 2, 8), :] = v
+            bufs[O][pl.ds(place(d * NC + q, 3) + 2, 8), :] = v
 
         put(write, m)
-    d, row = edge
-    m = two_rows(lambda q: source[pl.ds(len(slots) * 96 + q * 2, 2), :])
+    m = two_rows(lambda q: xnext[pl.ds(288 + q * 2, 2), :])
 
     def write_edge(q, v):
-        bufs[O][pl.ds(place(d * NC + q, xe) + row, 2), :] = v
+        bufs[O][pl.ds(place(3 * NC + q, 3), 2), :] = v
 
     put(write_edge, m)
-    buf, corner_dir, off = corner_to
+    fill_high(bufs, NC)
+
+
+def fill_corner(corner, buf, d, xe, off, bufs):
     m = two_rows(lambda q: corner[pl.ds(q * 4, 4), :])
 
     def write_corner(q, v):
-        bufs[buf][pl.ds(place(corner_dir * NC + q, xe) + off, 4, stride=2), :] = v
+        bufs[buf][pl.ds(place(d * NC + q, xe) + off, 4, stride=2), :] = v
 
     put(write_corner, m)
 
 
-def fill_links_next(xnext, corner, bufs):
-    fill_column(xnext, (1, 2, 3), corner, bufs, 3, (3, 0), (YM, 1, 2))
-    fill_high(bufs, NC)
-
-
-def fill_links_prev(xprev, corner, bufs):
-    fill_column(xprev, (0, 1, 2, 3), corner, bufs, 0, (0, 10), (YP, 0, 3))
-    fill_low(bufs, NC)
+def take_staples(xprev, bufs, ready):
+    for m in (1, 2, 3):
+        staple = two_rows(lambda q: xprev[pl.ds(((m - 1) * 12 + q) * 8, 8), :])
+        if m == 1:
+            whole = mm(staple, link(bufs, 0, step((0, -1), (1, 1)), 0))
+            staple = [
+                [tuple(jnp.where(first_rows(), staple[i][j][ri], whole[i][j][ri]) for ri in range(2)) for j in range(3)]
+                for i in range(3)
+            ]
+        for i in range(3):
+            for j in range(3):
+                for ri in range(2):
+                    ready[pl.ds(comp(m - 1, i, j, ri) * 8, 8), :] = staple[i][j][ri]
+
+
+def ready_staple(ready, m):
+    return load_matrix(lambda i, j, ri: ready[pl.ds(comp(m - 1, i, j, ri) * 8, 8), :])
 
 
 def fill_lambda_local(lam, bufs):
@@ -326,23 +357,14 @@
     fill_mixed(bufs, NA)
 
 
-def fill_lambda_x(xnext, xprev, bufs):
+def fill_lambda_next(xnext, bufs):
     zero = jnp.zeros((2, 128), jnp.float32)
-    for d in range(4):
-        for k in range(NA):
-            high, low = place(d * NA + k, 3), place(d * NA + k, 0)
-            if d != 0:
-                bufs[O][pl.ds(high + 2, 8), :] = xnext[pl.ds(((d - 1) * NA + k) * 8, 8), :]
-            bufs[O][pl.ds(low + 2, 8), :] = xprev[pl.ds((d * NA + k) * 8, 8), :]
-            if d == 3:
-                bufs[O][pl.ds(high, 2), :] = zero
-            if d == 0:
-                bufs[O][pl.ds(low + 10, 2), :] = zero
+    for c in range(24):
+        bufs[O][pl.ds(place(NA + c, 3) + 2, 8), :] = xnext[pl.ds(c * 8, 8), :]
     for k in range(NA):
+        bufs[O][pl.ds(place(3 * NA + k, 3), 2), :] = zero
         bufs[YM][pl.ds(place(NA + k, 3) + 2, 4, stride=2), :] = xnext[pl.ds(192 + k * 4, 4), :]
-        bufs[YP][pl.ds(place(k, 0) + 3, 4, stride=2), :] = xprev[pl.ds(256 + k * 4, 4), :]
     fill_high(bufs, NA)
-    fill_low(bufs, NA)
 
 
 def step(*signed):
@@ -374,7 +396,7 @@
     return unpack8([read(k) for k in range(NA)])
 
 
-def exponent_force(v, u, target, clow):
+def exponent_force(v, m, target, clow):
     a = v[:3]
     off = [(v[3 + 2 * k], v[4 + 2 * k]) for k in range(3)]
     norm = [r * r + s * s for r, s in off]
@@ -398,7 +420,6 @@
     p1i = dd * (1.0 / 24.0 + c * (1.0 / 360.0))
     p2r = 0.5 + c * (1.0 / 24.0 + c * (1.0 / 720.0))
     p2i = dd * (1.0 / 120.0)
-    m = mm(target, u, False, True)
     hd = [m[i][i][0] for i in range(3)]
     kd = [m[i][i][1] for i in range(3)]
     ho = [(0.5 * (m[i][j][0] + m[j][i][0]), 0.5 * (m[i][j][1] - m[j][i][1])) for i, j in UPPER]
@@ -481,7 +502,7 @@
         if x + offset[0] == -1:
             found = 3
         elif x + offset[0] == 2:
-            found = max(found, 2)
+            found = max(found, 3 if offset[1] else 2)
         elif offset[1]:
             found = max(found, 1)
     return found
@@ -517,7 +538,7 @@
         inner[pl.ds(c * 8 + 1, 4, stride=2), :] = incoming[pl.ds(c * 8 + 4, 4), :]
 
 
-def forward_items(wanted, bufs, omega, loops, low):
+def forward_items(wanted, bufs, omega, loops, low, ready=None):
     planes, lowers = items(wanted)
     begun = {(m, x) for w in range(wanted) for m, _, x in items(w)[1]}
     for p, m, n, x in planes:
@@ -533,14 +554,24 @@
             if not mine:
                 continue
             for n in mine:
-                e, g, h = [link(bufs, which, offset, x) for which, offset in lower_fields(m, n)]
-                term = mm(mm(e, g, True, False), h)
+                if n == 0 and x == 0:
+                    term = ready_staple(ready, m)
+                else:
+                    e, g, h = [link(bufs, which, offset, x) for which, offset in lower_fields(m, n)]
+                    term = mm(mm(e, g, True, False), h)
                 value = term if value is None else madd(value, term)
             store_cells(low, m * 18, x, value)
 
 
-def finish_forward(xs, bufs, inner, loops, low, lam_out, direct):
-    for x in xs:
+def target_products(bufs, inner, moved):
+    for x in range(2):
+        for m in range(4):
+            target = load_cells(inner, m * 18, x)
+            store_cells(moved, m * 18, x, mm(target, link(bufs, m, step(), x), False, True))
+
+
+def finish_forward(bufs, inner, moved, loops, low, lam_out, direct):
+    for x in range(2):
         for m in range(4):
             u = link(bufs, m, step(), x)
             below = load_cells(low, m * 18, x)
@@ -554,13 +585,13 @@
             v = [(0.5 * smear_weight) * (v[k] - mean) for k in range(3)] + [
                 (0.5 * smear_weight) * v[k] for k in range(3, 9)
             ]
-            lam, force = exponent_force(v, u, load_cells(inner, m * 18, x), below)
+            lam, force = exponent_force(v, load_cells(moved, m * 18, x), load_cells(inner, m * 18, x), below)
             for k, v in enumerate(lam[:2] + lam[3:]):
                 lam_out[cells(m * NA, k, x), :] = v
             store_cells(direct, m * 18, x, force)
 
 
-def backward_items(wanted, bufs, lams, omega, sums, acc):
+def backward_items(wanted, bufs, lams, omega, sums, acc, ready=None, xprev=None):
     planes, lowers = items(wanted)
     begun = {(d, x) for w in range(wanted) for _, m, n, x in items(w)[0] for d in (m, n)}
 
@@ -586,6 +617,10 @@
                 continue
             force = load_cells(acc, m * 18, x)
             for n in mine:
+                if n == 0 and x == 0:
+                    y = unpack8([xprev[pl.ds(((m - 1) * NA + k) * 8, 8), :] for k in range(NA)])
+                    force = madd(force, mm(anti(y), ready_staple(ready, m)))
+                    continue
                 fields = lower_fields(m, n)
                 e, g, h = [link(bufs, which, offset, x) for which, offset in fields]
                 le, lg, lh = [lam_at(lams, which, offset, x) for which, offset in fields]
@@ -615,21 +650,28 @@
 
 def links_y_body(*refs):
     ynext, yprev, incoming = refs[:3]
-    bufs, (omega, loops, low, inner) = refs[13:20], refs[20:]
+    bufs, (omega, loops, low, inner, moved) = refs[13:20], refs[20:]
     fill_links_y(ynext, yprev, bufs)
     take_incoming(incoming, inner)
     forward_items(1, bufs, omega, loops, low)
+    target_products(bufs, inner, moved)
+
+
+def links_next_body(*refs):
+    xnext = refs[0]
+    bufs, (omega, loops, low) = refs[11:18], refs[18:]
+    fill_links_next(xnext, bufs)
+    forward_items(2, bufs, omega, loops, low)
 
 
 def links_x_body(*refs):
-    xnext, cnext, xprev, cprev, inner = refs[:5]
-    bufs, (omega, loops, low, lam, direct, up, down) = refs[15:22], refs[22:]
-    fill_links_next(xnext, cnext, bufs)
-    forward_items(2, bufs, omega, loops, low)
-    finish_forward((1,), bufs, inner, loops, low, lam, direct)
-    fill_links_prev(xprev, cprev, bufs)
-    forward_items(3, bufs, omega, loops, low)
-    finish_forward((0,), bufs, inner, loops, low, lam, direct)
+    cnext, xprev, cprev, inner, moved = refs[:5]
+    bufs, (omega, loops, low, lam, direct, up, down, ready) = refs[15:22], refs[22:]
+    fill_corner(cnext, YM, 1, 3, 2, bufs)
+    fill_corner(cprev, YP, 0, 0, 3, bufs)
+    take_staples(xprev, bufs, ready)
+    forward_items(3, bufs, omega, loops, low, ready)
+    finish_forward(bufs, inner, moved, loops, low, lam, direct)
 
     def reader(row):
         return lambda d, q, x: lam[pl.ds(((d * NA + q) * 2 + x) * 8 + row, 4, stride=2), :]
@@ -644,19 +686,32 @@
     backward_items(0, bufs, lams, omega, sums, acc)
 
 
+def lambda_up_body(*refs):
+    ynext, yprev, links = refs[:3]
+    lams, up = refs[10:17], refs[17]
+    fill_lambda_y(ynext, yprev, lams)
+    here = step()
+    for m in (1, 2, 3):
+        a, d = link([links], 0, here, 1), link([links], m, here, 1)
+        la, ld, lc = lam_at(lams, 0, here, 1), lam_at(lams, m, here, 1), lam_at(lams, 0, step((m, 1)), 1)
+        lc = carried(d, lc)
+        y = carried_back(a, [ld[k] - la[k] + lc[k] for k in range(9)])
+        for k, v in enumerate(y[:2] + y[3:]):
+            up[pl.ds(((m - 1) * NA + k) * 8, 8), :] = v
+
+
 def lambda_y_body(*refs):
-    bufs, (omega, ynext, yprev) = refs[:7], refs[7:10]
-    acc, lams, sums = refs[19], refs[20:27], refs[27]
-    fill_lambda_y(ynext, yprev, lams)
+    bufs, omega, lams = refs[:7], refs[7], refs[8:15]
+    acc, sums = refs[17:]
     backward_items(1, bufs, lams, omega, sums, acc)
 
 
 def lambda_x_body(*refs):
-    bufs, (omega, xnext, xprev) = refs[:7], refs[7:10]
-    out, acc, lams, sums = refs[19], refs[20], refs[21:28], refs[28]
-    fill_lambda_x(xnext, xprev, lams)
+    bufs, (omega, ready, xnext, xprev) = refs[:7], refs[7:11]
+    out, acc, lams, sums = refs[20], refs[21], refs[22:29], refs[29]
+    fill_lambda_next(xnext, lams)
     backward_items(2, bufs, lams, omega, sums, acc)
-    backward_items(3, bufs, lams, omega, sums, acc)
+    backward_items(3, bufs, lams, omega, sums, acc, ready, xprev)
     finish_backward(bufs, sums, acc, out)
 
 
@@ -691,21 +746,26 @@
     links = jnp.transpose(links, (0, 1, 2, 3, 4, 6, 5, 7)).reshape(144 * ROWS, 128)
     shape = incoming.shape
     incoming = incoming.reshape(1152, 128)
-    xdown, xup, yup, ydown = call(pack_first_body, (links,), (312, 408, 408, 312))
-    xnext, xprev = shifted(xdown, "gx", -1), shifted(xup, "gx", 1)
+    xdown, yup, ydown = call(pack_first_body, (links,), (312, 408, 312))
+    xnext = shifted(xdown, "gx", -1)
     yprev, ynext = shifted(yup, "gy", 1), shifted(ydown, "gy", -1)
+    (xup,) = call(pack_up_body, (links,), (288,))
+    xprev = shifted(xup, "gx", 1)
     cup, cdown = call(pack_corners_body, (ynext, yprev), (48, 48))
     cprev, cnext = shifted(cup, "gx", 1), shifted(cdown, "gx", -1)
     kept = call(links_local_body, (links,), buffer_rows(NC) + [1728, 864, 1152])
-    *kept, inner = call(links_y_body, (ynext, yprev, incoming), (1152,), kept)
-    r = call(links_x_body, (xnext, cnext, xprev, cprev, inner), (512, 1152, 256, 192), kept)
-    bufs, omega, (lam, acc, yup, ydown) = r[:7], r[7], r[10:]
+    *kept, inner, moved = call(links_y_body, (ynext, yprev, incoming), (1152, 1152), kept)
+    kept = call(links_next_body, (xnext,), (), kept)
+    r = call(links_x_body, (cnext, xprev, cprev, inner, moved), (512, 1152, 256, 192, 432), kept)
+    bufs, omega, (lam, acc, yup, ydown, ready) = r[:7], r[7], r[10:]
     yprev, ynext = shifted(yup, "gy", 1), shifted(ydown, "gy", -1)
-    kept = call(lambda_local_body, (*bufs, omega, lam), buffer_rows(NA) + [1152], (acc,))
-    xup, xdown = call(pack_lambda_x_body, (lam, ynext, yprev, kept[-1]), (288, 224))
-    xprev, xnext = shifted(xup, "gx", 1), shifted(xdown, "gx", -1)
-    kept = call(lambda_y_body, (*bufs, omega, ynext, yprev), (), kept)
-    out = call(lambda_x_body, (*bufs, omega, xnext, xprev), (1152,), kept, first=1)[0]
+    acc, *lams, sums = call(lambda_local_body, (*bufs, omega, lam), buffer_rows(NA) + [1152], (acc,))
+    (xdown,) = call(pack_lambda_down_body, (lam, yprev, sums), (224,))
+    xnext = shifted(xdown, "gx", -1)
+    *lams, xup = call(lambda_up_body, (ynext, yprev, bufs[O]), (192,), lams)
+    xprev = shifted(xup, "gx", 1)
+    acc, sums = call(lambda_y_body, (*bufs, omega, *lams), (), (acc, sums))
+    out = call(lambda_x_body, (*bufs, omega, ready, xnext, xprev), (1152,), (acc, *lams, sums), first=1)[0]
     return out.reshape(shape)
 
 

time: 44.6 us -> 45.5 us (1.020)
  waiting for transfers between devices: 7.58 us -> 9.4 us
  starting transfers between devices: 25 us -> 23.6 us
    ppermute x10, waiting for transfers between devices: 7.58 us -> 9.4 us  [shifted(): lax.ppermute(shard, axis, [(i, (i + by) % length) for i in range(length)])]
    ppermute x10, starting transfers between devices: 25 us -> 23.6 us  [shifted(): lax.ppermute(shard, axis, [(i, (i + by) % length) for i in range(length)])]
    pallas_call x9 -> x12, Pallas kernels: 10.6 us -> 11 us  [call(): pl.pallas_call(body, out_shape=tuple(shapes), in_specs=[pl.BlockSpec(memo...]
  transfers between devices with their start and end apart: 10 -> 10, of which waited for: 7 -> 3; matrix products, arithmetic and copies ran while one was open for 0% -> 0% of each run, Pallas kernels for 13% -> 16%
where the time goes in v5:
time: 45.5 us; the launch traced here: 45.3 us
  starting transfers between devices  23.6 us (52%)
  Pallas kernels  11 us (24%)
  waiting for transfers between devices  9.4 us (21%)
  local copies, waits for them, and re-layouts  1.17 us (3%)
    ppermute x10, starting transfers between devices, shifted(): lax.ppermute(shard, axis, [(i, (i + by) % length) for i in range(length)])  23.6 us
    pallas_call x12, Pallas kernels, call(): pl.pallas_call(body, out_shape=tuple(shapes), in_specs=[pl.BlockSpec(memo...  11 us
    ppermute x10, waiting for transfers between devices, shifted(): lax.ppermute(shard, axis, [(i, (i + by) % length) for i in range(length)])  9.4 us
    unnamed x6, local copies, waits for them, and re-layouts  1.17 us
  transfers between devices with their start and end apart: 10, of which 3 were waited for; matrix products, arithmetic and copies ran while one was open for 0% of the time, Pallas kernels for 16%

profile of v5, /device:TPU:0, one launch (start us, length us, event | category | flops | bytes accessed | tf_op | source)
XLA Modules:
  0.0 45.3 jit_solution(6166013538896348843)
XLA Ops:
  0.0 1.2 %copy-done = f32[4,3,3,2,2,2,6,128]{7,5,6,4,3,2,1,0:T(2,128)S(1)} copy-done((f32[4,3,3,2,2,2,6,128]{7,5,6,4,3,2,1,0:T(2,128)S(1)}, f32[4,3,3,2,2,2,6,128]{7,5,6,4,3,2,1,0:T(2,128)}, u32[]{:S(2)}) %copy-start) | copy-done | bytes 884760
  1.2 0.1 shard_map.28
  1.3 0.1 collective-permute-start.1
  1.4 4.0 %collective-permute-start = (f32[312,128]{1,0:T(8,128)S(1)}, f32[312,128]{1,0:T(8,128)S(1)}, u32[]{:S(2)}, u32[]{:S(2)}) collective-permute-start(f32[312,128]{1,0:T(8,128)S(1)} %get-tuple-element.75), channel_id=1, source_target_pairs={{0,15},{1,0},{2,1},{3,2},{4,3},{5,4},{6,5},{7,6},{8,7},{9,8},{10,9... | collective-permute-start | bytes 479240 | tf_op jit(solution)/shard_map/ppermute | solution.py:742
  5.3 6.0 %collective-permute-start.5 = (f32[312,128]{1,0:T(8,128)S(1)}, f32[312,128]{1,0:T(8,128)S(1)}, u32[]{:S(2)}, u32[]{:S(2)}) collective-permute-start(f32[312,128]{1,0:T(8,128)S(1)} %get-tuple-element.91), channel_id=1, source_target_pairs={{0,112},{16,0},{32,16},{48,32},{64,48},{80,64},{96,80},{112,96},{1... | collective-permute-start | bytes 479240 | tf_op jit(solution)/shard_map/ppermute | solution.py:742
  11.4 0.1 shard_map.30
  11.5 0.1 collective-permute-start.3
  11.6 0.0 collective-permute-done.1.yprev.refs_1_
  11.6 5.7 %collective-permute-start.2 = (f32[48,128]{1,0:T(8,128)S(1)}, f32[48,128]{1,0:T(8,128)S(1)}, u32[]{:S(2)}, u32[]{:S(2)}) collective-permute-start(f32[48,128]{1,0:T(8,128)S(1)} %get-tuple-element.77), channel_id=1, source_target_pairs={{0,112},{16,0},{32,16},{48,32},{64,48},{80,64},{96,80},{112,96},{1... | collective-permute-start | bytes 73736 | tf_op jit(solution)/shard_map/ppermute | solution.py:742
  17.3 1.3 %shard_map.31 = (f32[3456,128]{1,0:T(8,128)S(1)}, f32[3456,128]{1,0:T(8,128)S(1)}, f32[3456,128]{1,0:T(8,128)S(1)}, f32[3456,128]{1,0:T(8,128)S(1)}, f32[3456,12...) custom-call(f32[1728,128]{1,0:T(8,128)S(1)} %bitcast.7), custom_call_target="tpu_custom_call" | custom-call | tf_op jit(solution)/shard_map/pallas_call | solution.py:729
  18.6 1.5 %shard_map.32 = (f32[3456,128]{1,0:T(8,128)S(1)}, f32[3456,128]{1,0:T(8,128)S(1)}, f32[3456,128]{1,0:T(8,128)S(1)}, f32[3456,128]{1,0:T(8,128)S(1)}, f32[3456,12...) custom-call(f32[312,128]{1,0:T(8,128)S(1)} %collective-permute-done., ...), custom_call_target="tpu_custom_call", output_to_operand_aliasing={{0}: (3, {}), {1}: (4, {}), {2}: (5, {}), {3}: (6, {}), {4}... | custom-call | tf_op jit(solution)/shard_map/pallas_call | solution.py:729
  20.1 0.4 shard_map.33
  20.5 4.2 %collective-permute-done.4.refs_2_ = f32[48,128]{1,0:T(8,128)S(1)} collective-permute-done((f32[48,128]{1,0:T(8,128)S(1)}, f32[48,128]{1,0:T(8,128)S(1)}, u32[]{:S(2)}, u32[]{:S(2)}) %collective-permute-start.4) | collective-permute-done | bytes 24608 | tf_op jit(solution)/shard_map/ppermute | solution.py:742
  24.7 1.6 %shard_map.34 = (f32[3456,128]{1,0:T(8,128)S(1)}, f32[3456,128]{1,0:T(8,128)S(1)}, f32[3456,128]{1,0:T(8,128)S(1)}, f32[3456,128]{1,0:T(8,128)S(1)}, f32[3456,12...) custom-call(f32[48,128]{1,0:T(8,128)S(1)} %collective-permute-done.2, ...), custom_call_target="tpu_custom_call", output_to_operand_aliasing={{0}: (5, {}), {1}: (6, {}), {2}: (7, {}), {3}: (8, {}), {4}... | custom-call | tf_op jit(solution)/shard_map/pallas_call | solution.py:729
  26.4 0.1 collective-permute-start.6
  26.4 3.8 %collective-permute-start.8 = (f32[192,128]{1,0:T(8,128)S(1)}, f32[192,128]{1,0:T(8,128)S(1)}, u32[]{:S(2)}, u32[]{:S(2)}) collective-permute-start(f32[192,128]{1,0:T(8,128)S(1)} %get-tuple-element.125), channel_id=1, source_target_pairs={{0,15},{1,0},{2,1},{3,2},{4,3},{5,4},{6,5},{7,6},{8,7},{9,8},{10,9... | collective-permute-start | bytes 294920 | tf_op jit(solution)/shard_map/ppermute | solution.py:742
  30.3 1.9 %shard_map.35 = (f32[1152,128]{1,0:T(8,128)S(1)}, f32[1536,128]{1,0:T(8,128)S(1)}, f32[1536,128]{1,0:T(8,128)S(1)}, f32[1536,128]{1,0:T(8,128)S(1)}, f32[1536,12...) custom-call(f32[3456,128]{1,0:T(8,128)S(1)} %get-tuple-element.112.r, ...), custom_call_target="tpu_custom_call", output_to_operand_aliasing={{0}: (9, {})} | custom-call | tf_op jit(solution)/shard_map/pallas_call | solution.py:729
  32.2 0.8 %collective-permute-done.6.yprev.refs_1_ = f32[256,128]{1,0:T(8,128)S(1)} collective-permute-done((f32[256,128]{1,0:T(8,128)S(1)}, f32[256,128]{1,0:T(8,128)S(1)}, u32[]{:S(2)}, u32[]{:S(2)}) %collective-permute-start.6) | collective-permute-done | bytes 131104 | tf_op jit(solution)/shard_map/ppermute | solution.py:742
  32.9 1.6 %collective-permute-start.7 = (f32[224,128]{1,0:T(8,128)S(1)}, f32[224,128]{1,0:T(8,128)S(1)}, u32[]{:S(2)}, u32[]{:S(2)}) collective-permute-start(f32[224,128]{1,0:T(8,128)S(1)} %shard_map.36), channel_id=1, source_target_pairs={{0,112},{16,0},{32,16},{48,32},{64,48},{80,64},{96,80},{112,96},{1... | collective-permute-start | bytes 344072 | tf_op jit(solution)/shard_map/ppermute | solution.py:742
  34.6 0.2 shard_map.37
  34.8 2.2 %collective-permute-start.9 = (f32[192,128]{1,0:T(8,128)S(1)}, f32[192,128]{1,0:T(8,128)S(1)}, u32[]{:S(2)}, u32[]{:S(2)}) collective-permute-start(f32[192,128]{1,0:T(8,128)S(1)} %get-tuple-element.133), channel_id=1, source_target_pairs={{0,16},{16,32},{32,48},{48,64},{64,80},{80,96},{96,112},{112,0},{1... | collective-permute-start | bytes 294920 | tf_op jit(solution)/shard_map/ppermute | solution.py:742
  37.0 1.9 %shard_map.38 = (f32[1152,128]{1,0:T(8,128)S(1)}, f32[1152,128]{1,0:T(8,128)S(1)}) custom-call(f32[3456,128]{1,0:T(8,128)S(1)} %get-tuple-element.112.refs_0_.refs_2_, f32[3456,128]{1,0:T(8,128)S(1)} %get-tuple-element.113.refs_1_, f32[3456,128]{1,0:T(8,128)S(1)} %get-tuple-element.114.refs_2_, ...), custom_call_target="tpu_custom_call", output_to_operand_aliasing={{0}: (15, {}), {1}: (16, {})} | custom-call | tf_op jit(solution)/shard_map/pallas_call | solution.py:729
  38.9 4.4 %collective-permute-done.9.refs_10_ = f32[192,128]{1,0:T(8,128)S(1)} collective-permute-done((f32[192,128]{1,0:T(8,128)S(1)}, f32[192,128]{1,0:T(8,128)S(1)}, u32[]{:S(2)}, u32[]{:S(2)}) %collective-permute-start.9) | collective-permute-done | bytes 98336 | tf_op jit(solution)/shard_map/ppermute | solution.py:742
  43.3 2.0 %shard_map.39 = (f32[1152,128]{1,0:T(8,128)}, f32[1152,128]{1,0:T(8,128)S(1)}, f32[1536,128]{1,0:T(8,128)S(1)}, f32[1536,128]{1,0:T(8,128)S(1)}, f32[1536,128]{1...) custom-call(f32[3456,128]{1,0:T(8,128)S(1)} %get-tuple-element.112.r, ...), custom_call_target="tpu_custom_call", output_to_operand_aliasing={{1}: (11, {}), {2}: (12, {}), {3}: (13, {}), {4}: (14, {}),... | custom-call | tf_op jit(solution)/shard_map/pallas_call | solution.py:729
  (14 shorter events, 0.0 us)
Async XLA Ops:
  0.0 1.2 %copy-start = (f32[4,3,3,2,2,2,6,128]{7,5,6,4,3,2,1,0:T(2,128)S(1)}, f32[4,3,3,2,2,2,6,128]{7,5,6,4,3,2,1,0:T(2,128)}, u32[]{:S(2)}) copy-start(f32[4,3,3,2,2,2,6,128]{7,5,6,4,3,2,1,0:T(2,128)} %param.2) | copy-start | bytes 2654212
  1.2 16.1 %copy-start.1 = (f32[4,3,3,2,2,2,6,128]{7,5,6,4,3,2,1,0:T(2,128)S(1)}, f32[4,3,3,2,2,2,6,128]{7,5,6,4,3,2,1,0:T(2,128)}, u32[]{:S(2)}) copy-start(f32[4,3,3,2,2,2,6,128]{7,5,6,4,3,2,1,0:T(2,128)} %param.2) | copy-start | bytes 2654212
  1.2 17.4 %copy-start.2 = (f32[4,3,3,2,2,2,4,128]{7,6,5,4,3,2,1,0:T(4,128)S(1)}, f32[4,3,3,2,2,2,4,128]{7,6,5,4,3,2,1,0:T(4,128)}, u32[]{:S(2)}) copy-start(f32[4,3,3,2,2,2,4,128]{7,6,5,4,3,2,1,0:T(4,128)} %param.3) | copy-start | bytes 1769476
  1.3 10.3 %collective-permute-start.1 = (f32[408,128]{1,0:T(8,128)S(1)}, f32[408,128]{1,0:T(8,128)S(1)}, u32[]{:S(2)}, u32[]{:S(2)}) collective-permute-start(f32[408,128]{1,0:T(8,128)S(1)} %get-tuple-element.76), channel_id=1, source_target_pairs={{0,1},{1,2},{2,3},{3,4},{4,5},{5,6},{6,7},{7,8},{8,9},{9,10},{10,1... | collective-permute-start | bytes 626696 | tf_op jit(solution)/shard_map/ppermute | solution.py:742
  1.4 10.2 %collective-permute-start = (f32[312,128]{1,0:T(8,128)S(1)}, f32[312,128]{1,0:T(8,128)S(1)}, u32[]{:S(2)}, u32[]{:S(2)}) collective-permute-start(f32[312,128]{1,0:T(8,128)S(1)} %get-tuple-element.75), channel_id=1, source_target_pairs={{0,15},{1,0},{2,1},{3,2},{4,3},{5,4},{6,5},{7,6},{8,7},{9,8},{10,9... | collective-permute-start | bytes 479240 | tf_op jit(solution)/shard_map/ppermute | solution.py:742
  5.3 14.8 %collective-permute-start.5 = (f32[312,128]{1,0:T(8,128)S(1)}, f32[312,128]{1,0:T(8,128)S(1)}, u32[]{:S(2)}, u32[]{:S(2)}) collective-permute-start(f32[312,128]{1,0:T(8,128)S(1)} %get-tuple-element.91), channel_id=1, source_target_pairs={{0,112},{16,0},{32,16},{48,32},{64,48},{80,64},{96,80},{112,96},{1... | collective-permute-start | bytes 479240 | tf_op jit(solution)/shard_map/ppermute | solution.py:742
  11.5 9.0 %collective-permute-start.3 = (f32[288,128]{1,0:T(8,128)S(1)}, f32[288,128]{1,0:T(8,128)S(1)}, u32[]{:S(2)}, u32[]{:S(2)}) collective-permute-start(f32[288,128]{1,0:T(8,128)S(1)} %shard_map.30), channel_id=1, source_target_pairs={{0,16},{16,32},{32,48},{48,64},{64,80},{80,96},{96,112},{112,0},{1... | collective-permute-start | bytes 442376 | tf_op jit(solution)/shard_map/ppermute | solution.py:742
  11.6 8.9 %collective-permute-start.2 = (f32[48,128]{1,0:T(8,128)S(1)}, f32[48,128]{1,0:T(8,128)S(1)}, u32[]{:S(2)}, u32[]{:S(2)}) collective-permute-start(f32[48,128]{1,0:T(8,128)S(1)} %get-tuple-element.77), channel_id=1, source_target_pairs={{0,112},{16,0},{32,16},{48,32},{64,48},{80,64},{96,80},{112,96},{1... | collective-permute-start | bytes 73736 | tf_op jit(solution)/shard_map/ppermute | solution.py:742
  17.3 7.4 %collective-permute-start.4 = (f32[48,128]{1,0:T(8,128)S(1)}, f32[48,128]{1,0:T(8,128)S(1)}, u32[]{:S(2)}, u32[]{:S(2)}) collective-permute-start(f32[48,128]{1,0:T(8,128)S(1)} %get-tuple-element.78), channel_id=1, source_target_pairs={{0,16},{16,32},{32,48},{48,64},{64,80},{80,96},{96,112},{112,0},{1... | collective-permute-start | bytes 73736 | tf_op jit(solution)/shard_map/ppermute | solution.py:742
  26.4 6.6 %collective-permute-start.6 = (f32[256,128]{1,0:T(8,128)S(1)}, f32[256,128]{1,0:T(8,128)S(1)}, u32[]{:S(2)}, u32[]{:S(2)}) collective-permute-start(f32[256,128]{1,0:T(8,128)S(1)} %get-tuple-element.122), channel_id=1, source_target_pairs={{0,1},{1,2},{2,3},{3,4},{4,5},{5,6},{6,7},{7,8},{8,9},{9,10},{10,1... | collective-permute-start | bytes 393224 | tf_op jit(solution)/shard_map/ppermute | solution.py:742
  26.4 8.1 %collective-permute-start.8 = (f32[192,128]{1,0:T(8,128)S(1)}, f32[192,128]{1,0:T(8,128)S(1)}, u32[]{:S(2)}, u32[]{:S(2)}) collective-permute-start(f32[192,128]{1,0:T(8,128)S(1)} %get-tuple-element.125), channel_id=1, source_target_pairs={{0,15},{1,0},{2,1},{3,2},{4,3},{5,4},{6,5},{7,6},{8,7},{9,8},{10,9... | collective-permute-start | bytes 294920 | tf_op jit(solution)/shard_map/ppermute | solution.py:742
  32.9 10.3 %collective-permute-start.7 = (f32[224,128]{1,0:T(8,128)S(1)}, f32[224,128]{1,0:T(8,128)S(1)}, u32[]{:S(2)}, u32[]{:S(2)}) collective-permute-start(f32[224,128]{1,0:T(8,128)S(1)} %shard_map.36), channel_id=1, source_target_pairs={{0,112},{16,0},{32,16},{48,32},{64,48},{80,64},{96,80},{112,96},{1... | collective-permute-start | bytes 344072 | tf_op jit(solution)/shard_map/ppermute | solution.py:742
  34.8 8.5 %collective-permute-start.9 = (f32[192,128]{1,0:T(8,128)S(1)}, f32[192,128]{1,0:T(8,128)S(1)}, u32[]{:S(2)}, u32[]{:S(2)}) collective-permute-start(f32[192,128]{1,0:T(8,128)S(1)} %get-tuple-element.133), channel_id=1, source_target_pairs={{0,16},{16,32},{32,48},{48,64},{64,80},{80,96},{96,112},{112,0},{1... | collective-permute-start | bytes 294920 | tf_op jit(solution)/shard_map/ppermute | solution.py:742

commit v6 on v5

--- a/solution.py
+++ b/solution.py
@@ -145,7 +145,7 @@
                     down[pl.ds(((DOWN_Y.index(d) * n + q) * 2 + x) * 4, 4), :] = read_down(d, q, x)
 
 
-def pack_first_body(links, xdown, yup, ydown):
+def pack_first_body(links, xdown, yup, ydown, cdown, cup):
     def reader(row):
         return lambda d, q, x: links[pl.ds(((d * 18 + q) * 2 + x) * ROWS + row, 4, stride=2), :]
 
@@ -157,6 +157,8 @@
         for d in range(1, 4):
             xdown[pl.ds(((d - 1) * 12 + q) * 8, 8), :] = links[pl.ds((d * 18 + q) * 2 * ROWS + 2, 8), :]
         xdown[pl.ds(288 + q * 2, 2), :] = links[pl.ds((54 + q) * 2 * ROWS, 2), :]
+        cdown[pl.ds(q * 4, 4), :] = links[pl.ds((18 + q) * 2 * ROWS + 3, 4, stride=2), :]
+        cup[pl.ds(q * 4, 4), :] = links[pl.ds((q * 2 + 1) * ROWS + 2, 4, stride=2), :]
 
 
 def pack_up_body(links, up):
@@ -177,12 +179,6 @@
                 for ri in range(2):
                     out = jnp.where(first_rows(), value[ri], half[i][j][ri]) if m == 1 else value[ri]
                     up[pl.ds(((m - 1) * 12 + (i * 3 + j) * 2 + ri) * 8, 8), :] = out
-
-
-def pack_corners_body(ynext, yprev, up, down):
-    for q in range(12):
-        up[pl.ds(q * 4, 4), :] = ynext[pl.ds(q * 8 + 4, 4), :]
-        down[pl.ds(q * 4, 4), :] = yprev[pl.ds((12 + q) * 8, 4), :]
 
 
 def pack_lambda_down_body(lam, yprev, after, down):
@@ -742,17 +738,22 @@
     return lax.ppermute(shard, axis, [(i, (i + by) % length) for i in range(length)])
 
 
+def diagonal(shard, by_x, by_y):
+    nx, ny = lax.axis_size("gx"), lax.axis_size("gy")
+    pairs = [(i * ny + j, (i + by_x) % nx * ny + (j + by_y) % ny) for i in range(nx) for j in range(ny)]
+    return lax.ppermute(shard, ("gx", "gy"), pairs)
+
+
 def body(links, incoming):
     links = jnp.transpose(links, (0, 1, 2, 3, 4, 6, 5, 7)).reshape(144 * ROWS, 128)
     shape = incoming.shape
     incoming = incoming.reshape(1152, 128)
-    xdown, yup, ydown = call(pack_first_body, (links,), (312, 408, 312))
+    xdown, yup, ydown, cdown, cup = call(pack_first_body, (links,), (312, 408, 312, 48, 48))
     xnext = shifted(xdown, "gx", -1)
     yprev, ynext = shifted(yup, "gy", 1), shifted(ydown, "gy", -1)
     (xup,) = call(pack_up_body, (links,), (288,))
     xprev = shifted(xup, "gx", 1)
-    cup, cdown = call(pack_corners_body, (ynext, yprev), (48, 48))
-    cprev, cnext = shifted(cup, "gx", 1), shifted(cdown, "gx", -1)
+    cprev, cnext = diagonal(cup, 1, -1), diagonal(cdown, -1, 1)
     kept = call(links_local_body, (links,), buffer_rows(NC) + [1728, 864, 1152])
     *kept, inner, moved = call(links_y_body, (ynext, yprev, incoming), (1152, 1152), kept)
     kept = call(links_next_body, (xnext,), (), kept)

time: 45.5 us -> 46.6 us (1.024)
  the two profiles are of different devices: /device:TPU:0 before, /device:TPU:32 now
where the time goes in v6:
time: 46.6 us; the launch traced here: 46.4 us
  starting transfers between devices  25 us (54%)
  Pallas kernels  11 us (24%)
  waiting for transfers between devices  9.13 us (20%)
  local copies, waits for them, and re-layouts  1.17 us (3%)
    ppermute x8, starting transfers between devices, shifted(): lax.ppermute(shard, axis, [(i, (i + by) % length) for i in range(length)])  21.1 us
    pallas_call x11, Pallas kernels, call(): pl.pallas_call(body, out_shape=tuple(shapes), in_specs=[pl.BlockSpec(memo...  11 us
    ppermute x8, waiting for transfers between devices, shifted(): lax.ppermute(shard, axis, [(i, (i + by) % length) for i in range(length)])  6.88 us
    ppermute x2, starting transfers between devices, diagonal(): return lax.ppermute(shard, ('gx', 'gy'), pairs)  3.92 us
    ppermute x2, waiting for transfers between devices, diagonal(): return lax.ppermute(shard, ('gx', 'gy'), pairs)  2.25 us
    unnamed x4, local copies, waits for them, and re-layouts  1.17 us
  transfers between devices with their start and end apart: 10, of which 3 were waited for; matrix products, arithmetic and copies ran while one was open for 0% of the time, Pallas kernels for 16%

profile of v6, /device:TPU:32, one launch (start us, length us, event | category | flops | bytes accessed | tf_op | source)
XLA Modules:
  0.0 46.4 jit_solution(3403063516881082575)
XLA Ops:
  0.0 1.2 %copy-done = f32[4,3,3,2,2,2,6,128]{7,5,6,4,3,2,1,0:T(2,128)S(1)} copy-done((f32[4,3,3,2,2,2,6,128]{7,5,6,4,3,2,1,0:T(2,128)S(1)}, f32[4,3,3,2,2,2,6,128]{7,5,6,4,3,2,1,0:T(2,128)}, u32[]{:S(2)}) %copy-start) | copy-done | bytes 884760
  1.2 0.1 shard_map.28
  1.3 0.1 collective-permute-start.4
  1.4 3.8 %collective-permute-start.3 = (f32[312,128]{1,0:T(8,128)S(1)}, f32[312,128]{1,0:T(8,128)S(1)}, u32[]{:S(2)}, u32[]{:S(2)}) collective-permute-start(f32[312,128]{1,0:T(8,128)S(1)} %get-tuple-element.77), channel_id=1, source_target_pairs={{0,15},{1,0},{2,1},{3,2},{4,3},{5,4},{6,5},{7,6},{8,7},{9,8},{10,9... | collective-permute-start | bytes 479240 | tf_op jit(solution)/shard_map/ppermute | solution.py:738
  5.2 5.2 %collective-permute-start.5 = (f32[312,128]{1,0:T(8,128)S(1)}, f32[312,128]{1,0:T(8,128)S(1)}, u32[]{:S(2)}, u32[]{:S(2)}) collective-permute-start(f32[312,128]{1,0:T(8,128)S(1)} %get-tuple-element.91), channel_id=1, source_target_pairs={{0,112},{16,0},{32,16},{48,32},{64,48},{80,64},{96,80},{112,96},{1... | collective-permute-start | bytes 479240 | tf_op jit(solution)/shard_map/ppermute | solution.py:738
  10.4 0.1 shard_map.29
  10.5 0.1 collective-permute-start.1
  10.6 2.5 %collective-permute-start = (f32[48,128]{1,0:T(8,128)S(1)}, f32[48,128]{1,0:T(8,128)S(1)}, u32[]{:S(2)}, u32[]{:S(2)}) collective-permute-start(f32[48,128]{1,0:T(8,128)S(1)} %get-tuple-element.75), channel_id=1, source_target_pairs={{0,113},{1,114},{2,115},{3,116},{4,117},{5,118},{6,119},{7,120},{8... | collective-permute-start | bytes 73736 | tf_op jit(solution)/shard_map/ppermute | solution.py:744
  13.1 1.4 %collective-permute-start.2 = (f32[48,128]{1,0:T(8,128)S(1)}, f32[48,128]{1,0:T(8,128)S(1)}, u32[]{:S(2)}, u32[]{:S(2)}) collective-permute-start(f32[48,128]{1,0:T(8,128)S(1)} %get-tuple-element.76), channel_id=1, source_target_pairs={{0,31},{1,16},{2,17},{3,18},{4,19},{5,20},{6,21},{7,22},{8,23},{9,... | collective-permute-start | bytes 73736 | tf_op jit(solution)/shard_map/ppermute | solution.py:744
  14.5 1.3 %shard_map.30 = (f32[3456,128]{1,0:T(8,128)S(1)}, f32[3456,128]{1,0:T(8,128)S(1)}, f32[3456,128]{1,0:T(8,128)S(1)}, f32[3456,128]{1,0:T(8,128)S(1)}, f32[3456,12...) custom-call(f32[1728,128]{1,0:T(8,128)S(1)} %bitcast.7), custom_call_target="tpu_custom_call" | custom-call | tf_op jit(solution)/shard_map/pallas_call | solution.py:725
  15.9 1.4 %shard_map.31 = (f32[3456,128]{1,0:T(8,128)S(1)}, f32[3456,128]{1,0:T(8,128)S(1)}, f32[3456,128]{1,0:T(8,128)S(1)}, f32[3456,128]{1,0:T(8,128)S(1)}, f32[3456,12...) custom-call(f32[312,128]{1,0:T(8,128)S(1)} %collective-permute-done., ...), custom_call_target="tpu_custom_call", output_to_operand_aliasing={{0}: (3, {}), {1}: (4, {}), {2}: (5, {}), {3}: (6, {}), {4}... | custom-call | tf_op jit(solution)/shard_map/pallas_call | solution.py:725
  17.3 0.4 shard_map.32
  17.7 2.3 %collective-permute-done.2.refs_2_ = f32[48,128]{1,0:T(8,128)S(1)} collective-permute-done((f32[48,128]{1,0:T(8,128)S(1)}, f32[48,128]{1,0:T(8,128)S(1)}, u32[]{:S(2)}, u32[]{:S(2)}) %collective-permute-start.2) | collective-permute-done | bytes 24608 | tf_op jit(solution)/shard_map/ppermute | solution.py:744
  20.0 1.6 %shard_map.33 = (f32[3456,128]{1,0:T(8,128)S(1)}, f32[3456,128]{1,0:T(8,128)S(1)}, f32[3456,128]{1,0:T(8,128)S(1)}, f32[3456,128]{1,0:T(8,128)S(1)}, f32[3456,12...) custom-call(f32[48,128]{1,0:T(8,128)S(1)} %collective-permute-done.r, ...), custom_call_target="tpu_custom_call", output_to_operand_aliasing={{0}: (5, {}), {1}: (6, {}), {2}: (7, {}), {3}: (8, {}), {4}... | custom-call | tf_op jit(solution)/shard_map/pallas_call | solution.py:725
  21.6 3.1 %collective-permute-start.6 = (f32[256,128]{1,0:T(8,128)S(1)}, f32[256,128]{1,0:T(8,128)S(1)}, u32[]{:S(2)}, u32[]{:S(2)}) collective-permute-start(f32[256,128]{1,0:T(8,128)S(1)} %get-tuple-element.122), channel_id=1, source_target_pairs={{0,1},{1,2},{2,3},{3,4},{4,5},{5,6},{6,7},{7,8},{8,9},{9,10},{10,1... | collective-permute-start | bytes 393224 | tf_op jit(solution)/shard_map/ppermute | solution.py:738
  24.7 5.0 %collective-permute-start.8 = (f32[192,128]{1,0:T(8,128)S(1)}, f32[192,128]{1,0:T(8,128)S(1)}, u32[]{:S(2)}, u32[]{:S(2)}) collective-permute-start(f32[192,128]{1,0:T(8,128)S(1)} %get-tuple-element.125), channel_id=1, source_target_pairs={{0,15},{1,0},{2,1},{3,2},{4,3},{5,4},{6,5},{7,6},{8,7},{9,8},{10,9... | collective-permute-start | bytes 294920 | tf_op jit(solution)/shard_map/ppermute | solution.py:738
  29.7 1.9 %shard_map.34 = (f32[1152,128]{1,0:T(8,128)S(1)}, f32[1536,128]{1,0:T(8,128)S(1)}, f32[1536,128]{1,0:T(8,128)S(1)}, f32[1536,128]{1,0:T(8,128)S(1)}, f32[1536,12...) custom-call(f32[3456,128]{1,0:T(8,128)S(1)} %get-tuple-element.112.r, ...), custom_call_target="tpu_custom_call", output_to_operand_aliasing={{0}: (9, {})} | custom-call | tf_op jit(solution)/shard_map/pallas_call | solution.py:725
  31.6 0.7 %collective-permute-done.6.yprev.refs_1_ = f32[256,128]{1,0:T(8,128)S(1)} collective-permute-done((f32[256,128]{1,0:T(8,128)S(1)}, f32[256,128]{1,0:T(8,128)S(1)}, u32[]{:S(2)}, u32[]{:S(2)}) %collective-permute-start.6) | collective-permute-done | bytes 131104 | tf_op jit(solution)/shard_map/ppermute | solution.py:738
  32.3 3.4 %collective-permute-start.7 = (f32[224,128]{1,0:T(8,128)S(1)}, f32[224,128]{1,0:T(8,128)S(1)}, u32[]{:S(2)}, u32[]{:S(2)}) collective-permute-start(f32[224,128]{1,0:T(8,128)S(1)} %shard_map.35), channel_id=1, source_target_pairs={{0,112},{16,0},{32,16},{48,32},{64,48},{80,64},{96,80},{112,96},{1... | collective-permute-start | bytes 344072 | tf_op jit(solution)/shard_map/ppermute | solution.py:738
  35.7 0.2 shard_map.36
  35.9 0.4 collective-permute-start.9
  36.4 1.9 %shard_map.37 = (f32[1152,128]{1,0:T(8,128)S(1)}, f32[1152,128]{1,0:T(8,128)S(1)}) custom-call(f32[3456,128]{1,0:T(8,128)S(1)} %get-tuple-element.112.refs_0_.refs_2_, f32[3456,128]{1,0:T(8,128)S(1)} %get-tuple-element.113.refs_1_, f32[3456,128]{1,0:T(8,128)S(1)} %get-tuple-element.114.refs_2_, ...), custom_call_target="tpu_custom_call", output_to_operand_aliasing={{0}: (15, {}), {1}: (16, {})} | custom-call | tf_op jit(solution)/shard_map/pallas_call | solution.py:725
  38.2 6.2 %collective-permute-done.9.refs_10_ = f32[192,128]{1,0:T(8,128)S(1)} collective-permute-done((f32[192,128]{1,0:T(8,128)S(1)}, f32[192,128]{1,0:T(8,128)S(1)}, u32[]{:S(2)}, u32[]{:S(2)}) %collective-permute-start.9) | collective-permute-done | bytes 98336 | tf_op jit(solution)/shard_map/ppermute | solution.py:738
  44.4 2.0 %shard_map.38 = (f32[1152,128]{1,0:T(8,128)}, f32[1152,128]{1,0:T(8,128)S(1)}, f32[1536,128]{1,0:T(8,128)S(1)}, f32[1536,128]{1,0:T(8,128)S(1)}, f32[1536,128]{1...) custom-call(f32[3456,128]{1,0:T(8,128)S(1)} %get-tuple-element.112.r, ...), custom_call_target="tpu_custom_call", output_to_operand_aliasing={{1}: (11, {}), {2}: (12, {}), {3}: (13, {}), {4}: (14, {}),... | custom-call | tf_op jit(solution)/shard_map/pallas_call | solution.py:725
  (11 shorter events, 0.0 us)
Async XLA Ops:
  0.0 1.2 %copy-start = (f32[4,3,3,2,2,2,6,128]{7,5,6,4,3,2,1,0:T(2,128)S(1)}, f32[4,3,3,2,2,2,6,128]{7,5,6,4,3,2,1,0:T(2,128)}, u32[]{:S(2)}) copy-start(f32[4,3,3,2,2,2,6,128]{7,5,6,4,3,2,1,0:T(2,128)} %param.2) | copy-start | bytes 2654212
  1.2 14.7 %copy-start.1 = (f32[4,3,3,2,2,2,4,128]{7,6,5,4,3,2,1,0:T(4,128)S(1)}, f32[4,3,3,2,2,2,4,128]{7,6,5,4,3,2,1,0:T(4,128)}, u32[]{:S(2)}) copy-start(f32[4,3,3,2,2,2,4,128]{7,6,5,4,3,2,1,0:T(4,128)} %param.3) | copy-start | bytes 1769476
  1.3 14.5 %collective-permute-start.4 = (f32[408,128]{1,0:T(8,128)S(1)}, f32[408,128]{1,0:T(8,128)S(1)}, u32[]{:S(2)}, u32[]{:S(2)}) collective-permute-start(f32[408,128]{1,0:T(8,128)S(1)} %get-tuple-element.78), channel_id=1, source_target_pairs={{0,1},{1,2},{2,3},{3,4},{4,5},{5,6},{6,7},{7,8},{8,9},{9,10},{10,1... | collective-permute-start | bytes 626696 | tf_op jit(solution)/shard_map/ppermute | solution.py:738
  1.4 11.7 %collective-permute-start.3 = (f32[312,128]{1,0:T(8,128)S(1)}, f32[312,128]{1,0:T(8,128)S(1)}, u32[]{:S(2)}, u32[]{:S(2)}) collective-permute-start(f32[312,128]{1,0:T(8,128)S(1)} %get-tuple-element.77), channel_id=1, source_target_pairs={{0,15},{1,0},{2,1},{3,2},{4,3},{5,4},{6,5},{7,6},{8,7},{9,8},{10,9... | collective-permute-start | bytes 479240 | tf_op jit(solution)/shard_map/ppermute | solution.py:738
  5.2 12.1 %collective-permute-start.5 = (f32[312,128]{1,0:T(8,128)S(1)}, f32[312,128]{1,0:T(8,128)S(1)}, u32[]{:S(2)}, u32[]{:S(2)}) collective-permute-start(f32[312,128]{1,0:T(8,128)S(1)} %get-tuple-element.91), channel_id=1, source_target_pairs={{0,112},{16,0},{32,16},{48,32},{64,48},{80,64},{96,80},{112,96},{1... | collective-permute-start | bytes 479240 | tf_op jit(solution)/shard_map/ppermute | solution.py:738
  10.5 9.5 %collective-permute-start.1 = (f32[288,128]{1,0:T(8,128)S(1)}, f32[288,128]{1,0:T(8,128)S(1)}, u32[]{:S(2)}, u32[]{:S(2)}) collective-permute-start(f32[288,128]{1,0:T(8,128)S(1)} %shard_map.29), channel_id=1, source_target_pairs={{0,16},{16,32},{32,48},{48,64},{64,80},{80,96},{96,112},{112,0},{1... | collective-permute-start | bytes 442376 | tf_op jit(solution)/shard_map/ppermute | solution.py:738
  10.6 7.1 %collective-permute-start = (f32[48,128]{1,0:T(8,128)S(1)}, f32[48,128]{1,0:T(8,128)S(1)}, u32[]{:S(2)}, u32[]{:S(2)}) collective-permute-start(f32[48,128]{1,0:T(8,128)S(1)} %get-tuple-element.75), channel_id=1, source_target_pairs={{0,113},{1,114},{2,115},{3,116},{4,117},{5,118},{6,119},{7,120},{8... | collective-permute-start | bytes 73736 | tf_op jit(solution)/shard_map/ppermute | solution.py:744
  13.1 6.9 %collective-permute-start.2 = (f32[48,128]{1,0:T(8,128)S(1)}, f32[48,128]{1,0:T(8,128)S(1)}, u32[]{:S(2)}, u32[]{:S(2)}) collective-permute-start(f32[48,128]{1,0:T(8,128)S(1)} %get-tuple-element.76), channel_id=1, source_target_pairs={{0,31},{1,16},{2,17},{3,18},{4,19},{5,20},{6,21},{7,22},{8,23},{9,... | collective-permute-start | bytes 73736 | tf_op jit(solution)/shard_map/ppermute | solution.py:744
  21.6 10.7 %collective-permute-start.6 = (f32[256,128]{1,0:T(8,128)S(1)}, f32[256,128]{1,0:T(8,128)S(1)}, u32[]{:S(2)}, u32[]{:S(2)}) collective-permute-start(f32[256,128]{1,0:T(8,128)S(1)} %get-tuple-element.122), channel_id=1, source_target_pairs={{0,1},{1,2},{2,3},{3,4},{4,5},{5,6},{6,7},{7,8},{8,9},{9,10},{10,1... | collective-permute-start | bytes 393224 | tf_op jit(solution)/shard_map/ppermute | solution.py:738
  24.7 11.0 %collective-permute-start.8 = (f32[192,128]{1,0:T(8,128)S(1)}, f32[192,128]{1,0:T(8,128)S(1)}, u32[]{:S(2)}, u32[]{:S(2)}) collective-permute-start(f32[192,128]{1,0:T(8,128)S(1)} %get-tuple-element.125), channel_id=1, source_target_pairs={{0,15},{1,0},{2,1},{3,2},{4,3},{5,4},{6,5},{7,6},{8,7},{9,8},{10,9... | collective-permute-start | bytes 294920 | tf_op jit(solution)/shard_map/ppermute | solution.py:738
  32.3 12.1 %collective-permute-start.7 = (f32[224,128]{1,0:T(8,128)S(1)}, f32[224,128]{1,0:T(8,128)S(1)}, u32[]{:S(2)}, u32[]{:S(2)}) collective-permute-start(f32[224,128]{1,0:T(8,128)S(1)} %shard_map.35), channel_id=1, source_target_pairs={{0,112},{16,0},{32,16},{48,32},{64,48},{80,64},{96,80},{112,96},{1... | collective-permute-start | bytes 344072 | tf_op jit(solution)/shard_map/ppermute | solution.py:738
  35.9 8.5 %collective-permute-start.9 = (f32[192,128]{1,0:T(8,128)S(1)}, f32[192,128]{1,0:T(8,128)S(1)}, u32[]{:S(2)}, u32[]{:S(2)}) collective-permute-start(f32[192,128]{1,0:T(8,128)S(1)} %get-tuple-element.133), channel_id=1, source_target_pairs={{0,16},{16,32},{32,48},{48,64},{64,80},{80,96},{96,112},{112,0},{1... | collective-permute-start | bytes 294920 | tf_op jit(solution)/shard_map/ppermute | solution.py:738

commit v7 on v4

--- a/solution.py
+++ b/solution.py
@@ -263,7 +263,7 @@
     fill_mixed(bufs, NC)
 
 
-def fill_column(source, slots, corner, bufs, xe, edge, corner_to):
+def fill_column(source, slots, bufs, xe, edge):
     for slot, d in enumerate(slots):
         m = two_rows(lambda q: source[pl.ds((slot * 12 + q) * 8, 8), :])
 
@@ -278,22 +278,25 @@
         bufs[O][pl.ds(place(d * NC + q, xe) + row, 2), :] = v
 
     put(write_edge, m)
-    buf, corner_dir, off = corner_to
+
+
+def fill_corner(corner, buf, d, xe, off, bufs):
     m = two_rows(lambda q: corner[pl.ds(q * 4, 4), :])
 
     def write_corner(q, v):
-        bufs[buf][pl.ds(place(corner_dir * NC + q, xe) + off, 4, stride=2), :] = v
+        bufs[buf][pl.ds(place(d * NC + q, xe) + off, 4, stride=2), :] = v
 
     put(write_corner, m)
 
 
-def fill_links_next(xnext, corner, bufs):
-    fill_column(xnext, (1, 2, 3), corner, bufs, 3, (3, 0), (YM, 1, 2))
+def fill_links_next(xnext, bufs):
+    fill_column(xnext, (1, 2, 3), bufs, 3, (3, 0))
     fill_high(bufs, NC)
 
 
 def fill_links_prev(xprev, corner, bufs):
-    fill_column(xprev, (0, 1, 2, 3), corner, bufs, 0, (0, 10), (YP, 0, 3))
+    fill_column(xprev, (0, 1, 2, 3), bufs, 0, (0, 10))
+    fill_corner(corner, YP, 0, 0, 3, bufs)
     fill_low(bufs, NC)
 
 
@@ -374,7 +377,7 @@
     return unpack8([read(k) for k in range(NA)])
 
 
-def exponent_force(v, u, target, clow):
+def exponent_force(v, m, target, clow):
     a = v[:3]
     off = [(v[3 + 2 * k], v[4 + 2 * k]) for k in range(3)]
     norm = [r * r + s * s for r, s in off]
@@ -398,7 +401,6 @@
     p1i = dd * (1.0 / 24.0 + c * (1.0 / 360.0))
     p2r = 0.5 + c * (1.0 / 24.0 + c * (1.0 / 720.0))
     p2i = dd * (1.0 / 120.0)
-    m = mm(target, u, False, True)
     hd = [m[i][i][0] for i in range(3)]
     kd = [m[i][i][1] for i in range(3)]
     ho = [(0.5 * (m[i][j][0] + m[j][i][0]), 0.5 * (m[i][j][1] - m[j][i][1])) for i, j in UPPER]
@@ -481,7 +483,7 @@
         if x + offset[0] == -1:
             found = 3
         elif x + offset[0] == 2:
-            found = max(found, 2)
+            found = max(found, 3 if offset[1] else 2)
         elif offset[1]:
             found = max(found, 1)
     return found
@@ -539,8 +541,15 @@
             store_cells(low, m * 18, x, value)
 
 
-def finish_forward(xs, bufs, inner, loops, low, lam_out, direct):
-    for x in xs:
+def target_products(bufs, inner, moved):
+    for x in range(2):
+        for m in range(4):
+            target = load_cells(inner, m * 18, x)
+            store_cells(moved, m * 18, x, mm(target, link(bufs, m, step(), x), False, True))
+
+
+def finish_forward(bufs, inner, moved, loops, low, lam_out, direct):
+    for x in range(2):
         for m in range(4):
             u = link(bufs, m, step(), x)
             below = load_cells(low, m * 18, x)
@@ -554,7 +563,7 @@
             v = [(0.5 * smear_weight) * (v[k] - mean) for k in range(3)] + [
                 (0.5 * smear_weight) * v[k] for k in range(3, 9)
             ]
-            lam, force = exponent_force(v, u, load_cells(inner, m * 18, x), below)
+            lam, force = exponent_force(v, load_cells(moved, m * 18, x), load_cells(inner, m * 18, x), below)
             for k, v in enumerate(lam[:2] + lam[3:]):
                 lam_out[cells(m * NA, k, x), :] = v
             store_cells(direct, m * 18, x, force)
@@ -594,12 +603,16 @@
             store_cells(acc, m * 18, x, force)
 
 
+def add_loops(bufs, sums, acc, m, x):
+    f = load_cells(sums, m * 18, x)
+    store_cells(acc, m * 18, x, madd(mm(f, link(bufs, m, step(), x)), load_cells(acc, m * 18, x)))
+
+
 def finish_backward(bufs, sums, acc, out):
     for x in range(2):
         for m in range(4):
-            f = load_cells(sums, m * 18, x)
-            force = madd(mm(f, link(bufs, m, step(), x)), load_cells(acc, m * 18, x))
-            store_cells(acc, m * 18, x, force)
+            if x == 1:
+                add_loops(bufs, sums, acc, m, x)
             for k in range(18):
                 at = ((m * 18 + k) * 2 + x) * 8
                 out[pl.ds(at, 4), :] = acc[pl.ds(at, 4, stride=2), :]
@@ -615,21 +628,27 @@
 
 def links_y_body(*refs):
     ynext, yprev, incoming = refs[:3]
-    bufs, (omega, loops, low, inner) = refs[13:20], refs[20:]
+    bufs, (omega, loops, low, inner, moved) = refs[13:20], refs[20:]
     fill_links_y(ynext, yprev, bufs)
     take_incoming(incoming, inner)
     forward_items(1, bufs, omega, loops, low)
+    target_products(bufs, inner, moved)
+
+
+def links_next_body(*refs):
+    xnext = refs[0]
+    bufs, (omega, loops, low) = refs[11:18], refs[18:]
+    fill_links_next(xnext, bufs)
+    forward_items(2, bufs, omega, loops, low)
 
 
 def links_x_body(*refs):
-    xnext, cnext, xprev, cprev, inner = refs[:5]
+    cnext, xprev, cprev, inner, moved = refs[:5]
     bufs, (omega, loops, low, lam, direct, up, down) = refs[15:22], refs[22:]
-    fill_links_next(xnext, cnext, bufs)
-    forward_items(2, bufs, omega, loops, low)
-    finish_forward((1,), bufs, inner, loops, low, lam, direct)
+    fill_corner(cnext, YM, 1, 3, 2, bufs)
     fill_links_prev(xprev, cprev, bufs)
     forward_items(3, bufs, omega, loops, low)
-    finish_forward((0,), bufs, inner, loops, low, lam, direct)
+    finish_forward(bufs, inner, moved, loops, low, lam, direct)
 
     def reader(row):
         return lambda d, q, x: lam[pl.ds(((d * NA + q) * 2 + x) * 8 + row, 4, stride=2), :]
@@ -649,6 +668,8 @@
     acc, lams, sums = refs[19], refs[20:27], refs[27]
     fill_lambda_y(ynext, yprev, lams)
     backward_items(1, bufs, lams, omega, sums, acc)
+    for m in range(4):
+        add_loops(bufs, sums, acc, m, 0)
 
 
 def lambda_x_body(*refs):
@@ -697,8 +718,9 @@
     cup, cdown = call(pack_corners_body, (ynext, yprev), (48, 48))
     cprev, cnext = shifted(cup, "gx", 1), shifted(cdown, "gx", -1)
     kept = call(links_local_body, (links,), buffer_rows(NC) + [1728, 864, 1152])
-    *kept, inner = call(links_y_body, (ynext, yprev, incoming), (1152,), kept)
-    r = call(links_x_body, (xnext, cnext, xprev, cprev, inner), (512, 1152, 256, 192), kept)
+    *kept, inner, moved = call(links_y_body, (ynext, yprev, incoming), (1152, 1152), kept)
+    kept = call(links_next_body, (xnext,), (), kept)
+    r = call(links_x_body, (cnext, xprev, cprev, inner, moved), (512, 1152, 256, 192), kept)
     bufs, omega, (lam, acc, yup, ydown) = r[:7], r[7], r[10:]
     yprev, ynext = shifted(yup, "gy", 1), shifted(ydown, "gy", -1)
     kept = call(lambda_local_body, (*bufs, omega, lam), buffer_rows(NA) + [1152], (acc,))

time: 44.6 us -> 43.9 us (0.984)
  waiting for transfers between devices: 7.58 us -> 6.88 us
    ppermute x10, waiting for transfers between devices: 7.58 us -> 6.88 us  [shifted(): lax.ppermute(shard, axis, [(i, (i + by) % length) for i in range(length)])]
    pallas_call x9 -> x10, Pallas kernels: 10.6 us -> 10.6 us  [call(): pl.pallas_call(body, out_shape=tuple(shapes), in_specs=[pl.BlockSpec(memo...]
  transfers between devices with their start and end apart: 10 -> 10, of which waited for: 7 -> 6; matrix products, arithmetic and copies ran while one was open for 0% -> 0% of each run, Pallas kernels for 13% -> 15%
where the time goes in v7:
time: 43.9 us; the launch traced here: 43.7 us
  starting transfers between devices  25 us (57%)
  Pallas kernels  10.6 us (24%)
  waiting for transfers between devices  6.88 us (16%)
  local copies, waits for them, and re-layouts  1.17 us (3%)
    ppermute x10, starting transfers between devices, shifted(): lax.ppermute(shard, axis, [(i, (i + by) % length) for i in range(length)])  25 us
    pallas_call x10, Pallas kernels, call(): pl.pallas_call(body, out_shape=tuple(shapes), in_specs=[pl.BlockSpec(memo...  10.6 us
    ppermute x10, waiting for transfers between devices, shifted(): lax.ppermute(shard, axis, [(i, (i + by) % length) for i in range(length)])  6.88 us
    unnamed x6, local copies, waits for them, and re-layouts  1.17 us
  transfers between devices with their start and end apart: 10, of which 6 were waited for; matrix products, arithmetic and copies ran while one was open for 0% of the time, Pallas kernels for 15%

profile of v7, /device:TPU:0, one launch (start us, length us, event | category | flops | bytes accessed | tf_op | source)
XLA Modules:
  0.0 43.7 jit_solution(4613370334673972411)
XLA Ops:
  0.0 1.2 %copy-done = f32[4,3,3,2,2,2,6,128]{7,5,6,4,3,2,1,0:T(2,128)S(1)} copy-done((f32[4,3,3,2,2,2,6,128]{7,5,6,4,3,2,1,0:T(2,128)S(1)}, f32[4,3,3,2,2,2,6,128]{7,5,6,4,3,2,1,0:T(2,128)}, u32[]{:S(2)}) %copy-start) | copy-done | bytes 884760
  1.2 0.1 shard_map.28
  1.3 0.1 collective-permute-start.1
  1.4 4.0 %collective-permute-start.3 = (f32[408,128]{1,0:T(8,128)S(1)}, f32[408,128]{1,0:T(8,128)S(1)}, u32[]{:S(2)}, u32[]{:S(2)}) collective-permute-start(f32[408,128]{1,0:T(8,128)S(1)} %get-tuple-element.79), channel_id=1, source_target_pairs={{0,16},{16,32},{32,48},{48,64},{64,80},{80,96},{96,112},{112,0},{1... | collective-permute-start | bytes 626696 | tf_op jit(solution)/shard_map/ppermute | solution.py:708
  5.4 2.9 %collective-permute-start = (f32[312,128]{1,0:T(8,128)S(1)}, f32[312,128]{1,0:T(8,128)S(1)}, u32[]{:S(2)}, u32[]{:S(2)}) collective-permute-start(f32[312,128]{1,0:T(8,128)S(1)} %get-tuple-element.76), channel_id=1, source_target_pairs={{0,15},{1,0},{2,1},{3,2},{4,3},{5,4},{6,5},{7,6},{8,7},{9,8},{10,9... | collective-permute-start | bytes 479240 | tf_op jit(solution)/shard_map/ppermute | solution.py:708
  8.3 3.1 %collective-permute-start.5 = (f32[312,128]{1,0:T(8,128)S(1)}, f32[312,128]{1,0:T(8,128)S(1)}, u32[]{:S(2)}, u32[]{:S(2)}) collective-permute-start(f32[312,128]{1,0:T(8,128)S(1)} %get-tuple-element.93), channel_id=1, source_target_pairs={{0,112},{16,0},{32,16},{48,32},{64,48},{80,64},{96,80},{112,96},{1... | collective-permute-start | bytes 479240 | tf_op jit(solution)/shard_map/ppermute | solution.py:708
  11.4 5.3 %collective-permute-start.2 = (f32[48,128]{1,0:T(8,128)S(1)}, f32[48,128]{1,0:T(8,128)S(1)}, u32[]{:S(2)}, u32[]{:S(2)}) collective-permute-start(f32[48,128]{1,0:T(8,128)S(1)} %get-tuple-element.78), channel_id=1, source_target_pairs={{0,112},{16,0},{32,16},{48,32},{64,48},{80,64},{96,80},{112,96},{1... | collective-permute-start | bytes 73736 | tf_op jit(solution)/shard_map/ppermute | solution.py:708
  16.7 1.1 %shard_map.30 = (f32[3456,128]{1,0:T(8,128)S(1)}, f32[3456,128]{1,0:T(8,128)S(1)}, f32[3456,128]{1,0:T(8,128)S(1)}, f32[3456,128]{1,0:T(8,128)S(1)}, f32[3456,12...) custom-call(f32[1728,128]{1,0:T(8,128)S(1)} %bitcast.6), custom_call_target="tpu_custom_call" | custom-call | tf_op jit(solution)/shard_map/pallas_call | solution.py:695
  17.8 1.4 %shard_map.31 = (f32[3456,128]{1,0:T(8,128)S(1)}, f32[3456,128]{1,0:T(8,128)S(1)}, f32[3456,128]{1,0:T(8,128)S(1)}, f32[3456,128]{1,0:T(8,128)S(1)}, f32[3456,12...) custom-call(f32[312,128]{1,0:T(8,128)S(1)} %collective-permute-done., ...), custom_call_target="tpu_custom_call", output_to_operand_aliasing={{0}: (3, {}), {1}: (4, {}), {2}: (5, {}), {3}: (6, {}), {4}... | custom-call | tf_op jit(solution)/shard_map/pallas_call | solution.py:695
  19.3 0.1 collective-permute-done.5.refs_0_
  19.4 0.4 shard_map.32
  19.8 4.3 %collective-permute-done.4.refs_2_ = f32[48,128]{1,0:T(8,128)S(1)} collective-permute-done((f32[48,128]{1,0:T(8,128)S(1)}, f32[48,128]{1,0:T(8,128)S(1)}, u32[]{:S(2)}, u32[]{:S(2)}) %collective-permute-start.4) | collective-permute-done | bytes 24608 | tf_op jit(solution)/shard_map/ppermute | solution.py:708
  24.1 1.7 %shard_map.33 = (f32[3456,128]{1,0:T(8,128)S(1)}, f32[3456,128]{1,0:T(8,128)S(1)}, f32[3456,128]{1,0:T(8,128)S(1)}, f32[3456,128]{1,0:T(8,128)S(1)}, f32[3456,12...) custom-call(f32[48,128]{1,0:T(8,128)S(1)} %collective-permute-done.2, ...), custom_call_target="tpu_custom_call", output_to_operand_aliasing={{0}: (5, {}), {1}: (6, {}), {2}: (7, {}), {3}: (8, {}), {4}... | custom-call | tf_op jit(solution)/shard_map/pallas_call | solution.py:695
  25.8 0.1 collective-permute-start.7
  25.9 3.8 %collective-permute-start.6 = (f32[192,128]{1,0:T(8,128)S(1)}, f32[192,128]{1,0:T(8,128)S(1)}, u32[]{:S(2)}, u32[]{:S(2)}) collective-permute-start(f32[192,128]{1,0:T(8,128)S(1)} %get-tuple-element.123), channel_id=1, source_target_pairs={{0,15},{1,0},{2,1},{3,2},{4,3},{5,4},{6,5},{7,6},{8,7},{9,8},{10,9... | collective-permute-start | bytes 294920 | tf_op jit(solution)/shard_map/ppermute | solution.py:708
  29.7 1.7 %shard_map.34 = (f32[1152,128]{1,0:T(8,128)S(1)}, f32[1536,128]{1,0:T(8,128)S(1)}, f32[1536,128]{1,0:T(8,128)S(1)}, f32[1536,128]{1,0:T(8,128)S(1)}, f32[1536,12...) custom-call(f32[3456,128]{1,0:T(8,128)S(1)} %get-tuple-element.114.r, ...), custom_call_target="tpu_custom_call", output_to_operand_aliasing={{0}: (9, {})} | custom-call | tf_op jit(solution)/shard_map/pallas_call | solution.py:695
  31.4 0.5 %collective-permute-done.6.ynext.refs_8_ = f32[192,128]{1,0:T(8,128)S(1)} collective-permute-done((f32[192,128]{1,0:T(8,128)S(1)}, f32[192,128]{1,0:T(8,128)S(1)}, u32[]{:S(2)}, u32[]{:S(2)}) %collective-permute-start.6) | collective-permute-done | bytes 98336 | tf_op jit(solution)/shard_map/ppermute | solution.py:708
  32.0 0.8 %collective-permute-done.7.yprev.refs_9_ = f32[256,128]{1,0:T(8,128)S(1)} collective-permute-done((f32[256,128]{1,0:T(8,128)S(1)}, f32[256,128]{1,0:T(8,128)S(1)}, u32[]{:S(2)}, u32[]{:S(2)}) %collective-permute-start.7) | collective-permute-done | bytes 131104 | tf_op jit(solution)/shard_map/ppermute | solution.py:708
  32.8 0.1 collective-permute-start.9
  32.9 5.6 %collective-permute-start.8 = (f32[224,128]{1,0:T(8,128)S(1)}, f32[224,128]{1,0:T(8,128)S(1)}, u32[]{:S(2)}, u32[]{:S(2)}) collective-permute-start(f32[224,128]{1,0:T(8,128)S(1)} %get-tuple-element.127), channel_id=1, source_target_pairs={{0,112},{16,0},{32,16},{48,32},{64,48},{80,64},{96,80},{112,96},{1... | collective-permute-start | bytes 344072 | tf_op jit(solution)/shard_map/ppermute | solution.py:708
  38.5 2.0 %shard_map.36 = (f32[1152,128]{1,0:T(8,128)S(1)}, f32[1536,128]{1,0:T(8,128)S(1)}, f32[1536,128]{1,0:T(8,128)S(1)}, f32[1536,128]{1,0:T(8,128)S(1)}, f32[1536,12...) custom-call(f32[3456,128]{1,0:T(8,128)S(1)} %get-tuple-element.114.r, ...), custom_call_target="tpu_custom_call", output_to_operand_aliasing={{0}: (10, {}), {1}: (11, {}), {2}: (12, {}), {3}: (13, {}),... | custom-call | tf_op jit(solution)/shard_map/pallas_call | solution.py:695
  40.5 0.4 collective-permute-done.8.refs_8_
  40.9 0.7 %collective-permute-done.9.refs_9_ = f32[288,128]{1,0:T(8,128)S(1)} collective-permute-done((f32[288,128]{1,0:T(8,128)S(1)}, f32[288,128]{1,0:T(8,128)S(1)}, u32[]{:S(2)}, u32[]{:S(2)}) %collective-permute-start.9) | collective-permute-done | bytes 147488 | tf_op jit(solution)/shard_map/ppermute | solution.py:708
  41.6 2.1 %shard_map.37 = (f32[1152,128]{1,0:T(8,128)}, f32[1152,128]{1,0:T(8,128)S(1)}, f32[1536,128]{1,0:T(8,128)S(1)}, f32[1536,128]{1,0:T(8,128)S(1)}, f32[1536,128]{1...) custom-call(f32[3456,128]{1,0:T(8,128)S(1)} %get-tuple-element.114.r, ...), custom_call_target="tpu_custom_call", output_to_operand_aliasing={{1}: (10, {}), {2}: (11, {}), {3}: (12, {}), {4}: (13, {}),... | custom-call | tf_op jit(solution)/shard_map/pallas_call | solution.py:695
  (12 shorter events, 0.1 us)
Async XLA Ops:
  0.0 1.2 %copy-start = (f32[4,3,3,2,2,2,6,128]{7,5,6,4,3,2,1,0:T(2,128)S(1)}, f32[4,3,3,2,2,2,6,128]{7,5,6,4,3,2,1,0:T(2,128)}, u32[]{:S(2)}) copy-start(f32[4,3,3,2,2,2,6,128]{7,5,6,4,3,2,1,0:T(2,128)} %param.2) | copy-start | bytes 2654212
  1.2 15.5 %copy-start.1 = (f32[4,3,3,2,2,2,6,128]{7,5,6,4,3,2,1,0:T(2,128)S(1)}, f32[4,3,3,2,2,2,6,128]{7,5,6,4,3,2,1,0:T(2,128)}, u32[]{:S(2)}) copy-start(f32[4,3,3,2,2,2,6,128]{7,5,6,4,3,2,1,0:T(2,128)} %param.2) | copy-start | bytes 2654212
  1.2 16.7 %copy-start.2 = (f32[4,3,3,2,2,2,4,128]{7,6,5,4,3,2,1,0:T(4,128)S(1)}, f32[4,3,3,2,2,2,4,128]{7,6,5,4,3,2,1,0:T(4,128)}, u32[]{:S(2)}) copy-start(f32[4,3,3,2,2,2,4,128]{7,6,5,4,3,2,1,0:T(4,128)} %param.3) | copy-start | bytes 1769476
  1.3 10.1 %collective-permute-start.1 = (f32[408,128]{1,0:T(8,128)S(1)}, f32[408,128]{1,0:T(8,128)S(1)}, u32[]{:S(2)}, u32[]{:S(2)}) collective-permute-start(f32[408,128]{1,0:T(8,128)S(1)} %get-tuple-element.77), channel_id=1, source_target_pairs={{0,1},{1,2},{2,3},{3,4},{4,5},{5,6},{6,7},{7,8},{8,9},{9,10},{10,1... | collective-permute-start | bytes 626696 | tf_op jit(solution)/shard_map/ppermute | solution.py:708
  1.4 18.4 %collective-permute-start.3 = (f32[408,128]{1,0:T(8,128)S(1)}, f32[408,128]{1,0:T(8,128)S(1)}, u32[]{:S(2)}, u32[]{:S(2)}) collective-permute-start(f32[408,128]{1,0:T(8,128)S(1)} %get-tuple-element.79), channel_id=1, source_target_pairs={{0,16},{16,32},{32,48},{48,64},{64,80},{80,96},{96,112},{112,0},{1... | collective-permute-start | bytes 626696 | tf_op jit(solution)/shard_map/ppermute | solution.py:708
  5.4 6.0 %collective-permute-start = (f32[312,128]{1,0:T(8,128)S(1)}, f32[312,128]{1,0:T(8,128)S(1)}, u32[]{:S(2)}, u32[]{:S(2)}) collective-permute-start(f32[312,128]{1,0:T(8,128)S(1)} %get-tuple-element.76), channel_id=1, source_target_pairs={{0,15},{1,0},{2,1},{3,2},{4,3},{5,4},{6,5},{7,6},{8,7},{9,8},{10,9... | collective-permute-start | bytes 479240 | tf_op jit(solution)/shard_map/ppermute | solution.py:708
  8.3 11.1 %collective-permute-start.5 = (f32[312,128]{1,0:T(8,128)S(1)}, f32[312,128]{1,0:T(8,128)S(1)}, u32[]{:S(2)}, u32[]{:S(2)}) collective-permute-start(f32[312,128]{1,0:T(8,128)S(1)} %get-tuple-element.93), channel_id=1, source_target_pairs={{0,112},{16,0},{32,16},{48,32},{64,48},{80,64},{96,80},{112,96},{1... | collective-permute-start | bytes 479240 | tf_op jit(solution)/shard_map/ppermute | solution.py:708
  11.4 8.4 %collective-permute-start.2 = (f32[48,128]{1,0:T(8,128)S(1)}, f32[48,128]{1,0:T(8,128)S(1)}, u32[]{:S(2)}, u32[]{:S(2)}) collective-permute-start(f32[48,128]{1,0:T(8,128)S(1)} %get-tuple-element.78), channel_id=1, source_target_pairs={{0,112},{16,0},{32,16},{48,32},{64,48},{80,64},{96,80},{112,96},{1... | collective-permute-start | bytes 73736 | tf_op jit(solution)/shard_map/ppermute | solution.py:708
  16.7 7.4 %collective-permute-start.4 = (f32[48,128]{1,0:T(8,128)S(1)}, f32[48,128]{1,0:T(8,128)S(1)}, u32[]{:S(2)}, u32[]{:S(2)}) collective-permute-start(f32[48,128]{1,0:T(8,128)S(1)} %get-tuple-element.80), channel_id=1, source_target_pairs={{0,16},{16,32},{32,48},{48,64},{64,80},{80,96},{96,112},{112,0},{1... | collective-permute-start | bytes 73736 | tf_op jit(solution)/shard_map/ppermute | solution.py:708
  25.8 6.9 %collective-permute-start.7 = (f32[256,128]{1,0:T(8,128)S(1)}, f32[256,128]{1,0:T(8,128)S(1)}, u32[]{:S(2)}, u32[]{:S(2)}) collective-permute-start(f32[256,128]{1,0:T(8,128)S(1)} %get-tuple-element.124), channel_id=1, source_target_pairs={{0,1},{1,2},{2,3},{3,4},{4,5},{5,6},{6,7},{7,8},{8,9},{9,10},{10,1... | collective-permute-start | bytes 393224 | tf_op jit(solution)/shard_map/ppermute | solution.py:708
  25.9 6.1 %collective-permute-start.6 = (f32[192,128]{1,0:T(8,128)S(1)}, f32[192,128]{1,0:T(8,128)S(1)}, u32[]{:S(2)}, u32[]{:S(2)}) collective-permute-start(f32[192,128]{1,0:T(8,128)S(1)} %get-tuple-element.123), channel_id=1, source_target_pairs={{0,15},{1,0},{2,1},{3,2},{4,3},{5,4},{6,5},{7,6},{8,7},{9,8},{10,9... | collective-permute-start | bytes 294920 | tf_op jit(solution)/shard_map/ppermute | solution.py:708
  32.8 8.8 %collective-permute-start.9 = (f32[288,128]{1,0:T(8,128)S(1)}, f32[288,128]{1,0:T(8,128)S(1)}, u32[]{:S(2)}, u32[]{:S(2)}) collective-permute-start(f32[288,128]{1,0:T(8,128)S(1)} %get-tuple-element.128), channel_id=1, source_target_pairs={{0,16},{16,32},{32,48},{48,64},{64,80},{80,96},{96,112},{112,0},{1... | collective-permute-start | bytes 442376 | tf_op jit(solution)/shard_map/ppermute | solution.py:708
  32.9 8.0 %collective-permute-start.8 = (f32[224,128]{1,0:T(8,128)S(1)}, f32[224,128]{1,0:T(8,128)S(1)}, u32[]{:S(2)}, u32[]{:S(2)}) collective-permute-start(f32[224,128]{1,0:T(8,128)S(1)} %get-tuple-element.127), channel_id=1, source_target_pairs={{0,112},{16,0},{32,16},{48,32},{64,48},{80,64},{96,80},{112,96},{1... | collective-permute-start | bytes 344072 | tf_op jit(solution)/shard_map/ppermute | solution.py:708

commit v8 on v5

--- a/solution.py
+++ b/solution.py
@@ -145,11 +145,13 @@
                     down[pl.ds(((DOWN_Y.index(d) * n + q) * 2 + x) * 4, 4), :] = read_down(d, q, x)
 
 
-def pack_first_body(links, xdown, yup, ydown):
+def pack_first_body(links, xup, xdown, yup, ydown):
     def reader(row):
         return lambda d, q, x: links[pl.ds(((d * 18 + q) * 2 + x) * ROWS + row, 4, stride=2), :]
 
     pack_y(yup, ydown, 12, reader(3), reader(2))
+    pack_up(links, xup)
+    xup[pl.ds(288, 32), :] = jnp.zeros((32, 128), jnp.float32)
     for q in range(12):
         for x in range(2):
             yup[pl.ds(384 + q * 2 + x, 1), :] = links[pl.ds(((18 + q) * 2 + x) * ROWS + 11, 1), :]
@@ -159,7 +161,7 @@
         xdown[pl.ds(288 + q * 2, 2), :] = links[pl.ds((54 + q) * 2 * ROWS, 2), :]
 
 
-def pack_up_body(links, up):
+def pack_up(links, up):
     def read(d, row):
         return load_matrix(lambda i, j, ri: links[pl.ds((comp(d, i, j, ri) * 2 + 1) * ROWS + row, 8), :])
 
@@ -185,7 +187,7 @@
         down[pl.ds(q * 4, 4), :] = yprev[pl.ds((12 + q) * 8, 4), :]
 
 
-def pack_lambda_down_body(lam, yprev, after, down):
+def pack_lambda_down(lam, yprev, down):
     for c in range(24):
         down[pl.ds(c * 8, 8), :] = lam[pl.ds((c + NA) * 16, 8), :]
     for k in range(NA):
@@ -396,7 +398,7 @@
     return unpack8([read(k) for k in range(NA)])
 
 
-def exponent_force(v, m, target, clow):
+def exponent_force(v, m):
     a = v[:3]
     off = [(v[3 + 2 * k], v[4 + 2 * k]) for k in range(3)]
     norm = [r * r + s * s for r, s in off]
@@ -482,8 +484,7 @@
             (p2r * sr - p1i * s) - (p2i * si - p1r * r),
             -(p1i * r + p2i * sr) - (p2r * si + p1r * s),
         )
-    direct = msub(mm(edag, target), mm(anti(lam), clow))
-    return lam, direct
+    return lam, edag
 
 
 def plane_fields(m, n):
@@ -570,7 +571,7 @@
             store_cells(moved, m * 18, x, mm(target, link(bufs, m, step(), x), False, True))
 
 
-def finish_forward(bufs, inner, moved, loops, low, lam_out, direct):
+def finish_forward(bufs, moved, loops, low, lam_out, edag):
     for x in range(2):
         for m in range(4):
             u = link(bufs, m, step(), x)
@@ -585,10 +586,10 @@
             v = [(0.5 * smear_weight) * (v[k] - mean) for k in range(3)] + [
                 (0.5 * smear_weight) * v[k] for k in range(3, 9)
             ]
-            lam, force = exponent_force(v, load_cells(moved, m * 18, x), load_cells(inner, m * 18, x), below)
+            lam, smearing = exponent_force(v, load_cells(moved, m * 18, x))
             for k, v in enumerate(lam[:2] + lam[3:]):
                 lam_out[cells(m * NA, k, x), :] = v
-            store_cells(direct, m * 18, x, force)
+            store_cells(edag, m * 18, x, smearing)
 
 
 def backward_items(wanted, bufs, lams, omega, sums, acc, ready=None, xprev=None):
@@ -629,12 +630,16 @@
             store_cells(acc, m * 18, x, force)
 
 
+def add_loops(bufs, sums, acc, m, x):
+    f = load_cells(sums, m * 18, x)
+    store_cells(acc, m * 18, x, madd(mm(f, link(bufs, m, step(), x)), load_cells(acc, m * 18, x)))
+
+
 def finish_backward(bufs, sums, acc, out):
     for x in range(2):
         for m in range(4):
-            f = load_cells(sums, m * 18, x)
-            force = madd(mm(f, link(bufs, m, step(), x)), load_cells(acc, m * 18, x))
-            store_cells(acc, m * 18, x, force)
+            if x == 1:
+                add_loops(bufs, sums, acc, m, x)
             for k in range(18):
                 at = ((m * 18 + k) * 2 + x) * 8
                 out[pl.ds(at, 4), :] = acc[pl.ds(at, 4, stride=2), :]
@@ -665,13 +670,13 @@
 
 
 def links_x_body(*refs):
-    cnext, xprev, cprev, inner, moved = refs[:5]
-    bufs, (omega, loops, low, lam, direct, up, down, ready) = refs[15:22], refs[22:]
+    cnext, xprev, cprev, moved = refs[:4]
+    bufs, (omega, loops, low, lam, edag, up, down, ready) = refs[14:21], refs[21:]
     fill_corner(cnext, YM, 1, 3, 2, bufs)
     fill_corner(cprev, YP, 0, 0, 3, bufs)
     take_staples(xprev, bufs, ready)
     forward_items(3, bufs, omega, loops, low, ready)
-    finish_forward(bufs, inner, moved, loops, low, lam, direct)
+    finish_forward(bufs, moved, loops, low, lam, edag)
 
     def reader(row):
         return lambda d, q, x: lam[pl.ds(((d * NA + q) * 2 + x) * 8 + row, 4, stride=2), :]
@@ -680,15 +685,21 @@
 
 
 def lambda_local_body(*refs):
-    bufs, (omega, lam) = refs[:7], refs[7:9]
-    acc, lams, sums = refs[10], refs[11:18], refs[18]
+    bufs, (omega, lam, inner, low) = refs[:7], refs[7:11]
+    acc, lams, sums = refs[12], refs[13:20], refs[20]
     fill_lambda_local(lam, lams)
+    for x in range(2):
+        for m in range(4):
+            own = anti(unpack8([lam[cells(m * NA, k, x), :] for k in range(NA)]))
+            force = mm(load_cells(acc, m * 18, x), load_cells(inner, m * 18, x))
+            store_cells(acc, m * 18, x, msub(force, mm(own, load_cells(low, m * 18, x))))
     backward_items(0, bufs, lams, omega, sums, acc)
 
 
 def lambda_up_body(*refs):
-    ynext, yprev, links = refs[:3]
-    lams, up = refs[10:17], refs[17]
+    ynext, yprev, links, lam = refs[:4]
+    lams, (up, down) = refs[11:18], refs[18:]
+    pack_lambda_down(lam, yprev, down)
     fill_lambda_y(ynext, yprev, lams)
     here = step()
     for m in (1, 2, 3):
@@ -704,6 +715,8 @@
     bufs, omega, lams = refs[:7], refs[7], refs[8:15]
     acc, sums = refs[17:]
     backward_items(1, bufs, lams, omega, sums, acc)
+    for m in range(4):
+        add_loops(bufs, sums, acc, m, 0)
 
 
 def lambda_x_body(*refs):
@@ -746,24 +759,20 @@
     links = jnp.transpose(links, (0, 1, 2, 3, 4, 6, 5, 7)).reshape(144 * ROWS, 128)
     shape = incoming.shape
     incoming = incoming.reshape(1152, 128)
-    xdown, yup, ydown = call(pack_first_body, (links,), (312, 408, 312))
-    xnext = shifted(xdown, "gx", -1)
+    xup, xdown, yup, ydown = call(pack_first_body, (links,), (320, 312, 408, 312))
+    xprev, xnext = shifted(xup, "gx", 1), shifted(xdown, "gx", -1)
     yprev, ynext = shifted(yup, "gy", 1), shifted(ydown, "gy", -1)
-    (xup,) = call(pack_up_body, (links,), (288,))
-    xprev = shifted(xup, "gx", 1)
     cup, cdown = call(pack_corners_body, (ynext, yprev), (48, 48))
     cprev, cnext = shifted(cup, "gx", 1), shifted(cdown, "gx", -1)
     kept = call(links_local_body, (links,), buffer_rows(NC) + [1728, 864, 1152])
     *kept, inner, moved = call(links_y_body, (ynext, yprev, incoming), (1152, 1152), kept)
     kept = call(links_next_body, (xnext,), (), kept)
-    r = call(links_x_body, (cnext, xprev, cprev, inner, moved), (512, 1152, 256, 192, 432), kept)
-    bufs, omega, (lam, acc, yup, ydown, ready) = r[:7], r[7], r[10:]
+    r = call(links_x_body, (cnext, xprev, cprev, moved), (512, 1152, 256, 192, 432), kept)
+    bufs, omega, low, (lam, acc, yup, ydown, ready) = r[:7], r[7], r[9], r[10:]
     yprev, ynext = shifted(yup, "gy", 1), shifted(ydown, "gy", -1)
-    acc, *lams, sums = call(lambda_local_body, (*bufs, omega, lam), buffer_rows(NA) + [1152], (acc,))
-    (xdown,) = call(pack_lambda_down_body, (lam, yprev, sums), (224,))
-    xnext = shifted(xdown, "gx", -1)
-    *lams, xup = call(lambda_up_body, (ynext, yprev, bufs[O]), (192,), lams)
-    xprev = shifted(xup, "gx", 1)
+    acc, *lams, sums = call(lambda_local_body, (*bufs, omega, lam, inner, low), buffer_rows(NA) + [1152], (acc,))
+    *lams, xup, xdown = call(lambda_up_body, (ynext, yprev, bufs[O], lam), (192, 224), lams)
+    xprev, xnext = shifted(xup, "gx", 1), shifted(xdown, "gx", -1)
     acc, sums = call(lambda_y_body, (*bufs, omega, *lams), (), (acc, sums))
     out = call(lambda_x_body, (*bufs, omega, ready, xnext, xprev), (1152,), (acc, *lams, sums), first=1)[0]
     return out.reshape(shape)

time: 45.5 us -> 43.5 us (0.956)
  starting transfers between devices: 23.6 us -> 22.7 us
  Pallas kernels: 11 us -> 10.3 us
    ppermute x10, starting transfers between devices: 23.6 us -> 22.7 us  [shifted(): lax.ppermute(shard, axis, [(i, (i + by) % length) for i in range(length)])]
    pallas_call x12 -> x10, Pallas kernels: 11 us -> 10.3 us  [call(): pl.pallas_call(body, out_shape=tuple(shapes), in_specs=[pl.BlockSpec(memo...]
  transfers between devices with their start and end apart: 10 -> 10, of which waited for: 3 -> 5; matrix products, arithmetic and copies ran while one was open for 0% -> 0% of each run, Pallas kernels for 16% -> 16%
where the time goes in v8:
time: 43.5 us; the launch traced here: 43.4 us
  starting transfers between devices  22.7 us (52%)
  Pallas kernels  10.3 us (24%)
  waiting for transfers between devices  9.09 us (21%)
  local copies, waits for them, and re-layouts  1.17 us (3%)
    ppermute x10, starting transfers between devices, shifted(): lax.ppermute(shard, axis, [(i, (i + by) % length) for i in range(length)])  22.7 us
    pallas_call x10, Pallas kernels, call(): pl.pallas_call(body, out_shape=tuple(shapes), in_specs=[pl.BlockSpec(memo...  10.3 us
    ppermute x10, waiting for transfers between devices, shifted(): lax.ppermute(shard, axis, [(i, (i + by) % length) for i in range(length)])  9.09 us
    unnamed x6, local copies, waits for them, and re-layouts  1.17 us
  transfers between devices with their start and end apart: 10, of which 5 were waited for; matrix products, arithmetic and copies ran while one was open for 0% of the time, Pallas kernels for 16%

profile of v8, /device:TPU:0, one launch (start us, length us, event | category | flops | bytes accessed | tf_op | source)
XLA Modules:
  0.0 43.4 jit_solution(16690903266238040092)
XLA Ops:
  0.0 1.2 %copy-done = f32[4,3,3,2,2,2,6,128]{7,5,6,4,3,2,1,0:T(2,128)S(1)} copy-done((f32[4,3,3,2,2,2,6,128]{7,5,6,4,3,2,1,0:T(2,128)S(1)}, f32[4,3,3,2,2,2,6,128]{7,5,6,4,3,2,1,0:T(2,128)}, u32[]{:S(2)}) %copy-start) | copy-done | bytes 884760
  1.2 0.2 shard_map.28
  1.3 0.1 collective-permute-start.1
  1.4 4.0 %collective-permute-start = (f32[312,128]{1,0:T(8,128)S(1)}, f32[312,128]{1,0:T(8,128)S(1)}, u32[]{:S(2)}, u32[]{:S(2)}) collective-permute-start(f32[312,128]{1,0:T(8,128)S(1)} %get-tuple-element.78), channel_id=1, source_target_pairs={{0,15},{1,0},{2,1},{3,2},{4,3},{5,4},{6,5},{7,6},{8,7},{9,8},{10,9... | collective-permute-start | bytes 479240 | tf_op jit(solution)/shard_map/ppermute | solution.py:755
  5.4 3.8 %collective-permute-start.3 = (f32[320,128]{1,0:T(8,128)S(1)}, f32[320,128]{1,0:T(8,128)S(1)}, u32[]{:S(2)}, u32[]{:S(2)}) collective-permute-start(f32[320,128]{1,0:T(8,128)S(1)} %get-tuple-element.81), channel_id=1, source_target_pairs={{0,16},{16,32},{32,48},{48,64},{64,80},{80,96},{96,112},{112,0},{1... | collective-permute-start | bytes 491528 | tf_op jit(solution)/shard_map/ppermute | solution.py:755
  9.2 2.2 %collective-permute-start.5 = (f32[312,128]{1,0:T(8,128)S(1)}, f32[312,128]{1,0:T(8,128)S(1)}, u32[]{:S(2)}, u32[]{:S(2)}) collective-permute-start(f32[312,128]{1,0:T(8,128)S(1)} %get-tuple-element.94), channel_id=1, source_target_pairs={{0,112},{16,0},{32,16},{48,32},{64,48},{80,64},{96,80},{112,96},{1... | collective-permute-start | bytes 479240 | tf_op jit(solution)/shard_map/ppermute | solution.py:755
  11.4 5.1 %collective-permute-start.2 = (f32[48,128]{1,0:T(8,128)S(1)}, f32[48,128]{1,0:T(8,128)S(1)}, u32[]{:S(2)}, u32[]{:S(2)}) collective-permute-start(f32[48,128]{1,0:T(8,128)S(1)} %get-tuple-element.80), channel_id=1, source_target_pairs={{0,112},{16,0},{32,16},{48,32},{64,48},{80,64},{96,80},{112,96},{1... | collective-permute-start | bytes 73736 | tf_op jit(solution)/shard_map/ppermute | solution.py:755
  16.6 1.1 %shard_map.30 = (f32[3456,128]{1,0:T(8,128)S(1)}, f32[3456,128]{1,0:T(8,128)S(1)}, f32[3456,128]{1,0:T(8,128)S(1)}, f32[3456,128]{1,0:T(8,128)S(1)}, f32[3456,12...) custom-call(f32[1728,128]{1,0:T(8,128)S(1)} %bitcast.6), custom_call_target="tpu_custom_call" | custom-call | tf_op jit(solution)/shard_map/pallas_call | solution.py:742
  17.7 1.4 %shard_map.31 = (f32[3456,128]{1,0:T(8,128)S(1)}, f32[3456,128]{1,0:T(8,128)S(1)}, f32[3456,128]{1,0:T(8,128)S(1)}, f32[3456,128]{1,0:T(8,128)S(1)}, f32[3456,12...) custom-call(f32[312,128]{1,0:T(8,128)S(1)} %collective-permute-done., ...), custom_call_target="tpu_custom_call", output_to_operand_aliasing={{0}: (3, {}), {1}: (4, {}), {2}: (5, {}), {3}: (6, {}), {4}... | custom-call | tf_op jit(solution)/shard_map/pallas_call | solution.py:742
  19.2 0.1 collective-permute-done.5.refs_0_
  19.3 0.4 shard_map.32
  19.8 4.3 %collective-permute-done.4.refs_2_ = f32[48,128]{1,0:T(8,128)S(1)} collective-permute-done((f32[48,128]{1,0:T(8,128)S(1)}, f32[48,128]{1,0:T(8,128)S(1)}, u32[]{:S(2)}, u32[]{:S(2)}) %collective-permute-start.4) | collective-permute-done | bytes 24608 | tf_op jit(solution)/shard_map/ppermute | solution.py:755
  24.0 1.1 %shard_map.33 = (f32[3456,128]{1,0:T(8,128)S(1)}, f32[3456,128]{1,0:T(8,128)S(1)}, f32[3456,128]{1,0:T(8,128)S(1)}, f32[3456,128]{1,0:T(8,128)S(1)}, f32[3456,12...) custom-call(f32[48,128]{1,0:T(8,128)S(1)} %collective-permute-done.2, ...), custom_call_target="tpu_custom_call", output_to_operand_aliasing={{0}: (4, {}), {1}: (5, {}), {2}: (6, {}), {3}: (7, {}), {4}... | custom-call | tf_op jit(solution)/shard_map/pallas_call | solution.py:742
  25.1 0.1 collective-permute-start.7
  25.2 3.8 %collective-permute-start.6 = (f32[192,128]{1,0:T(8,128)S(1)}, f32[192,128]{1,0:T(8,128)S(1)}, u32[]{:S(2)}, u32[]{:S(2)}) collective-permute-start(f32[192,128]{1,0:T(8,128)S(1)} %get-tuple-element.124), channel_id=1, source_target_pairs={{0,15},{1,0},{2,1},{3,2},{4,3},{5,4},{6,5},{7,6},{8,7},{9,8},{10,9... | collective-permute-start | bytes 294920 | tf_op jit(solution)/shard_map/ppermute | solution.py:755
  29.1 2.1 %shard_map.34 = (f32[1152,128]{1,0:T(8,128)S(1)}, f32[1536,128]{1,0:T(8,128)S(1)}, f32[1536,128]{1,0:T(8,128)S(1)}, f32[1536,128]{1,0:T(8,128)S(1)}, f32[1536,12...) custom-call(f32[3456,128]{1,0:T(8,128)S(1)} %get-tuple-element.115.r, ...), custom_call_target="tpu_custom_call", output_to_operand_aliasing={{0}: (11, {})} | custom-call | tf_op jit(solution)/shard_map/pallas_call | solution.py:742
  31.1 0.2 collective-permute-done.6.refs_0_
  31.3 0.4 collective-permute-done.7.refs_1_
  31.7 0.2 shard_map.35
  31.9 1.4 %collective-permute-start.8 = (f32[224,128]{1,0:T(8,128)S(1)}, f32[224,128]{1,0:T(8,128)S(1)}, u32[]{:S(2)}, u32[]{:S(2)}) collective-permute-start(f32[224,128]{1,0:T(8,128)S(1)} %get-tuple-element.137), channel_id=1, source_target_pairs={{0,112},{16,0},{32,16},{48,32},{64,48},{80,64},{96,80},{112,96},{1... | collective-permute-start | bytes 344072 | tf_op jit(solution)/shard_map/ppermute | solution.py:755
  33.3 2.2 %collective-permute-start.9 = (f32[192,128]{1,0:T(8,128)S(1)}, f32[192,128]{1,0:T(8,128)S(1)}, u32[]{:S(2)}, u32[]{:S(2)}) collective-permute-start(f32[192,128]{1,0:T(8,128)S(1)} %get-tuple-element.138), channel_id=1, source_target_pairs={{0,16},{16,32},{32,48},{48,64},{64,80},{80,96},{96,112},{112,0},{1... | collective-permute-start | bytes 294920 | tf_op jit(solution)/shard_map/ppermute | solution.py:755
  35.5 1.9 %shard_map.36 = (f32[1152,128]{1,0:T(8,128)S(1)}, f32[1152,128]{1,0:T(8,128)S(1)}) custom-call(f32[3456,128]{1,0:T(8,128)S(1)} %get-tuple-element.115.refs_0_.refs_2_, f32[3456,128]{1,0:T(8,128)S(1)} %get-tuple-element.116.refs_1_, f32[3456,128]{1,0:T(8,128)S(1)} %get-tuple-element.117.refs_2_, ...), custom_call_target="tpu_custom_call", output_to_operand_aliasing={{0}: (15, {}), {1}: (16, {})} | custom-call | tf_op jit(solution)/shard_map/pallas_call | solution.py:742
  37.5 4.0 %collective-permute-done.9.refs_10_ = f32[192,128]{1,0:T(8,128)S(1)} collective-permute-done((f32[192,128]{1,0:T(8,128)S(1)}, f32[192,128]{1,0:T(8,128)S(1)}, u32[]{:S(2)}, u32[]{:S(2)}) %collective-permute-start.9) | collective-permute-done | bytes 98336 | tf_op jit(solution)/shard_map/ppermute | solution.py:755
  41.5 1.9 %shard_map.37 = (f32[1152,128]{1,0:T(8,128)}, f32[1152,128]{1,0:T(8,128)S(1)}, f32[1536,128]{1,0:T(8,128)S(1)}, f32[1536,128]{1,0:T(8,128)S(1)}, f32[1536,128]{1...) custom-call(f32[3456,128]{1,0:T(8,128)S(1)} %get-tuple-element.115.r, ...), custom_call_target="tpu_custom_call", output_to_operand_aliasing={{1}: (11, {}), {2}: (12, {}), {3}: (13, {}), {4}: (14, {}),... | custom-call | tf_op jit(solution)/shard_map/pallas_call | solution.py:742
  (12 shorter events, 0.1 us)
Async XLA Ops:
  0.0 1.2 %copy-start = (f32[4,3,3,2,2,2,6,128]{7,5,6,4,3,2,1,0:T(2,128)S(1)}, f32[4,3,3,2,2,2,6,128]{7,5,6,4,3,2,1,0:T(2,128)}, u32[]{:S(2)}) copy-start(f32[4,3,3,2,2,2,6,128]{7,5,6,4,3,2,1,0:T(2,128)} %param.2) | copy-start | bytes 2654212
  1.2 15.4 %copy-start.1 = (f32[4,3,3,2,2,2,6,128]{7,5,6,4,3,2,1,0:T(2,128)S(1)}, f32[4,3,3,2,2,2,6,128]{7,5,6,4,3,2,1,0:T(2,128)}, u32[]{:S(2)}) copy-start(f32[4,3,3,2,2,2,6,128]{7,5,6,4,3,2,1,0:T(2,128)} %param.2) | copy-start | bytes 2654212
  1.2 16.6 %copy-start.2 = (f32[4,3,3,2,2,2,4,128]{7,6,5,4,3,2,1,0:T(4,128)S(1)}, f32[4,3,3,2,2,2,4,128]{7,6,5,4,3,2,1,0:T(4,128)}, u32[]{:S(2)}) copy-start(f32[4,3,3,2,2,2,4,128]{7,6,5,4,3,2,1,0:T(4,128)} %param.3) | copy-start | bytes 1769476
  1.3 10.1 %collective-permute-start.1 = (f32[408,128]{1,0:T(8,128)S(1)}, f32[408,128]{1,0:T(8,128)S(1)}, u32[]{:S(2)}, u32[]{:S(2)}) collective-permute-start(f32[408,128]{1,0:T(8,128)S(1)} %get-tuple-element.79), channel_id=1, source_target_pairs={{0,1},{1,2},{2,3},{3,4},{4,5},{5,6},{6,7},{7,8},{8,9},{9,10},{10,1... | collective-permute-start | bytes 626696 | tf_op jit(solution)/shard_map/ppermute | solution.py:755
  1.4 10.0 %collective-permute-start = (f32[312,128]{1,0:T(8,128)S(1)}, f32[312,128]{1,0:T(8,128)S(1)}, u32[]{:S(2)}, u32[]{:S(2)}) collective-permute-start(f32[312,128]{1,0:T(8,128)S(1)} %get-tuple-element.78), channel_id=1, source_target_pairs={{0,15},{1,0},{2,1},{3,2},{4,3},{5,4},{6,5},{7,6},{8,7},{9,8},{10,9... | collective-permute-start | bytes 479240 | tf_op jit(solution)/shard_map/ppermute | solution.py:755
  5.4 14.3 %collective-permute-start.3 = (f32[320,128]{1,0:T(8,128)S(1)}, f32[320,128]{1,0:T(8,128)S(1)}, u32[]{:S(2)}, u32[]{:S(2)}) collective-permute-start(f32[320,128]{1,0:T(8,128)S(1)} %get-tuple-element.81), channel_id=1, source_target_pairs={{0,16},{16,32},{32,48},{48,64},{64,80},{80,96},{96,112},{112,0},{1... | collective-permute-start | bytes 491528 | tf_op jit(solution)/shard_map/ppermute | solution.py:755
  9.2 10.1 %collective-permute-start.5 = (f32[312,128]{1,0:T(8,128)S(1)}, f32[312,128]{1,0:T(8,128)S(1)}, u32[]{:S(2)}, u32[]{:S(2)}) collective-permute-start(f32[312,128]{1,0:T(8,128)S(1)} %get-tuple-element.94), channel_id=1, source_target_pairs={{0,112},{16,0},{32,16},{48,32},{64,48},{80,64},{96,80},{112,96},{1... | collective-permute-start | bytes 479240 | tf_op jit(solution)/shard_map/ppermute | solution.py:755
  11.4 8.3 %collective-permute-start.2 = (f32[48,128]{1,0:T(8,128)S(1)}, f32[48,128]{1,0:T(8,128)S(1)}, u32[]{:S(2)}, u32[]{:S(2)}) collective-permute-start(f32[48,128]{1,0:T(8,128)S(1)} %get-tuple-element.80), channel_id=1, source_target_pairs={{0,112},{16,0},{32,16},{48,32},{64,48},{80,64},{96,80},{112,96},{1... | collective-permute-start | bytes 73736 | tf_op jit(solution)/shard_map/ppermute | solution.py:755
  16.6 7.4 %collective-permute-start.4 = (f32[48,128]{1,0:T(8,128)S(1)}, f32[48,128]{1,0:T(8,128)S(1)}, u32[]{:S(2)}, u32[]{:S(2)}) collective-permute-start(f32[48,128]{1,0:T(8,128)S(1)} %get-tuple-element.82), channel_id=1, source_target_pairs={{0,16},{16,32},{32,48},{48,64},{64,80},{80,96},{96,112},{112,0},{1... | collective-permute-start | bytes 73736 | tf_op jit(solution)/shard_map/ppermute | solution.py:755
  25.1 6.6 %collective-permute-start.7 = (f32[256,128]{1,0:T(8,128)S(1)}, f32[256,128]{1,0:T(8,128)S(1)}, u32[]{:S(2)}, u32[]{:S(2)}) collective-permute-start(f32[256,128]{1,0:T(8,128)S(1)} %get-tuple-element.125), channel_id=1, source_target_pairs={{0,1},{1,2},{2,3},{3,4},{4,5},{5,6},{6,7},{7,8},{8,9},{9,10},{10,1... | collective-permute-start | bytes 393224 | tf_op jit(solution)/shard_map/ppermute | solution.py:755
  25.2 6.1 %collective-permute-start.6 = (f32[192,128]{1,0:T(8,128)S(1)}, f32[192,128]{1,0:T(8,128)S(1)}, u32[]{:S(2)}, u32[]{:S(2)}) collective-permute-start(f32[192,128]{1,0:T(8,128)S(1)} %get-tuple-element.124), channel_id=1, source_target_pairs={{0,15},{1,0},{2,1},{3,2},{4,3},{5,4},{6,5},{7,6},{8,7},{9,8},{10,9... | collective-permute-start | bytes 294920 | tf_op jit(solution)/shard_map/ppermute | solution.py:755
  31.9 9.6 %collective-permute-start.8 = (f32[224,128]{1,0:T(8,128)S(1)}, f32[224,128]{1,0:T(8,128)S(1)}, u32[]{:S(2)}, u32[]{:S(2)}) collective-permute-start(f32[224,128]{1,0:T(8,128)S(1)} %get-tuple-element.137), channel_id=1, source_target_pairs={{0,112},{16,0},{32,16},{48,32},{64,48},{80,64},{96,80},{112,96},{1... | collective-permute-start | bytes 344072 | tf_op jit(solution)/shard_map/ppermute | solution.py:755
  33.3 8.2 %collective-permute-start.9 = (f32[192,128]{1,0:T(8,128)S(1)}, f32[192,128]{1,0:T(8,128)S(1)}, u32[]{:S(2)}, u32[]{:S(2)}) collective-permute-start(f32[192,128]{1,0:T(8,128)S(1)} %get-tuple-element.138), channel_id=1, source_target_pairs={{0,16},{16,32},{32,48},{48,64},{64,80},{80,96},{96,112},{112,0},{1... | collective-permute-start | bytes 294920 | tf_op jit(solution)/shard_map/ppermute | solution.py:755

commit v9 on v8

--- a/solution.py
+++ b/solution.py
@@ -151,7 +151,6 @@
 
     pack_y(yup, ydown, 12, reader(3), reader(2))
     pack_up(links, xup)
-    xup[pl.ds(288, 32), :] = jnp.zeros((32, 128), jnp.float32)
     for q in range(12):
         for x in range(2):
             yup[pl.ds(384 + q * 2 + x, 1), :] = links[pl.ds(((18 + q) * 2 + x) * ROWS + 11, 1), :]
@@ -759,7 +758,7 @@
     links = jnp.transpose(links, (0, 1, 2, 3, 4, 6, 5, 7)).reshape(144 * ROWS, 128)
     shape = incoming.shape
     incoming = incoming.reshape(1152, 128)
-    xup, xdown, yup, ydown = call(pack_first_body, (links,), (320, 312, 408, 312))
+    xup, xdown, yup, ydown = call(pack_first_body, (links,), (288, 312, 408, 312))
     xprev, xnext = shifted(xup, "gx", 1), shifted(xdown, "gx", -1)
     yprev, ynext = shifted(yup, "gy", 1), shifted(ydown, "gy", -1)
     cup, cdown = call(pack_corners_body, (ynext, yprev), (48, 48))

time: 43.5 us -> 44 us (1.011)
  starting transfers between devices: 22.7 us -> 23.3 us
    ppermute x10, starting transfers between devices: 22.7 us -> 23.3 us  [shifted(): lax.ppermute(shard, axis, [(i, (i + by) % length) for i in range(length)])]
  transfers between devices with their start and end apart: 10 -> 10, of which waited for: 5 -> 4; matrix products, arithmetic and copies ran while one was open for 0% -> 0% of each run, Pallas kernels for 16% -> 16%
where the time goes in v9:
time: 44 us; the launch traced here: 43.9 us
  starting transfers between devices  23.3 us (53%)
  Pallas kernels  10.3 us (23%)
  waiting for transfers between devices  9.03 us (21%)
  local copies, waits for them, and re-layouts  1.17 us (3%)
    ppermute x10, starting transfers between devices, shifted(): lax.ppermute(shard, axis, [(i, (i + by) % length) for i in range(length)])  23.3 us
    pallas_call x10, Pallas kernels, call(): pl.pallas_call(body, out_shape=tuple(shapes), in_specs=[pl.BlockSpec(memo...  10.3 us
    ppermute x10, waiting for transfers between devices, shifted(): lax.ppermute(shard, axis, [(i, (i + by) % length) for i in range(length)])  9.03 us
    unnamed x6, local copies, waits for them, and re-layouts  1.17 us
  transfers between devices with their start and end apart: 10, of which 4 were waited for; matrix products, arithmetic and copies ran while one was open for 0% of the time, Pallas kernels for 16%

profile of v9, /device:TPU:0, one launch (start us, length us, event | category | flops | bytes accessed | tf_op | source)
XLA Modules:
  0.0 43.9 jit_solution(1337247744964984913)
XLA Ops:
  0.0 1.2 %copy-done = f32[4,3,3,2,2,2,6,128]{7,5,6,4,3,2,1,0:T(2,128)S(1)} copy-done((f32[4,3,3,2,2,2,6,128]{7,5,6,4,3,2,1,0:T(2,128)S(1)}, f32[4,3,3,2,2,2,6,128]{7,5,6,4,3,2,1,0:T(2,128)}, u32[]{:S(2)}) %copy-start) | copy-done | bytes 884760
  1.2 0.2 shard_map.28
  1.3 0.1 collective-permute-start.1
  1.4 4.0 %collective-permute-start = (f32[312,128]{1,0:T(8,128)S(1)}, f32[312,128]{1,0:T(8,128)S(1)}, u32[]{:S(2)}, u32[]{:S(2)}) collective-permute-start(f32[312,128]{1,0:T(8,128)S(1)} %get-tuple-element.78), channel_id=1, source_target_pairs={{0,15},{1,0},{2,1},{3,2},{4,3},{5,4},{6,5},{7,6},{8,7},{9,8},{10,9... | collective-permute-start | bytes 479240 | tf_op jit(solution)/shard_map/ppermute | solution.py:754
  5.4 6.0 %collective-permute-start.5 = (f32[312,128]{1,0:T(8,128)S(1)}, f32[312,128]{1,0:T(8,128)S(1)}, u32[]{:S(2)}, u32[]{:S(2)}) collective-permute-start(f32[312,128]{1,0:T(8,128)S(1)} %get-tuple-element.94), channel_id=1, source_target_pairs={{0,112},{16,0},{32,16},{48,32},{64,48},{80,64},{96,80},{112,96},{1... | collective-permute-start | bytes 479240 | tf_op jit(solution)/shard_map/ppermute | solution.py:754
  11.5 5.7 %collective-permute-start.2 = (f32[48,128]{1,0:T(8,128)S(1)}, f32[48,128]{1,0:T(8,128)S(1)}, u32[]{:S(2)}, u32[]{:S(2)}) collective-permute-start(f32[48,128]{1,0:T(8,128)S(1)} %get-tuple-element.80), channel_id=1, source_target_pairs={{0,112},{16,0},{32,16},{48,32},{64,48},{80,64},{96,80},{112,96},{1... | collective-permute-start | bytes 73736 | tf_op jit(solution)/shard_map/ppermute | solution.py:754
  17.2 1.1 %shard_map.30 = (f32[3456,128]{1,0:T(8,128)S(1)}, f32[3456,128]{1,0:T(8,128)S(1)}, f32[3456,128]{1,0:T(8,128)S(1)}, f32[3456,128]{1,0:T(8,128)S(1)}, f32[3456,12...) custom-call(f32[1728,128]{1,0:T(8,128)S(1)} %bitcast.6), custom_call_target="tpu_custom_call" | custom-call | tf_op jit(solution)/shard_map/pallas_call | solution.py:741
  18.3 1.4 %shard_map.31 = (f32[3456,128]{1,0:T(8,128)S(1)}, f32[3456,128]{1,0:T(8,128)S(1)}, f32[3456,128]{1,0:T(8,128)S(1)}, f32[3456,128]{1,0:T(8,128)S(1)}, f32[3456,12...) custom-call(f32[312,128]{1,0:T(8,128)S(1)} %collective-permute-done., ...), custom_call_target="tpu_custom_call", output_to_operand_aliasing={{0}: (3, {}), {1}: (4, {}), {2}: (5, {}), {3}: (6, {}), {4}... | custom-call | tf_op jit(solution)/shard_map/pallas_call | solution.py:741
  19.8 0.0 collective-permute-done.5.refs_0_
  19.8 0.4 shard_map.32
  20.2 0.0 collective-permute-done.3.refs_1_
  20.2 4.4 %collective-permute-done.4.refs_2_ = f32[48,128]{1,0:T(8,128)S(1)} collective-permute-done((f32[48,128]{1,0:T(8,128)S(1)}, f32[48,128]{1,0:T(8,128)S(1)}, u32[]{:S(2)}, u32[]{:S(2)}) %collective-permute-start.4) | collective-permute-done | bytes 24608 | tf_op jit(solution)/shard_map/ppermute | solution.py:754
  24.6 1.1 %shard_map.33 = (f32[3456,128]{1,0:T(8,128)S(1)}, f32[3456,128]{1,0:T(8,128)S(1)}, f32[3456,128]{1,0:T(8,128)S(1)}, f32[3456,128]{1,0:T(8,128)S(1)}, f32[3456,12...) custom-call(f32[48,128]{1,0:T(8,128)S(1)} %collective-permute-done.2, ...), custom_call_target="tpu_custom_call", output_to_operand_aliasing={{0}: (4, {}), {1}: (5, {}), {2}: (6, {}), {3}: (7, {}), {4}... | custom-call | tf_op jit(solution)/shard_map/pallas_call | solution.py:741
  25.7 0.1 collective-permute-start.7
  25.8 3.8 %collective-permute-start.6 = (f32[192,128]{1,0:T(8,128)S(1)}, f32[192,128]{1,0:T(8,128)S(1)}, u32[]{:S(2)}, u32[]{:S(2)}) collective-permute-start(f32[192,128]{1,0:T(8,128)S(1)} %get-tuple-element.124), channel_id=1, source_target_pairs={{0,15},{1,0},{2,1},{3,2},{4,3},{5,4},{6,5},{7,6},{8,7},{9,8},{10,9... | collective-permute-start | bytes 294920 | tf_op jit(solution)/shard_map/ppermute | solution.py:754
  29.6 2.1 %shard_map.34 = (f32[1152,128]{1,0:T(8,128)S(1)}, f32[1536,128]{1,0:T(8,128)S(1)}, f32[1536,128]{1,0:T(8,128)S(1)}, f32[1536,128]{1,0:T(8,128)S(1)}, f32[1536,12...) custom-call(f32[3456,128]{1,0:T(8,128)S(1)} %get-tuple-element.115.r, ...), custom_call_target="tpu_custom_call", output_to_operand_aliasing={{0}: (11, {})} | custom-call | tf_op jit(solution)/shard_map/pallas_call | solution.py:741
  31.7 0.2 collective-permute-done.6.refs_0_
  31.8 0.9 %collective-permute-done.7.refs_1_ = f32[256,128]{1,0:T(8,128)S(1)} collective-permute-done((f32[256,128]{1,0:T(8,128)S(1)}, f32[256,128]{1,0:T(8,128)S(1)}, u32[]{:S(2)}, u32[]{:S(2)}) %collective-permute-start.7) | collective-permute-done | bytes 131104 | tf_op jit(solution)/shard_map/ppermute | solution.py:754
  32.7 0.2 shard_map.35
  32.9 0.9 %collective-permute-start.8 = (f32[224,128]{1,0:T(8,128)S(1)}, f32[224,128]{1,0:T(8,128)S(1)}, u32[]{:S(2)}, u32[]{:S(2)}) collective-permute-start(f32[224,128]{1,0:T(8,128)S(1)} %get-tuple-element.137), channel_id=1, source_target_pairs={{0,112},{16,0},{32,16},{48,32},{64,48},{80,64},{96,80},{112,96},{1... | collective-permute-start | bytes 344072 | tf_op jit(solution)/shard_map/ppermute | solution.py:754
  33.8 2.7 %collective-permute-start.9 = (f32[192,128]{1,0:T(8,128)S(1)}, f32[192,128]{1,0:T(8,128)S(1)}, u32[]{:S(2)}, u32[]{:S(2)}) collective-permute-start(f32[192,128]{1,0:T(8,128)S(1)} %get-tuple-element.138), channel_id=1, source_target_pairs={{0,16},{16,32},{32,48},{48,64},{64,80},{80,96},{96,112},{112,0},{1... | collective-permute-start | bytes 294920 | tf_op jit(solution)/shard_map/ppermute | solution.py:754
  36.5 1.9 %shard_map.36 = (f32[1152,128]{1,0:T(8,128)S(1)}, f32[1152,128]{1,0:T(8,128)S(1)}) custom-call(f32[3456,128]{1,0:T(8,128)S(1)} %get-tuple-element.115.refs_0_.refs_2_, f32[3456,128]{1,0:T(8,128)S(1)} %get-tuple-element.116.refs_1_, f32[3456,128]{1,0:T(8,128)S(1)} %get-tuple-element.117.refs_2_, ...), custom_call_target="tpu_custom_call", output_to_operand_aliasing={{0}: (15, {}), {1}: (16, {})} | custom-call | tf_op jit(solution)/shard_map/pallas_call | solution.py:741
  38.5 3.6 %collective-permute-done.9.refs_10_ = f32[192,128]{1,0:T(8,128)S(1)} collective-permute-done((f32[192,128]{1,0:T(8,128)S(1)}, f32[192,128]{1,0:T(8,128)S(1)}, u32[]{:S(2)}, u32[]{:S(2)}) %collective-permute-start.9) | collective-permute-done | bytes 98336 | tf_op jit(solution)/shard_map/ppermute | solution.py:754
  42.0 1.9 %shard_map.37 = (f32[1152,128]{1,0:T(8,128)}, f32[1152,128]{1,0:T(8,128)S(1)}, f32[1536,128]{1,0:T(8,128)S(1)}, f32[1536,128]{1,0:T(8,128)S(1)}, f32[1536,128]{1...) custom-call(f32[3456,128]{1,0:T(8,128)S(1)} %get-tuple-element.115.r, ...), custom_call_target="tpu_custom_call", output_to_operand_aliasing={{1}: (11, {}), {2}: (12, {}), {3}: (13, {}), {4}: (14, {}),... | custom-call | tf_op jit(solution)/shard_map/pallas_call | solution.py:741
  (12 shorter events, 0.0 us)
Async XLA Ops:
  0.0 1.2 %copy-start = (f32[4,3,3,2,2,2,6,128]{7,5,6,4,3,2,1,0:T(2,128)S(1)}, f32[4,3,3,2,2,2,6,128]{7,5,6,4,3,2,1,0:T(2,128)}, u32[]{:S(2)}) copy-start(f32[4,3,3,2,2,2,6,128]{7,5,6,4,3,2,1,0:T(2,128)} %param.2) | copy-start | bytes 2654212
  1.2 16.0 %copy-start.1 = (f32[4,3,3,2,2,2,6,128]{7,5,6,4,3,2,1,0:T(2,128)S(1)}, f32[4,3,3,2,2,2,6,128]{7,5,6,4,3,2,1,0:T(2,128)}, u32[]{:S(2)}) copy-start(f32[4,3,3,2,2,2,6,128]{7,5,6,4,3,2,1,0:T(2,128)} %param.2) | copy-start | bytes 2654212
  1.2 17.1 %copy-start.2 = (f32[4,3,3,2,2,2,4,128]{7,6,5,4,3,2,1,0:T(4,128)S(1)}, f32[4,3,3,2,2,2,4,128]{7,6,5,4,3,2,1,0:T(4,128)}, u32[]{:S(2)}) copy-start(f32[4,3,3,2,2,2,4,128]{7,6,5,4,3,2,1,0:T(4,128)} %param.3) | copy-start | bytes 1769476
  1.3 10.1 %collective-permute-start.1 = (f32[408,128]{1,0:T(8,128)S(1)}, f32[408,128]{1,0:T(8,128)S(1)}, u32[]{:S(2)}, u32[]{:S(2)}) collective-permute-start(f32[408,128]{1,0:T(8,128)S(1)} %get-tuple-element.79), channel_id=1, source_target_pairs={{0,1},{1,2},{2,3},{3,4},{4,5},{5,6},{6,7},{7,8},{8,9},{9,10},{10,1... | collective-permute-start | bytes 626696 | tf_op jit(solution)/shard_map/ppermute | solution.py:754
  1.4 10.0 %collective-permute-start = (f32[312,128]{1,0:T(8,128)S(1)}, f32[312,128]{1,0:T(8,128)S(1)}, u32[]{:S(2)}, u32[]{:S(2)}) collective-permute-start(f32[312,128]{1,0:T(8,128)S(1)} %get-tuple-element.78), channel_id=1, source_target_pairs={{0,15},{1,0},{2,1},{3,2},{4,3},{5,4},{6,5},{7,6},{8,7},{9,8},{10,9... | collective-permute-start | bytes 479240 | tf_op jit(solution)/shard_map/ppermute | solution.py:754
  5.4 14.4 %collective-permute-start.5 = (f32[312,128]{1,0:T(8,128)S(1)}, f32[312,128]{1,0:T(8,128)S(1)}, u32[]{:S(2)}, u32[]{:S(2)}) collective-permute-start(f32[312,128]{1,0:T(8,128)S(1)} %get-tuple-element.94), channel_id=1, source_target_pairs={{0,112},{16,0},{32,16},{48,32},{64,48},{80,64},{96,80},{112,96},{1... | collective-permute-start | bytes 479240 | tf_op jit(solution)/shard_map/ppermute | solution.py:754
  11.4 8.8 %collective-permute-start.3 = (f32[288,128]{1,0:T(8,128)S(1)}, f32[288,128]{1,0:T(8,128)S(1)}, u32[]{:S(2)}, u32[]{:S(2)}) collective-permute-start(f32[288,128]{1,0:T(8,128)S(1)} %get-tuple-element.81), channel_id=1, source_target_pairs={{0,16},{16,32},{32,48},{48,64},{64,80},{80,96},{96,112},{112,0},{1... | collective-permute-start | bytes 442376 | tf_op jit(solution)/shard_map/ppermute | solution.py:754
  11.5 8.7 %collective-permute-start.2 = (f32[48,128]{1,0:T(8,128)S(1)}, f32[48,128]{1,0:T(8,128)S(1)}, u32[]{:S(2)}, u32[]{:S(2)}) collective-permute-start(f32[48,128]{1,0:T(8,128)S(1)} %get-tuple-element.80), channel_id=1, source_target_pairs={{0,112},{16,0},{32,16},{48,32},{64,48},{80,64},{96,80},{112,96},{1... | collective-permute-start | bytes 73736 | tf_op jit(solution)/shard_map/ppermute | solution.py:754
  17.2 7.4 %collective-permute-start.4 = (f32[48,128]{1,0:T(8,128)S(1)}, f32[48,128]{1,0:T(8,128)S(1)}, u32[]{:S(2)}, u32[]{:S(2)}) collective-permute-start(f32[48,128]{1,0:T(8,128)S(1)} %get-tuple-element.82), channel_id=1, source_target_pairs={{0,16},{16,32},{32,48},{48,64},{64,80},{80,96},{96,112},{112,0},{1... | collective-permute-start | bytes 73736 | tf_op jit(solution)/shard_map/ppermute | solution.py:754
  25.7 7.0 %collective-permute-start.7 = (f32[256,128]{1,0:T(8,128)S(1)}, f32[256,128]{1,0:T(8,128)S(1)}, u32[]{:S(2)}, u32[]{:S(2)}) collective-permute-start(f32[256,128]{1,0:T(8,128)S(1)} %get-tuple-element.125), channel_id=1, source_target_pairs={{0,1},{1,2},{2,3},{3,4},{4,5},{5,6},{6,7},{7,8},{8,9},{9,10},{10,1... | collective-permute-start | bytes 393224 | tf_op jit(solution)/shard_map/ppermute | solution.py:754
  25.8 6.1 %collective-permute-start.6 = (f32[192,128]{1,0:T(8,128)S(1)}, f32[192,128]{1,0:T(8,128)S(1)}, u32[]{:S(2)}, u32[]{:S(2)}) collective-permute-start(f32[192,128]{1,0:T(8,128)S(1)} %get-tuple-element.124), channel_id=1, source_target_pairs={{0,15},{1,0},{2,1},{3,2},{4,3},{5,4},{6,5},{7,6},{8,7},{9,8},{10,9... | collective-permute-start | bytes 294920 | tf_op jit(solution)/shard_map/ppermute | solution.py:754
  32.9 9.1 %collective-permute-start.8 = (f32[224,128]{1,0:T(8,128)S(1)}, f32[224,128]{1,0:T(8,128)S(1)}, u32[]{:S(2)}, u32[]{:S(2)}) collective-permute-start(f32[224,128]{1,0:T(8,128)S(1)} %get-tuple-element.137), channel_id=1, source_target_pairs={{0,112},{16,0},{32,16},{48,32},{64,48},{80,64},{96,80},{112,96},{1... | collective-permute-start | bytes 344072 | tf_op jit(solution)/shard_map/ppermute | solution.py:754
  33.8 8.2 %collective-permute-start.9 = (f32[192,128]{1,0:T(8,128)S(1)}, f32[192,128]{1,0:T(8,128)S(1)}, u32[]{:S(2)}, u32[]{:S(2)}) collective-permute-start(f32[192,128]{1,0:T(8,128)S(1)} %get-tuple-element.138), channel_id=1, source_target_pairs={{0,16},{16,32},{32,48},{48,64},{64,80},{80,96},{96,112},{112,0},{1... | collective-permute-start | bytes 294920 | tf_op jit(solution)/shard_map/ppermute | solution.py:754
